TPU v7x, 32 devices: a whole 2x2x4 slice. The times are simulated.
32 devices in a mesh: groups: 2 (over x), branch: 8 (over z, y), sub: 2 (over core).
Axes of the slice: x: 2, y: 2, z: 4, core: 2. Of those that a mesh axis runs over, the one named last changes fastest.
Arguments:
- right_sides: bfloat16 [32, 262144], P('groups', ('branch', 'sub')), parts along dimension 0, may hold values from -6 to 6
- near_blocks: bfloat16 [5, 64, 262144], P(None, None, ('branch', 'sub')), may hold values from -0.3125 to 0.3125
- near_leaves: int32 [4096, 5], P(('branch', 'sub')), may hold values from 0 to 4095, as said below
- leaf_basis: bfloat16 [32, 262144], P(None, ('branch', 'sub')), may hold values from -0.75 to 0.75
- transfer_first: bfloat16 [32, 32, 4096], P(None, None, ('branch', 'sub')), may hold values from -0.75 to 0.75
- transfer_second: bfloat16 [32, 32, 2048], P(None, None, ('branch', 'sub')), may hold values from -0.75 to 0.75
- transfer_third: bfloat16 [32, 32, 1024], P(None, None, ('branch', 'sub')), may hold values from -0.75 to 0.75
- coupling_first: bfloat16 [3, 32, 32, 2048], P(None, None, None, ('branch', 'sub')), may hold values from -0.625 to 0.625
- coupling_second: bfloat16 [3, 32, 32, 1024], P(None, None, None, ('branch', 'sub')), may hold values from -0.625 to 0.625
- list_first: int32 [2048, 3], P(('branch', 'sub')), may hold values from 0 to 2047, as said below
- list_second: int32 [1024, 3], P(('branch', 'sub')), may hold values from 0 to 1023, as said below
- top_coupling: bfloat16 [8, 32, 32, 512], P(None, None, None, ('branch', 'sub')), may hold values from -0.375 to 0.375
- top_nodes: int32 [512, 8], P(('branch', 'sub')), may hold values from 0 to 511
Outputs:
- first_image: bfloat16 [32, 262144], P('groups', ('branch', 'sub')), parts along dimension 0
- second_image: bfloat16 [32, 262144], P('groups', ('branch', 'sub')), parts along dimension 0
There are 2 independent parts, one for each index of `groups`. A program takes and returns all parts, laid end to end along the dimension named above; an argument that names none is the same for every part. Nothing has to cross between parts.
Inputs may be any that keep to these rules, and one draw needn't show every extreme that they name: `near_leaves`: each entry is a leaf within 2 leaves of its row's leaf. `list_first`: each entry is a node within 2 nodes of its row's node. `list_second`: each entry is a node within 2 nodes of its row's node.
All inputs are finite; a program needn't handle non-finite values.
Results may differ from a plain program's by a relative error of at most 0.012.
Values may be sent and summed in bfloat16 or wider, within the bound.
No kernel may reach another device: no remote copies, remote signals or barrier semaphores. Data moves between devices by JAX's collectives and lax.ppermute only.
A program may use at most 192 MiB of HBM per device.

v0:
```python
import functools

import jax
import jax.numpy as jnp
from jax import lax
from jax.experimental import pallas as pl
from jax.experimental.pallas import tpu as pltpu
from jax.sharding import PartitionSpec as P

M = 64
K = 32
NEAR = 5
NC = 3
NFAR = 8
HN = 2
HC = 2
LANES = 128
AXES = ("branch", "sub")
PIECES = 3
CHUNK = 1024
F32 = jnp.float32
BF16 = jnp.bfloat16
NT = (((1,), (1,)), ((), ()))


def iota(shape, dim):
    return lax.broadcasted_iota(jnp.int32, shape, dim)


def place(node, count, levels):
    where = jnp.zeros_like(node)
    for level in range(levels):
        count //= 2
        where = where + (node & 1) * count
        node = node >> 1
    return where + node


def place_static(node, count, levels):
    where = 0
    for level in range(levels):
        count //= 2
        where += (node & 1) * count
        node >>= 1
    return where + node


def lane_order(count, levels, copies=1):
    rows = place(iota((count, count * copies), 0), count, levels)
    columns = iota((count, count * copies), 1) & (count - 1)
    return jnp.where(rows == columns, 1.0, 0.0).astype(BF16)


def dot(a, b):
    return jnp.dot(a, b, preferred_element_type=F32)


def rounded(x):
    return x.astype(BF16).astype(F32)


def contract(terms, init, lanes):
    def step(position, accs):
        for matrix_at, x_at in terms:
            matrix = matrix_at(position).astype(F32)
            accs = tuple(acc + matrix * x_at(r, position) for r, acc in enumerate(accs))
        return accs

    return lax.fori_loop(0, K, step, init, unroll=4)


def prep_up_kernel(first_ref, second_ref, third_ref, up1_ref, up2_ref, up3_ref):
    for source, target, levels, copies in ((first_ref, up1_ref, 3, 1), (second_ref, up2_ref, 2, 1), (third_ref, up3_ref, 1, 2)):
        count = source.shape[2]
        order = lane_order(count, levels, copies)
        for k in range(0, K, 4):
            rows = source[k : k + 4].reshape(4 * K, count)
            target[k : k + 4] = dot(rows, order).astype(BF16).reshape(4, K, count * copies)


def prep_rest_kernel(up1_ref, up2_ref, up3_ref, c1_ref, c2_ref, c3_ref, d1_ref, d2_ref, d3_ref, m1_ref, m2_ref, m3_ref, wide_ref):
    for source, target in ((up1_ref, d1_ref), (up2_ref, d2_ref), (up3_ref, d3_ref)):
        for tile in range(source.shape[2] // LANES):
            lanes = slice(tile * LANES, (tile + 1) * LANES)
            wide_ref[...] = source[:, :, lanes].astype(F32).reshape(K * K, LANES)
            for m in range(K):
                target[m, :, lanes] = wide_ref[pl.ds(m, K, stride=K), :].astype(BF16)
    for source, target, levels, copies in ((c1_ref, m1_ref, 2, 1), (c2_ref, m2_ref, 1, 2)):
        count = source.shape[3]
        order = lane_order(count, levels, copies)
        for j in range(NC):
            for k in range(0, K, 8):
                rows = source[j, k : k + 8].reshape(8 * K, count)
                target[j, k : k + 8] = dot(rows, order).astype(BF16).reshape(8, K, LANES)
    top = c3_ref.shape[3]
    group = LANES // top
    for h in range(NFAR // group):
        for k in range(0, K, 8):
            total = None
            for q in range(group):
                put = jnp.where(iota((top, LANES), 0) + q * top == iota((top, LANES), 1), 1.0, 0.0).astype(BF16)
                part = dot(c3_ref[h * group + q, k : k + 8].reshape(8 * K, top), put)
                total = part if total is None else total + part
            m3_ref[h, k : k + 8] = total.astype(BF16).reshape(8, K, LANES)


def up_kernel(z_ref, basis_ref, up1_ref, up2_ref, up3_ref, sent_ref, coef1_ref, coef2_ref, rows_ref, x0_ref, x1_ref, x2_ref):
    rhs, order = z_ref.shape
    leaves = order // M
    top = leaves // 8
    low = iota((rhs, LANES), 1) < M
    zero = jnp.zeros((rhs, LANES), BF16)

    @pl.loop(0, leaves // 16)
    def _(outer):
        for inner in range(4):
            chunk = outer * 4 + inner
            lanes = pl.ds(pl.multiple_of(chunk * 256, 256), 256)
            z = z_ref[:, lanes]
            left, right = z[:, :LANES], z[:, LANES:]
            none = jnp.zeros_like(left)
            masked = jnp.concatenate(
                [
                    jnp.concatenate([jnp.where(low, left, none), none], axis=1),
                    jnp.concatenate([jnp.where(low, none, left), none], axis=1),
                    jnp.concatenate([none, jnp.where(low, right, none)], axis=1),
                    jnp.concatenate([none, jnp.where(low, none, right)], axis=1),
                ],
                axis=0,
            )
            coef = lax.dot_general(masked, basis_ref[:, lanes], NT, preferred_element_type=F32)
            rows_ref[pl.ds(pl.multiple_of(chunk * 64, 64), 64), :K] = coef

    unit = jnp.where(iota((K, K), 0) == iota((K, K), 1), 1.0, 0.0).astype(BF16)
    for r in range(rhs):
        pieces = []
        for c in range(2):
            for b in range(2):
                for a in range(2):
                    pieces.append(rows_ref[pl.ds(rhs * (4 * a + 2 * b + c) + r, top, stride=8 * rhs), :K])
        tall = jnp.concatenate(pieces, axis=0).astype(BF16)
        wide = lax.dot_general(unit, tall, NT, preferred_element_type=F32)
        x0_ref[0, r] = wide[:, :LANES]
        x0_ref[1, r] = wide[:, LANES:]

    half = rhs // 2
    zeros = tuple(jnp.zeros((K, LANES), F32) for _ in range(half))
    for first in (0, half):
        terms = [
            (
                functools.partial(lambda s, k: up1_ref[k, :, s * LANES : (s + 1) * LANES], s),
                functools.partial(lambda s, r, k: x0_ref[s, first + r, pl.ds(k, 1), :], s),
            )
            for s in range(2)
        ]
        for r, acc in enumerate(contract(terms, zeros, LANES)):
            coef1_ref[first + r] = acc.astype(BF16)
            x1_ref[first + r] = rounded(acc)
    low = iota((K, LANES), 1) < M
    for first in (0, half):
        terms = [(lambda k: up2_ref[k], lambda r, k: x1_ref[first + r, pl.ds(k, 1), :])]
        for r, acc in enumerate(contract(terms, zeros, LANES)):
            total = rounded(acc + pltpu.roll(acc, 64, 1))
            if first == 0:
                x2_ref[r] = total
            else:
                both = jnp.where(low, x2_ref[r], total)
                x2_ref[r] = both
                coef2_ref[r] = both.astype(BF16)
    terms = [(lambda k: up3_ref[k], lambda r, k: x2_ref[r, pl.ds(k, 1), :])]
    sums = [acc + pltpu.roll(acc, 32, 1) for acc in contract(terms, zeros, LANES)]
    odd = (iota((K, LANES), 1) & 32) > 0
    for r in range(half // 2):
        sent_ref[r * K : (r + 1) * K] = jnp.where(odd, sums[r], pltpu.roll(sums[r + half // 2], 96, 1)).astype(BF16)

    def ends(count, offset, shift):
        row, column = iota((LANES, LANES), 0), iota((LANES, LANES), 1)
        hit = (row == -1)
        for copy in range(LANES // count):
            for e, node in enumerate((0, 1, count - 2, count - 1)):
                at = place_static(node, count, 2 if count == LANES else 1)
                hit = hit | ((row == copy * count + at) & (column == copy * M + offset + e))
        return jnp.where(hit, 1.0, 0.0).astype(BF16)

    first_ends = dot(x1_ref[...].astype(BF16).reshape(rhs * K, LANES), ends(LANES, 0, 0)).reshape(rhs, K, LANES)
    second_ends = dot(x2_ref[...].astype(BF16).reshape(half * K, LANES), ends(M, 4, 64)).reshape(half, K, LANES)
    packed = jnp.zeros((K, LANES), F32)
    for r in range(rhs):
        value = first_ends[r]
        if r < half:
            value = value + second_ends[r]
        packed = packed + (pltpu.roll(value, 8 * r, 1) if r else value)
    base = half // 2 * K
    sent_ref[base : base + K] = packed.astype(BF16)
    sent_ref[base + K : base + K + rhs] = z_ref[:, :LANES]
    sent_ref[base + K + rhs : base + K + 2 * rhs] = z_ref[:, order - LANES :]


def put_leaves(target_ref, tile, slot):
    low = iota(tile.shape, 1) < M
    wide = tile.astype(F32)
    swapped = pltpu.roll(wide, M, 1)
    target_ref[slot] = jnp.where(low, wide, swapped).astype(BF16)
    target_ref[slot + 1] = jnp.where(low, swapped, wide).astype(BF16)


def own_blocks(res, rhs):
    low = iota((rhs, LANES), 1) < M
    return jnp.concatenate(
        [
            jnp.where(low, res[:rhs, :LANES], res[rhs : 2 * rhs, :LANES]),
            jnp.where(low, res[2 * rhs : 3 * rhs, LANES:], res[3 * rhs :, LANES:]),
        ],
        axis=1,
    )


def near_group(read, weights, rhs):
    low = iota((rhs, LANES), 1) < M
    rows = []
    for leaf in range(4):
        z = [read(j, leaf) for j in range(NEAR)]
        rows.append(jnp.concatenate([jnp.where(low, z[0], z[1]), jnp.where(low, z[2], z[3]), z[4][:, :M]], axis=1))
    return own_blocks(dot(jnp.concatenate(rows, axis=0), weights), rhs)


def near_kernel(chunk0, leaves_ref, z_ref, blocks_hbm, out_ref, z_leaves_ref, blocks_ref, sems):
    rhs, order = z_ref.shape
    chunks = out_ref.shape[1] // CHUNK

    def copy(c):
        there = pl.ds(pl.multiple_of((chunk0 + c) * CHUNK, CHUNK), CHUNK)
        here = pl.ds(pl.multiple_of(c * CHUNK, CHUNK), CHUNK)
        return pltpu.make_async_copy(blocks_hbm.at[:, :, there], blocks_ref.at[:, :, here], sems.at[c])

    for c in range(chunks):
        copy(c).start()
    per = CHUNK // M
    first_tile = max(chunk0 * (CHUNK // LANES) - 1, 0)
    last_tile = min((chunk0 + chunks) * (CHUNK // LANES) + 1, order // LANES)
    for t in range(first_tile, last_tile):
        put_leaves(z_leaves_ref, z_ref[:, t * LANES : (t + 1) * LANES], 2 * t + HN)

    @pl.loop(0, chunks)
    def _(c):
        copy(c).wait()
        for g in range(CHUNK // 256):
            leaf0 = (chunk0 + c) * per + 4 * g
            lanes = pl.ds(pl.multiple_of(c * CHUNK + g * 256, 256), 256)
            weights = blocks_ref[:, :, lanes].reshape(NEAR * M, 256)
            out_ref[:, lanes] = near_group(lambda j, e: z_leaves_ref[leaves_ref[j, leaf0 + e]], weights, rhs)


def bit_reverse(value, bits):
    out = jnp.zeros_like(value)
    for b in range(bits):
        out = out + (((value >> b) & 1) << (bits - 1 - b))
    return out


def list_rows(nodes, me, count, halo0):
    local = nodes - me * count
    inside = place(jnp.clip(local, 0, count - 1), count, 2 if count == LANES else 1)
    left = halo0 + 4 + local
    right = halo0 + local - count
    return jnp.where(local < 0, left, jnp.where(local >= count, right, inside))


def in_order(rows, count, levels):
    wide = jnp.concatenate([rows.astype(F32)] + [jnp.zeros((8 - rows.shape[0], count), F32)], axis=0).astype(BF16)
    return dot(wide, lane_order(count, levels)).astype(jnp.int32)


def down_kernel(
    bits, me_ref, leaves_ref, early_ref, late_ref, coef1_ref, coef2_ref, z_ref, *refs
):
    near_refs = refs[:PIECES]
    (head_ref, tail_ref, basis_ref, list1_ref, list2_ref, top_ref, m1_ref, m2_ref, m3_ref, d1_ref, d2_ref, d3_ref,
     out_ref, every_ref, picks_ref, far1_ref, x_ref, x0_ref, rows_ref, z_leaves_ref) = refs[PIECES:]
    rhs, order = z_ref.shape
    leaves = order // M
    top = leaves // 8
    half = rhs // 2
    me = me_ref[0]
    devices = 1 << bits
    own_rows = half // 2 * K

    def block(device, rows):
        at = bit_reverse(jnp.bitwise_xor(device, me), bits)
        early = early_ref[jnp.minimum(at, devices // 2 - 1), rows]
        late = late_ref[jnp.maximum(at - devices // 2, 0), rows]
        return jnp.where(at < devices // 2, early.astype(F32), late.astype(F32))

    before = jnp.maximum(me - 1, 0)
    after = jnp.minimum(me + 1, devices - 1)

    z_before = block(before, slice(own_rows + K + rhs, own_rows + K + 2 * rhs)).astype(BF16)
    z_after = block(after, slice(own_rows + K, own_rows + K + rhs)).astype(BF16)
    put_leaves(z_leaves_ref, z_before, 0)
    for t in range(3):
        put_leaves(z_leaves_ref, z_ref[:, t * LANES : (t + 1) * LANES], 2 + 2 * t)
        put_leaves(z_leaves_ref, z_ref[:, order - (3 - t) * LANES : order - (2 - t) * LANES or None], 8 + 2 * t)
    put_leaves(z_leaves_ref, z_after, 14)
    head = near_group(lambda j, e: z_leaves_ref[leaves_ref[j, e]], head_ref[...].reshape(NEAR * M, 256), rhs)
    skip = leaves + 2 * HN - 16
    tail = near_group(
        lambda j, e: z_leaves_ref[leaves_ref[j, leaves - 4 + e] - skip], tail_ref[...].reshape(NEAR * M, 256), rhs
    )

    sides = slice(own_rows, own_rows + K)
    halo = jnp.where((iota((K, LANES), 1) & 2) > 0, block(before, sides), block(after, sides))

    group = iota((own_rows, LANES), 1) // top
    per = LANES // top
    for tile in range(devices // per):
        source = early_ref if tile < devices // per // 2 else late_ref
        first = tile * per - (0 if tile < devices // per // 2 else devices // 2)
        parts = [source[first + q, :own_rows].astype(F32) for q in range(per)]
        for g in range(per):
            merged = None
            for q in range(per):
                shift = (q - g) * top % LANES
                moved = pltpu.roll(parts[q], shift, 1) if shift else parts[q]
                merged = moved if merged is None else jnp.where(group == q, moved, merged)
            every_ref[g * own_rows : (g + 1) * own_rows, tile * LANES : (tile + 1) * LANES] = merged.astype(BF16)
    nodes = top_ref[...]
    rows = bit_reverse(jnp.bitwise_xor(nodes // top, me), bits) * top + nodes % top
    hot = []
    for j in range(NFAR):
        hot.append(jnp.where(iota((devices * top, top), 0) == rows[j : j + 1], 1.0, 0.0).astype(BF16))
    for h in range(NFAR // per):
        wide = None
        for q in range(per):
            put = jnp.where(iota((top, LANES), 0) + q * top == iota((top, LANES), 1), 1.0, 0.0).astype(BF16)
            part = dot(hot[h * per + q], put)
            wide = part if wide is None else wide + part
        picked = dot(every_ref[...], wide.astype(BF16))
        picks_ref[:, h * K : (h + 1) * K, :] = picked.reshape(rhs, K, LANES)
    zeros = tuple(jnp.zeros((K, LANES), F32) for _ in range(half))
    groups_of = [1, 0, 3, 2]

    def slot(r):
        quarter = rhs // 4
        return groups_of[r // quarter] * quarter + r % quarter

    low = iota((K, LANES), 1) < M
    kept = {}
    for first in range(0, rhs, half):
        terms = [
            (
                functools.partial(lambda h, k: m3_ref[h, k], h),
                functools.partial(lambda h, r, k: picks_ref[slot(first + r), pl.ds(h * K + k, 1), :], h),
            )
            for h in range(NFAR // per)
        ]
        for r, acc in enumerate(contract(terms, zeros, LANES)):
            acc = acc + pltpu.roll(acc, 64, 1)
            acc = rounded(acc + pltpu.roll(acc, 32, 1))
            if first == 0:
                x_ref[r] = acc
            else:
                x_ref[r] = jnp.where(low, x_ref[r], acc)

    rows = in_order(list_rows(list2_ref[...], me, M, 4), M, 1)
    hot = []
    for j in range(NC):
        row = jnp.concatenate([rows[j : j + 1], rows[j : j + 1]], axis=1)
        column_half = (iota((LANES, LANES), 1) // M) * M
        index = iota((LANES, LANES), 0) - column_half
        hot.append((row, index))
    local = list2_ref[...] - me * M
    outside = in_order(jnp.where((local < 0) | (local >= M), 1, 0), M, 1)
    tables = []
    for j in range(NC):
        row, index = hot[j]
        out = jnp.concatenate([outside[j : j + 1], outside[j : j + 1]], axis=1)
        own = jnp.where((row == index) & (out == 0), 1.0, 0.0)
        far = jnp.where((row == index) & (out == 1), 1.0, 0.0)
        tables.append(jnp.concatenate([own, far], axis=0).astype(BF16))
    table = jnp.concatenate(tables, axis=1)
    for r in range(half):
        turned = pltpu.roll(halo, LANES - 8 * r, 1) if r else halo
        picked = dot(jnp.concatenate([coef2_ref[r], turned.astype(BF16)], axis=1), table)
        for j in range(NC):
            picks_ref[r, j * K : (j + 1) * K, :] = picked[:, j * LANES : (j + 1) * LANES]
    terms = [
        (
            functools.partial(lambda j, k: m2_ref[j, k], j),
            functools.partial(lambda j, r, k: picks_ref[r, pl.ds(j * K + k, 1), :], j),
        )
        for j in range(NC)
    ] + [(lambda m: d3_ref[m], lambda r, m: x_ref[r, pl.ds(m, 1), :])]
    second = [rounded(acc) for acc in contract(terms, zeros, LANES)]
    for r, value in enumerate(second):
        swapped = pltpu.roll(value, M, 1)
        x_ref[r] = jnp.where(low, value, swapped)
        x_ref[r + half] = jnp.where(low, swapped, value)

    rows = in_order(list_rows(list1_ref[...], me, LANES, LANES), LANES, 2)
    table = jnp.concatenate(
        [jnp.where(iota((2 * LANES, LANES), 0) == rows[j : j + 1], 1.0, 0.0) for j in range(NC)], axis=1
    ).astype(BF16)
    for r in range(rhs):
        turned = pltpu.roll(halo, LANES - 8 * r, 1) if r else halo
        picked = dot(jnp.concatenate([coef1_ref[r], turned.astype(BF16)], axis=1), table)
        for j in range(NC):
            picks_ref[r, j * K : (j + 1) * K, :] = picked[:, j * LANES : (j + 1) * LANES]
    for first in (0, half):
        terms = [
            (
                functools.partial(lambda j, k: m1_ref[j, k], j),
                functools.partial(lambda j, r, k: picks_ref[first + r, pl.ds(j * K + k, 1), :], j),
            )
            for j in range(NC)
        ] + [(lambda m: d2_ref[m], lambda r, m: x_ref[first + r, pl.ds(m, 1), :])]
        for r, acc in enumerate(contract(terms, zeros, LANES)):
            far1_ref[first + r] = rounded(acc)

    for first in (0, half):
        for s in range(2):
            lanes = slice(s * LANES, (s + 1) * LANES)
            terms = [(lambda m: d1_ref[m, :, lanes], lambda r, m: far1_ref[first + r, pl.ds(m, 1), :])]
            for r, acc in enumerate(contract(terms, zeros, LANES)):
                x0_ref[s, first + r] = acc
    unit = jnp.where(iota((leaves, leaves), 0) == iota((leaves, leaves), 1), 1.0, 0.0).astype(BF16)
    for r in range(rhs):
        tall = lax.dot_general(unit, jnp.concatenate([x0_ref[0, r], x0_ref[1, r]], axis=1).astype(BF16), NT, preferred_element_type=F32)
        at = 0
        for c in range(2):
            for b in range(2):
                for a in range(2):
                    rows_ref[pl.ds(rhs * (4 * a + 2 * b + c) + r, top, stride=8 * rhs), :K] = tall[at : at + top]
                    at += top
    chunk = 0
    for piece in range(PIECES):
        count = near_refs[piece].shape[1] // 256

        def leaf_group(g, near_value):
            lanes = pl.ds(pl.multiple_of(g * 256, 256), 256)
            coefs = rows_ref[pl.ds(pl.multiple_of(g * 64, 64), 64), :K].astype(BF16)
            far = own_blocks(dot(coefs, basis_ref[:, lanes]), rhs)
            out_ref[:, lanes] = (near_value + far).astype(BF16)

        start, stop = 0, count
        if piece == 0:
            leaf_group(0, head)
            start = 4
            for g in range(1, 4):
                leaf_group(chunk + g, near_refs[piece][:, g * 256 : (g + 1) * 256])
        if piece == PIECES - 1:
            stop = count - 4
            for g in range(stop, count - 1):
                leaf_group(chunk + g, near_refs[piece][:, g * 256 : (g + 1) * 256])
            leaf_group(chunk + count - 1, tail)

        @pl.loop(start // 4, stop // 4)
        def _(outer):
            for inner in range(4):
                g = outer * 4 + inner
                lanes = pl.ds(pl.multiple_of(g * 256, 256), 256)
                leaf_group(chunk + g, near_refs[piece][:, lanes])

        chunk += count


VM = pl.BlockSpec(memory_space=pltpu.VMEM)
SM = pl.BlockSpec(memory_space=pltpu.SMEM)
HBM = pl.BlockSpec(memory_space=pl.ANY)
PARAMS = pltpu.CompilerParams(vmem_limit_bytes=56 * 2**20)


def cost(flops, moved):
    return pl.CostEstimate(flops=flops, bytes_accessed=moved, transcendentals=0)


def shape(dims, kind=BF16):
    return jax.ShapeDtypeStruct(dims, kind)


def body(
    right_sides, near_blocks, near_leaves, leaf_basis, transfer_first, transfer_second, transfer_third,
    coupling_first, coupling_second, list_first, list_second, top_coupling, top_nodes,
):
    position = lax.axis_index(AXES)
    devices = lax.axis_size("branch") * lax.axis_size("sub")
    bits = devices.bit_length() - 1
    rhs, order = right_sides.shape
    leaves = order // M
    half = rhs // 2
    me = position.astype(jnp.int32).reshape(1)
    near_local = near_leaves.T - (position * leaves - HN)
    lists = (list_first.T, list_second.T, top_nodes.T)

    ups = pl.pallas_call(
        prep_up_kernel,
        out_shape=(shape((K, K, leaves)), shape((K, K, LANES)), shape((K, K, LANES))),
        in_specs=[VM] * 3,
        out_specs=(VM,) * 3,
        compiler_params=PARAMS,
    )(transfer_first, transfer_second, transfer_third)
    downs = pl.pallas_call(
        prep_rest_kernel,
        out_shape=(
            shape((K, K, leaves)), shape((K, K, LANES)), shape((K, K, LANES)),
            shape((NC, K, K, LANES)), shape((NC, K, K, LANES)), shape((NFAR * top_coupling.shape[3] // LANES, K, K, LANES)),
        ),
        in_specs=[VM] * 6,
        out_specs=(VM,) * 6,
        scratch_shapes=[pltpu.VMEM((K * K, LANES), F32)],
        compiler_params=PARAMS,
        cost_estimate=cost(10**9, 9 * 2**20),
    )(*ups, coupling_first, coupling_second, top_coupling)
    d1, d2, d3, m1, m2, m3 = downs
    sent_rows = half // 2 * K + K + 2 * rhs
    chunks = order // CHUNK
    cuts = [chunks * i // PIECES for i in range(PIECES + 1)]

    def product(vectors):
        sent, coef1, coef2 = pl.pallas_call(
            up_kernel,
            out_shape=(shape((sent_rows, LANES)), shape((rhs, K, LANES)), shape((half, K, LANES))),
            in_specs=[VM] * 5,
            out_specs=(VM,) * 3,
            scratch_shapes=[
                pltpu.VMEM((leaves * rhs, LANES), F32),
                pltpu.VMEM((leaves // LANES, rhs, K, LANES), F32),
                pltpu.VMEM((rhs, K, LANES), F32),
                pltpu.VMEM((half, K, LANES), F32),
            ],
            compiler_params=PARAMS,
            cost_estimate=cost(10**8, 3 * 2**20),
        )(vectors, leaf_basis, *ups)
        nears = []
        for i in range(PIECES):
            count = cuts[i + 1] - cuts[i]
            nears.append(
                pl.pallas_call(
                    functools.partial(near_kernel, cuts[i]),
                    out_shape=shape((rhs, count * CHUNK), F32),
                    in_specs=[SM, VM, HBM],
                    out_specs=VM,
                    scratch_shapes=[
                        pltpu.VMEM((leaves + 2 * HN, rhs, LANES), BF16),
                        pltpu.VMEM((NEAR, M, count * CHUNK), BF16),
                        pltpu.SemaphoreType.DMA((count,)),
                    ],
                    compiler_params=PARAMS,
                    cost_estimate=cost(10**9, 8 * 2**20),
                )(near_local, vectors, near_blocks)
            )
        every = sent[None]
        for b in reversed(range(bits)):
            pairs = [(i, i ^ (1 << b)) for i in range(devices)]
            other = lax.ppermute(every, AXES, pairs)
            if b:
                every = jnp.concatenate([every, other], axis=0)
        return pl.pallas_call(
            functools.partial(down_kernel, bits),
            grid=(1,),
            out_shape=shape((rhs, order)),
            in_specs=[SM, SM] + [VM] * 5 + [VM] * PIECES
            + [
                pl.BlockSpec((NEAR, M, 256), lambda i: (0, 0, 0)),
                pl.BlockSpec((NEAR, M, 256), lambda i: (0, 0, order // 256 - 1)),
            ]
            + [VM] * 10,
            out_specs=VM,
            scratch_shapes=[
                pltpu.VMEM((rhs * K, devices * (leaves // 8)), BF16),
                pltpu.VMEM((rhs, NC * K, LANES), F32),
                pltpu.VMEM((rhs, K, LANES), F32),
                pltpu.VMEM((rhs, K, LANES), F32),
                pltpu.VMEM((leaves // LANES, rhs, K, LANES), F32),
                pltpu.VMEM((leaves * rhs, LANES), F32),
                pltpu.VMEM((16, rhs, LANES), BF16),
            ],
            compiler_params=PARAMS,
            cost_estimate=cost(10**9, 8 * 2**20),
        )(me, near_local, every, other, coef1, coef2, vectors, *nears, near_blocks, near_blocks, leaf_basis,
          *lists, m1, m2, m3, d1, d2, d3)

    first_image = product(right_sides)
    second_image = product(first_image)
    return (first_image, second_image)


def solution(mesh):
    tree = P(None, None, AXES)
    placed = (
        P("groups", AXES), tree, P(AXES, None), P(None, AXES), tree, tree, tree,
        P(None, None, None, AXES), P(None, None, None, AXES), P(AXES, None), P(AXES, None),
        P(None, None, None, AXES), P(AXES, None),
    )
    return jax.shard_map(
        body, mesh=mesh, in_specs=placed, out_specs=(P("groups", AXES), P("groups", AXES)), check_vma=False
    )
```

profile of v0, /device:TPU:0, one launch (start us, length us, event | category | flops | bytes accessed | tf_op | source)
XLA Modules:
  0.0 130.0 jit_solution(3852093208195724057)
XLA Ops:
  0.6 2.5 %shard_map.140 = (bf16[32,32,256]{2,1,0:T(8,128)(2,1)}, bf16[32,32,128]{2,1,0:T(8,128)(2,1)}, bf16[32,32,128]{2,1,0:T(8,128)(2,1)}) custom-call(bf16[32,32,256]{2,1,0:T(8,128)(2,1)} %first_ref.1, bf16[32,32,128]{2,1,0:T(8,128)(2,1)} %second_ref.1, bf16[32,32,64]{2,1,0:T(8,128)(2,1)} %third_ref.1), custom_call_target="tpu_custom_call" | custom-call | tf_op jit(solution)/shard_map/pallas_call | solution.py:494
  3.2 9.2 %shard_map.141 = (bf16[192,128]{1,0:T(8,128)(2,1)}, bf16[16,32,128]{2,1,0:T(8,128)(2,1)}, bf16[8,32,128]{2,1,0:T(8,128)(2,1)}) custom-call(bf16[16,16384]{1,0:T(8,128)(2,1)} %z_ref.9, bf16[32,16384]{1,0:T(8,128)(2,1)} %refs_5_.3, bf16[32,32,256]{2,1,0:T(8,128)(2,1)} %get-tuple-element.17.up1_ref, bf16[32,32,128]{2,1,0:T(8,128)(2,1)} %get-tuple-element.18.up2_ref, ...), custom_call_target="tpu_custom_call" | custom-call | flops 100000000 | bytes 3145728 | tf_op jit(solution)/shard_map/pallas_call | solution.py:519
  12.4 4.0 %collective-permute-start = (bf16[1,192,128]{2,1,0:T(8,128)(2,1)}, bf16[1,192,128]{2,1,0:T(8,128)(2,1)S(1)}, u32[]{:S(2)}, u32[]{:S(2)}) collective-permute-start(bf16[1,192,128]{2,1,0:T(8,128)(2,1)} %bitcast.8), channel_id=1, source_target_pairs={{0,8},{1,9},{2,10},{3,11},{4,12},{5,13},{6,14},{7,15},{8,0},{9,1},... | collective-permute-start | bytes 147464 | tf_op jit(solution)/shard_map/ppermute | solution.py:554
  16.4 2.8 %collective-permute-done = bf16[1,192,128]{2,1,0:T(8,128)(2,1)S(1)} collective-permute-done((bf16[1,192,128]{2,1,0:T(8,128)(2,1)}, bf16[1,192,128]{2,1,0:T(8,128)(2,1)S(1)}, u32[]{:S(2)}, u32[]{:S(2)}) %collective-permute-start) | collective-permute-done | bytes 49184 | tf_op jit(solution)/shard_map/ppermute | solution.py:554
  20.0 1.5 %collective-permute-start.1 = (bf16[2,192,128]{2,1,0:T(8,128)(2,1)S(1)}, bf16[2,192,128]{2,1,0:T(8,128)(2,1)S(1)}, u32[]{:S(2)}, u32[]{:S(2)}) collective-permute-start(bf16[2,192,128]{2,1,0:T(8,128)(2,1)S(1)} %pad_maximum_fusion.4), channel_id=1, source_target_pairs={{0,4},{1,5},{2,6},{3,7},{4,0},{5,1},{6,2},{7,3},{8,12},{9,13},{10,... | collective-permute-start | bytes 294920 | tf_op jit(solution)/shard_map/ppermute | solution.py:554
  21.5 3.2 %collective-permute-done.1 = bf16[2,192,128]{2,1,0:T(8,128)(2,1)S(1)} collective-permute-done((bf16[2,192,128]{2,1,0:T(8,128)(2,1)S(1)}, bf16[2,192,128]{2,1,0:T(8,128)(2,1)S(1)}, u32[]{:S(2)}, u32[]{:S(2)}) %collective-permute-start.1) | collective-permute-done | bytes 98336 | tf_op jit(solution)/shard_map/ppermute | solution.py:554
  25.5 1.8 %collective-permute-start.2 = (bf16[4,192,128]{2,1,0:T(8,128)(2,1)S(1)}, bf16[4,192,128]{2,1,0:T(8,128)(2,1)S(1)}, u32[]{:S(2)}, u32[]{:S(2)}) collective-permute-start(bf16[4,192,128]{2,1,0:T(8,128)(2,1)S(1)} %pad_maximum_fusion.2), channel_id=1, source_target_pairs={{0,2},{1,3},{2,0},{3,1},{4,6},{5,7},{6,4},{7,5},{8,10},{9,11},{10,... | collective-permute-start | bytes 589832 | tf_op jit(solution)/shard_map/ppermute | solution.py:554
  27.3 3.9 %collective-permute-done.2 = bf16[4,192,128]{2,1,0:T(8,128)(2,1)S(1)} collective-permute-done((bf16[4,192,128]{2,1,0:T(8,128)(2,1)S(1)}, bf16[4,192,128]{2,1,0:T(8,128)(2,1)S(1)}, u32[]{:S(2)}, u32[]{:S(2)}) %collective-permute-start.2) | collective-permute-done | bytes 196640 | tf_op jit(solution)/shard_map/ppermute | solution.py:554
  33.5 4.3 %shard_map.143.refs_1_ = f32[16,5120]{1,0:T(8,128)} custom-call(s32[5,256]{1,0:T(8,128)} %subtract_bitcast_fusion.leaves_ref, bf16[16,16384]{1,0:T(8,128)(2,1)} %z_ref.9, bf16[5,64,16384]{2,1,0:T(8,128)(2,1)} %refs_4_.3), custom_call_target="tpu_custom_call" | custom-call | flops 1000000000 | bytes 8388608 | tf_op jit(solution)/shard_map/pallas_call | solution.py:537
  37.9 4.3 %shard_map.142.refs_0_ = f32[16,5120]{1,0:T(8,128)} custom-call(s32[5,256]{1,0:T(8,128)} %subtract_bitcast_fusion.leaves_ref, bf16[16,16384]{1,0:T(8,128)(2,1)} %z_ref.9, bf16[5,64,16384]{2,1,0:T(8,128)(2,1)} %refs_4_.3), custom_call_target="tpu_custom_call" | custom-call | flops 1000000000 | bytes 8388608 | tf_op jit(solution)/shard_map/pallas_call | solution.py:537
  42.2 4.7 %shard_map.144.refs_2_ = f32[16,6144]{1,0:T(8,128)} custom-call(s32[5,256]{1,0:T(8,128)} %subtract_bitcast_fusion.leaves_ref, bf16[16,16384]{1,0:T(8,128)(2,1)} %z_ref.9, bf16[5,64,16384]{2,1,0:T(8,128)(2,1)} %refs_4_.3), custom_call_target="tpu_custom_call" | custom-call | flops 1000000000 | bytes 8388608 | tf_op jit(solution)/shard_map/pallas_call | solution.py:537
  46.9 5.4 %shard_map.145 = (bf16[32,32,256]{2,1,0:T(8,128)(2,1)}, bf16[32,32,128]{2,1,0:T(8,128)(2,1)}, bf16[32,32,128]{2,1,0:T(8,128)(2,1)}, bf16[3,32,32,128]{3,2,1,0:T(...) custom-call(bf16[32,32,256]{2,1,0:T(8,128)(2,1)} %get-tuple-element.17.up1_ref, ...), custom_call_target="tpu_custom_call" | custom-call | flops 1000000000 | bytes 9437184 | tf_op jit(solution)/shard_map/pallas_call | solution.py:501
  53.0 17.4 %shard_map.146.z_ref = bf16[16,16384]{1,0:T(8,128)(2,1)} custom-call(s32[1]{0:T(128)} %bitcast.me_ref, s32[5,256]{1,0:T(8,128)} %subtract_bitcast_fusion.leaves_ref, bf16[8,192,128]{2,1,0:T(8,128)(2,1)} %copy-done, bf16[8,192,128]{2,1,0:T(8,128)(2,1)} %copy-done.2, bf16[16,32,128]{2,1,0:T(8,128)(2,1)} %get-tuple-element.21.coef1_ref, ...), custom_call_target="tpu_custom_call" | custom-call | flops 1000000000 | bytes 8388608 | tf_op jit(solution)/shard_map/pallas_call | solution.py:557
  70.5 9.4 %shard_map.147 = (bf16[192,128]{1,0:T(8,128)(2,1)}, bf16[16,32,128]{2,1,0:T(8,128)(2,1)}, bf16[8,32,128]{2,1,0:T(8,128)(2,1)}) custom-call(bf16[16,16384]{1,0:T(8,128)(2,1)} %shard_map.146.z_ref, bf16[32,16384]{1,0:T(8,128)(2,1)} %refs_5_.3, bf16[32,32,256]{2,1,0:T(8,128)(2,1)} %get-tuple-element.17.up1_ref, bf16[32,32,128]{2,1,0:T(8,128)(2,1)} %get-tuple-element.18.up2_ref, ...), custom_call_target="tpu_custom_call" | custom-call | flops 100000000 | bytes 3145728 | tf_op jit(solution)/shard_map/pallas_call | solution.py:519
  79.8 2.4 %collective-permute-start.4 = (bf16[1,192,128]{2,1,0:T(8,128)(2,1)}, bf16[1,192,128]{2,1,0:T(8,128)(2,1)S(1)}, u32[]{:S(2)}, u32[]{:S(2)}) collective-permute-start(bf16[1,192,128]{2,1,0:T(8,128)(2,1)} %bitcast.12), channel_id=1, source_target_pairs={{0,8},{1,9},{2,10},{3,11},{4,12},{5,13},{6,14},{7,15},{8,0},{9,1},... | collective-permute-start | bytes 147464 | tf_op jit(solution)/shard_map/ppermute | solution.py:554
  82.3 2.8 %collective-permute-done.4 = bf16[1,192,128]{2,1,0:T(8,128)(2,1)S(1)} collective-permute-done((bf16[1,192,128]{2,1,0:T(8,128)(2,1)}, bf16[1,192,128]{2,1,0:T(8,128)(2,1)S(1)}, u32[]{:S(2)}, u32[]{:S(2)}) %collective-permute-start.4) | collective-permute-done | bytes 49184 | tf_op jit(solution)/shard_map/ppermute | solution.py:554
  85.8 1.8 %collective-permute-start.5 = (bf16[2,192,128]{2,1,0:T(8,128)(2,1)S(1)}, bf16[2,192,128]{2,1,0:T(8,128)(2,1)S(1)}, u32[]{:S(2)}, u32[]{:S(2)}) collective-permute-start(bf16[2,192,128]{2,1,0:T(8,128)(2,1)S(1)} %pad_maximum_fusion.5), channel_id=1, source_target_pairs={{0,4},{1,5},{2,6},{3,7},{4,0},{5,1},{6,2},{7,3},{8,12},{9,13},{10,... | collective-permute-start | bytes 294920 | tf_op jit(solution)/shard_map/ppermute | solution.py:554
  87.7 3.0 %collective-permute-done.5 = bf16[2,192,128]{2,1,0:T(8,128)(2,1)S(1)} collective-permute-done((bf16[2,192,128]{2,1,0:T(8,128)(2,1)S(1)}, bf16[2,192,128]{2,1,0:T(8,128)(2,1)S(1)}, u32[]{:S(2)}, u32[]{:S(2)}) %collective-permute-start.5) | collective-permute-done | bytes 98336 | tf_op jit(solution)/shard_map/ppermute | solution.py:554
  91.4 1.7 %collective-permute-start.6 = (bf16[4,192,128]{2,1,0:T(8,128)(2,1)S(1)}, bf16[4,192,128]{2,1,0:T(8,128)(2,1)S(1)}, u32[]{:S(2)}, u32[]{:S(2)}) collective-permute-start(bf16[4,192,128]{2,1,0:T(8,128)(2,1)S(1)} %pad_maximum_fusion.3), channel_id=1, source_target_pairs={{0,2},{1,3},{2,0},{3,1},{4,6},{5,7},{6,4},{7,5},{8,10},{9,11},{10,... | collective-permute-start | bytes 589832 | tf_op jit(solution)/shard_map/ppermute | solution.py:554
  93.1 4.3 %collective-permute-done.6 = bf16[4,192,128]{2,1,0:T(8,128)(2,1)S(1)} collective-permute-done((bf16[4,192,128]{2,1,0:T(8,128)(2,1)S(1)}, bf16[4,192,128]{2,1,0:T(8,128)(2,1)S(1)}, u32[]{:S(2)}, u32[]{:S(2)}) %collective-permute-start.6) | collective-permute-done | bytes 196640 | tf_op jit(solution)/shard_map/ppermute | solution.py:554
  98.4 4.4 %shard_map.149.refs_1_ = f32[16,5120]{1,0:T(8,128)} custom-call(s32[5,256]{1,0:T(8,128)} %subtract_bitcast_fusion.leaves_ref, bf16[16,16384]{1,0:T(8,128)(2,1)} %shard_map.146.z_ref, bf16[5,64,16384]{2,1,0:T(8,128)(2,1)} %refs_4_.3), custom_call_target="tpu_custom_call" | custom-call | flops 1000000000 | bytes 8388608 | tf_op jit(solution)/shard_map/pallas_call | solution.py:537
  102.8 4.3 %shard_map.148.refs_0_ = f32[16,5120]{1,0:T(8,128)} custom-call(s32[5,256]{1,0:T(8,128)} %subtract_bitcast_fusion.leaves_ref, bf16[16,16384]{1,0:T(8,128)(2,1)} %shard_map.146.z_ref, bf16[5,64,16384]{2,1,0:T(8,128)(2,1)} %refs_4_.3), custom_call_target="tpu_custom_call" | custom-call | flops 1000000000 | bytes 8388608 | tf_op jit(solution)/shard_map/pallas_call | solution.py:537
  107.1 4.6 %shard_map.150.refs_2_ = f32[16,6144]{1,0:T(8,128)} custom-call(s32[5,256]{1,0:T(8,128)} %subtract_bitcast_fusion.leaves_ref, bf16[16,16384]{1,0:T(8,128)(2,1)} %shard_map.146.z_ref, bf16[5,64,16384]{2,1,0:T(8,128)(2,1)} %refs_4_.3), custom_call_target="tpu_custom_call" | custom-call | flops 1000000000 | bytes 8388608 | tf_op jit(solution)/shard_map/pallas_call | solution.py:537
  112.5 17.4 %shard_map.151 = bf16[16,16384]{1,0:T(8,128)(2,1)} custom-call(s32[1]{0:T(128)} %bitcast.me_ref, s32[5,256]{1,0:T(8,128)} %subtract_bitcast_fusion.leaves_ref, bf16[8,192,128]{2,1,0:T(8,128)(2,1)} %copy-done.1, bf16[8,192,128]{2,1,0:T(8,128)(2,1)} %copy-done.3, bf16[16,32,128]{2,1,0:T(8,128)(2,1)} %get-tuple-element.30.coef1_ref, ...), custom_call_target="tpu_custom_call" | custom-call | flops 1000000000 | bytes 8388608 | tf_op jit(solution)/shard_map/pallas_call | solution.py:557
  (19 shorter events, 7.9 us)
Async XLA Ops:
  12.4 6.8 %collective-permute-start = (bf16[1,192,128]{2,1,0:T(8,128)(2,1)}, bf16[1,192,128]{2,1,0:T(8,128)(2,1)S(1)}, u32[]{:S(2)}, u32[]{:S(2)}) collective-permute-start(bf16[1,192,128]{2,1,0:T(8,128)(2,1)} %bitcast.8), channel_id=1, source_target_pairs={{0,8},{1,9},{2,10},{3,11},{4,12},{5,13},{6,14},{7,15},{8,0},{9,1},... | collective-permute-start | bytes 147464 | tf_op jit(solution)/shard_map/ppermute | solution.py:554
  20.0 4.7 %collective-permute-start.1 = (bf16[2,192,128]{2,1,0:T(8,128)(2,1)S(1)}, bf16[2,192,128]{2,1,0:T(8,128)(2,1)S(1)}, u32[]{:S(2)}, u32[]{:S(2)}) collective-permute-start(bf16[2,192,128]{2,1,0:T(8,128)(2,1)S(1)} %pad_maximum_fusion.4), channel_id=1, source_target_pairs={{0,4},{1,5},{2,6},{3,7},{4,0},{5,1},{6,2},{7,3},{8,12},{9,13},{10,... | collective-permute-start | bytes 294920 | tf_op jit(solution)/shard_map/ppermute | solution.py:554
  25.5 5.7 %collective-permute-start.2 = (bf16[4,192,128]{2,1,0:T(8,128)(2,1)S(1)}, bf16[4,192,128]{2,1,0:T(8,128)(2,1)S(1)}, u32[]{:S(2)}, u32[]{:S(2)}) collective-permute-start(bf16[4,192,128]{2,1,0:T(8,128)(2,1)S(1)} %pad_maximum_fusion.2), channel_id=1, source_target_pairs={{0,2},{1,3},{2,0},{3,1},{4,6},{5,7},{6,4},{7,5},{8,10},{9,11},{10,... | collective-permute-start | bytes 589832 | tf_op jit(solution)/shard_map/ppermute | solution.py:554
  32.1 10.1 %copy-start = (bf16[8,192,128]{2,1,0:T(8,128)(2,1)}, bf16[8,192,128]{2,1,0:T(8,128)(2,1)S(1)}, u32[]{:S(2)}) copy-start(bf16[8,192,128]{2,1,0:T(8,128)(2,1)S(1)} %pad_maximum_fusion.early_ref) | copy-start | bytes 1179652
  32.1 20.2 %collective-permute-start.3 = (bf16[8,192,128]{2,1,0:T(8,128)(2,1)S(1)}, bf16[8,192,128]{2,1,0:T(8,128)(2,1)S(1)}, u32[]{:S(2)}, u32[]{:S(2)}) collective-permute-start(bf16[8,192,128]{2,1,0:T(8,128)(2,1)S(1)} %pad_maximum_fusion.early_ref), channel_id=1, source_target_pairs={{0,1},{1,0},{2,3},{3,2},{4,5},{5,4},{6,7},{7,6},{8,9},{9,8},{10,11... | collective-permute-start | bytes 1179656 | tf_op jit(solution)/shard_map/ppermute | solution.py:554
  52.3 0.7 copy-start.2
  79.8 5.2 %collective-permute-start.4 = (bf16[1,192,128]{2,1,0:T(8,128)(2,1)}, bf16[1,192,128]{2,1,0:T(8,128)(2,1)S(1)}, u32[]{:S(2)}, u32[]{:S(2)}) collective-permute-start(bf16[1,192,128]{2,1,0:T(8,128)(2,1)} %bitcast.12), channel_id=1, source_target_pairs={{0,8},{1,9},{2,10},{3,11},{4,12},{5,13},{6,14},{7,15},{8,0},{9,1},... | collective-permute-start | bytes 147464 | tf_op jit(solution)/shard_map/ppermute | solution.py:554
  85.8 4.8 %collective-permute-start.5 = (bf16[2,192,128]{2,1,0:T(8,128)(2,1)S(1)}, bf16[2,192,128]{2,1,0:T(8,128)(2,1)S(1)}, u32[]{:S(2)}, u32[]{:S(2)}) collective-permute-start(bf16[2,192,128]{2,1,0:T(8,128)(2,1)S(1)} %pad_maximum_fusion.5), channel_id=1, source_target_pairs={{0,4},{1,5},{2,6},{3,7},{4,0},{5,1},{6,2},{7,3},{8,12},{9,13},{10,... | collective-permute-start | bytes 294920 | tf_op jit(solution)/shard_map/ppermute | solution.py:554
  91.4 6.0 %collective-permute-start.6 = (bf16[4,192,128]{2,1,0:T(8,128)(2,1)S(1)}, bf16[4,192,128]{2,1,0:T(8,128)(2,1)S(1)}, u32[]{:S(2)}, u32[]{:S(2)}) collective-permute-start(bf16[4,192,128]{2,1,0:T(8,128)(2,1)S(1)} %pad_maximum_fusion.3), channel_id=1, source_target_pairs={{0,2},{1,3},{2,0},{3,1},{4,6},{5,7},{6,4},{7,5},{8,10},{9,11},{10,... | collective-permute-start | bytes 589832 | tf_op jit(solution)/shard_map/ppermute | solution.py:554
  98.3 8.8 %copy-start.1 = (bf16[8,192,128]{2,1,0:T(8,128)(2,1)}, bf16[8,192,128]{2,1,0:T(8,128)(2,1)S(1)}, u32[]{:S(2)}) copy-start(bf16[8,192,128]{2,1,0:T(8,128)(2,1)S(1)} %pad_maximum_fusion.1.early_ref) | copy-start | bytes 1179652
  98.3 13.5 %collective-permute-start.7 = (bf16[8,192,128]{2,1,0:T(8,128)(2,1)S(1)}, bf16[8,192,128]{2,1,0:T(8,128)(2,1)S(1)}, u32[]{:S(2)}, u32[]{:S(2)}) collective-permute-start(bf16[8,192,128]{2,1,0:T(8,128)(2,1)S(1)} %pad_maximum_fusion.1.early_ref), channel_id=1, source_target_pairs={{0,1},{1,0},{2,3},{3,2},{4,5},{5,4},{6,7},{7,6},{8,9},{9,8},{10,11... | collective-permute-start | bytes 1179656 | tf_op jit(solution)/shard_map/ppermute | solution.py:554
  111.8 0.8 copy-start.3
where the time goes:
time: 131 us; the launch traced here: 130 us
  Pallas kernels  88 us (67%)
  waiting for transfers between devices  20 us (15%)
  starting transfers between devices  13.4 us (10%)
  other arithmetic  6.27 us (5%)
  local copies, waits for them, and re-layouts  1.48 us (1%)
    pallas_call x2, Pallas kernels, product(): pl.pallas_call(functools.partial(down_kernel, bits), grid=(1,), out_shape...  34.8 us
    pallas_call x6, Pallas kernels, product(): pl.pallas_call(functools.partial(near_kernel, cuts[i]), out_shape=shape((...  26.7 us
    ppermute x8, waiting for transfers between devices, product(): other = lax.ppermute(every, AXES, pairs)  20 us
    pallas_call x2, Pallas kernels, product(): pl.pallas_call(up_kernel, out_shape=(shape((sent_rows, LANES)), shape((rh...  18.6 us
    ppermute x8, starting transfers between devices, product(): other = lax.ppermute(every, AXES, pairs)  13.4 us
    pallas_call x1, Pallas kernels, body(): pl.pallas_call(prep_rest_kernel, out_shape=(shape((K, K, leaves)), shape(...  5.44 us
    concatenate x6, other arithmetic, product(): every = jnp.concatenate([every, other], axis=0)  4.93 us
  transfers between devices with their start and end apart: 8, of which 6 were waited for; matrix products, arithmetic and copies ran while one was open for 1% of the time, Pallas kernels for 25%

commit v1 on v0

v1 whole, which is shorter than its diff:
```python
import functools

import jax
import jax.numpy as jnp
from jax import lax
from jax.experimental import pallas as pl
from jax.experimental.pallas import tpu as pltpu
from jax.sharding import PartitionSpec as P

M = 64
K = 32
NEAR = 5
NC = 3
NFAR = 8
HN = 2
HC = 2
LANES = 128
AXES = ("branch", "sub")
PIECES = 2
GROUPS = 64
UNROLL = 32
FIRST = 1
BATCH = 4
CHUNK = 1024
F32 = jnp.float32
BF16 = jnp.bfloat16
NT = (((1,), (1,)), ((), ()))


def iota(shape, dim):
    return lax.broadcasted_iota(jnp.int32, shape, dim)


def place(node, count, levels):
    where = jnp.zeros_like(node)
    for level in range(levels):
        count //= 2
        where = where + (node & 1) * count
        node = node >> 1
    return where + node


def place_static(node, count, levels):
    where = 0
    for level in range(levels):
        count //= 2
        where += (node & 1) * count
        node >>= 1
    return where + node


def lane_order(count, levels, copies=1):
    rows = place(iota((count, count * copies), 0), count, levels)
    columns = iota((count, count * copies), 1) & (count - 1)
    return jnp.where(rows == columns, 1.0, 0.0).astype(BF16)


def dot(a, b):
    return jnp.dot(a, b, preferred_element_type=F32)


def end_nodes(count):
    return (0, 1, count - 2, count - 1)


def end_columns(count, offset):
    row, lane = iota((count, LANES), 0), iota((count, LANES), 1) & 7
    hit = row < 0
    for e, node in enumerate(end_nodes(count)):
        hit = hit | ((row == node) & (lane == offset + e))
    return jnp.where(hit, 1.0, 0.0).astype(BF16)


def rounded(x):
    return x.astype(BF16).astype(F32)


def contract(terms, init, lanes):
    def step(position, accs):
        for matrix_at, x_at in terms:
            matrix = matrix_at(position).astype(F32)
            accs = tuple(acc + matrix * x_at(r, position) for r, acc in enumerate(accs))
        return accs

    return lax.fori_loop(0, K, step, init, unroll=UNROLL)


def prep_up_kernel(first_ref, second_ref, third_ref, up1_ref, up2_ref, up3_ref):
    for source, target, levels, copies in ((first_ref, up1_ref, 3, 1), (second_ref, up2_ref, 2, 1), (third_ref, up3_ref, 1, 2)):
        count = source.shape[2]
        order = lane_order(count, levels, copies)
        for k in range(0, K, 4):
            rows = source[k : k + 4].reshape(4 * K, count)
            target[k : k + 4] = dot(rows, order).astype(BF16).reshape(4, K, count * copies)


def prep_rest_kernel(up1_ref, up2_ref, up3_ref, c1_ref, c2_ref, c3_ref, d1_ref, d2_ref, d3_ref, m1_ref, m2_ref, m3_ref, ends_ref, wide_ref):
    for source, target in ((up1_ref, d1_ref), (up2_ref, d2_ref), (up3_ref, d3_ref)):
        for tile in range(source.shape[2] // LANES):
            lanes = slice(tile * LANES, (tile + 1) * LANES)
            wide_ref[...] = source[:, :, lanes].astype(F32).reshape(K * K, LANES)
            for m in range(K):
                target[m, :, lanes] = wide_ref[pl.ds(m, K, stride=K), :].astype(BF16)
    for source, target, levels, copies in ((c1_ref, m1_ref, 2, 1), (c2_ref, m2_ref, 1, 2)):
        count = source.shape[3]
        order = lane_order(count, levels, copies)
        for j in range(NC):
            for k in range(0, K, 8):
                rows = source[j, k : k + 8].reshape(8 * K, count)
                target[j, k : k + 8] = dot(rows, order).astype(BF16).reshape(8, K, LANES)
    low_ends = end_columns(LANES, 0)
    high_ends = end_columns(M, 4)
    for j in range(NC):
        for k in range(0, K, 8):
            low = dot(c1_ref[j, k : k + 8].reshape(8 * K, LANES), low_ends)
            high = dot(c2_ref[j, k : k + 8].reshape(8 * K, M), high_ends)
            ends_ref[j, k : k + 8] = (low + high).astype(BF16).reshape(8, K, LANES)
    top = c3_ref.shape[3]
    group = LANES // top
    for h in range(NFAR // group):
        for k in range(0, K, 8):
            total = None
            for q in range(group):
                put = jnp.where(iota((top, LANES), 0) + q * top == iota((top, LANES), 1), 1.0, 0.0).astype(BF16)
                part = dot(c3_ref[h * group + q, k : k + 8].reshape(8 * K, top), put)
                total = part if total is None else total + part
            m3_ref[h, k : k + 8] = total.astype(BF16).reshape(8, K, LANES)


def up_kernel(z_ref, basis_ref, up1_ref, up2_ref, up3_ref, sent_ref, coef1_ref, coef2_ref, rows_ref, x0_ref, x1_ref, x2_ref):
    rhs, order = z_ref.shape
    leaves = order // M
    top = leaves // 8
    low = iota((rhs, LANES), 1) < M
    zero = jnp.zeros((rhs, LANES), BF16)

    for outer in range(leaves // (4 * GROUPS)):
        coefs = []
        for inner in range(GROUPS):
            lanes = pl.ds(pl.multiple_of((outer * GROUPS + inner) * 256, 256), 256)
            z = z_ref[:, lanes]
            left, right = z[:, :LANES], z[:, LANES:]
            first = jnp.concatenate([jnp.where(low, left, zero), jnp.where(low, zero, left)], axis=0)
            second = jnp.concatenate([jnp.where(low, right, zero), jnp.where(low, zero, right)], axis=0)
            none = jnp.zeros_like(first)
            masked = jnp.concatenate(
                [jnp.concatenate([first, none], axis=1), jnp.concatenate([none, second], axis=1)], axis=0
            )
            coefs.append(lax.dot_general(masked, basis_ref[:, lanes], NT, preferred_element_type=F32))
        for inner in range(GROUPS):
            rows_ref[pl.ds(pl.multiple_of((outer * GROUPS + inner) * 64, 64), 64), :K] = coefs[inner]

    unit = jnp.where(iota((K, K), 0) == iota((K, K), 1), 1.0, 0.0).astype(BF16)
    for outer in range(rhs // 4):
        turned = []
        for inner in range(4):
            r = outer * 4 + inner
            pieces = []
            for c in range(2):
                for b in range(2):
                    for a in range(2):
                        pieces.append(rows_ref[pl.ds(rhs * (4 * a + 2 * b + c) + r, top, stride=8 * rhs), :K])
            tall = jnp.concatenate(pieces, axis=0).astype(BF16)
            turned.append(lax.dot_general(unit, tall, NT, preferred_element_type=F32))
        for inner in range(4):
            x0_ref[0, outer * 4 + inner] = turned[inner][:, :LANES]
            x0_ref[1, outer * 4 + inner] = turned[inner][:, LANES:]

    half = rhs // 2
    zeros = tuple(jnp.zeros((K, LANES), F32) for _ in range(half))
    for first in (0, half):
        terms = [
            (
                functools.partial(lambda s, k: up1_ref[k, :, s * LANES : (s + 1) * LANES], s),
                functools.partial(lambda s, r, k: x0_ref[s, first + r, pl.ds(k, 1), :], s),
            )
            for s in range(2)
        ]
        for r, acc in enumerate(contract(terms, zeros, LANES)):
            coef1_ref[first + r] = acc.astype(BF16)
            x1_ref[first + r] = rounded(acc)
    low = iota((K, LANES), 1) < M
    for first in (0, half):
        terms = [(lambda k: up2_ref[k], lambda r, k: x1_ref[first + r, pl.ds(k, 1), :])]
        for r, acc in enumerate(contract(terms, zeros, LANES)):
            total = rounded(acc + pltpu.roll(acc, 64, 1))
            if first == 0:
                x2_ref[r] = total
            else:
                both = jnp.where(low, x2_ref[r], total)
                x2_ref[r] = both
                coef2_ref[r] = both.astype(BF16)
    terms = [(lambda k: up3_ref[k], lambda r, k: x2_ref[r, pl.ds(k, 1), :])]
    sums = [acc + pltpu.roll(acc, 32, 1) for acc in contract(terms, zeros, LANES)]
    odd = (iota((K, LANES), 1) & 32) > 0
    for r in range(half // 2):
        sent_ref[r * K : (r + 1) * K] = jnp.where(odd, sums[r], pltpu.roll(sums[r + half // 2], 96, 1)).astype(BF16)

    def ends(count, offset, shift):
        row, column = iota((LANES, LANES), 0), iota((LANES, LANES), 1)
        hit = (row == -1)
        for copy in range(LANES // count):
            for e, node in enumerate((0, 1, count - 2, count - 1)):
                at = place_static(node, count, 2 if count == LANES else 1)
                hit = hit | ((row == copy * count + at) & (column == copy * M + offset + e))
        return jnp.where(hit, 1.0, 0.0).astype(BF16)

    first_ends = dot(x1_ref[...].astype(BF16).reshape(rhs * K, LANES), ends(LANES, 0, 0)).reshape(rhs, K, LANES)
    second_ends = dot(x2_ref[...].astype(BF16).reshape(half * K, LANES), ends(M, 4, 64)).reshape(half, K, LANES)
    packed = jnp.zeros((K, LANES), F32)
    for r in range(rhs):
        value = first_ends[r]
        if r < half:
            value = value + second_ends[r]
        packed = packed + (pltpu.roll(value, 8 * r, 1) if r else value)
    base = half // 2 * K
    sent_ref[base : base + K] = packed.astype(BF16)
    sent_ref[base + K : base + K + rhs] = z_ref[:, :LANES]
    sent_ref[base + K + rhs : base + K + 2 * rhs] = z_ref[:, order - LANES :]


def first_kernel(
    z_ref, basis_ref, first_ref, second_ref, third_ref,
    sent_ref, coef1_ref, coef2_ref, up1_ref, up2_ref, up3_ref, *scratch
):
    prep_up_kernel(first_ref, second_ref, third_ref, up1_ref, up2_ref, up3_ref)
    up_kernel(z_ref, basis_ref, up1_ref, up2_ref, up3_ref, sent_ref, coef1_ref, coef2_ref, *scratch)


def put_leaves(target_ref, tile, slot):
    low = iota(tile.shape, 1) < M
    wide = tile.astype(F32)
    swapped = pltpu.roll(wide, M, 1)
    target_ref[slot] = jnp.where(low, wide, swapped).astype(BF16)
    target_ref[slot + 1] = jnp.where(low, swapped, wide).astype(BF16)


def own_blocks(res, rhs):
    low = iota((rhs, LANES), 1) < M
    return jnp.concatenate(
        [
            jnp.where(low, res[:rhs, :LANES], res[rhs : 2 * rhs, :LANES]),
            jnp.where(low, res[2 * rhs : 3 * rhs, LANES:], res[3 * rhs :, LANES:]),
        ],
        axis=1,
    )


def near_group(read, weights, rhs):
    low = iota((rhs, LANES), 1) < M
    rows = []
    for leaf in range(4):
        z = [read(j, leaf) for j in range(NEAR)]
        rows.append(jnp.concatenate([jnp.where(low, z[0], z[1]), jnp.where(low, z[2], z[3]), z[4][:, :M]], axis=1))
    return own_blocks(dot(jnp.concatenate(rows, axis=0), weights), rhs)


def near_kernel(chunk0, leaves_ref, z_ref, blocks_ref, out_ref, z_leaves_ref):
    rhs, order = z_ref.shape
    chunks = out_ref.shape[1] // CHUNK
    per = CHUNK // M
    first_tile = max(chunk0 * (CHUNK // LANES) - 1, 0)
    last_tile = min((chunk0 + chunks) * (CHUNK // LANES) + 1, order // LANES)
    for t in range(first_tile, last_tile):
        put_leaves(z_leaves_ref, z_ref[:, t * LANES : (t + 1) * LANES], 2 * t + HN)

    @pl.loop(0, chunks)
    def _(c):
        for g in range(CHUNK // 256):
            leaf0 = (chunk0 + c) * per + 4 * g
            here = pl.ds(pl.multiple_of(c * CHUNK + g * 256, 256), 256)
            there = pl.ds(pl.multiple_of((chunk0 + c) * CHUNK + g * 256, 256), 256)
            weights = blocks_ref[:, :, there].reshape(NEAR * M, 256)
            out_ref[:, here] = near_group(lambda j, e: z_leaves_ref[leaves_ref[j, leaf0 + e]], weights, rhs)


def bit_reverse(value, bits):
    out = jnp.zeros_like(value)
    for b in range(bits):
        out = out + (((value >> b) & 1) << (bits - 1 - b))
    return out


def in_order(rows, count, levels):
    wide = jnp.concatenate([rows.astype(F32)] + [jnp.zeros((8 - rows.shape[0], count), F32)], axis=0).astype(BF16)
    return dot(wide, lane_order(count, levels)).astype(jnp.int32)


def own_rows_of(nodes, me, count, levels):
    local = nodes - me * count
    inside = (local >= 0) & (local < count)
    return in_order(jnp.where(inside, place(jnp.clip(local, 0, count - 1), count, levels), -1), count, levels)


def couple_kernel(me_ref, coef1_ref, coef2_ref, list1_ref, list2_ref, m1_ref, m2_ref, far1_ref, far2_ref, picks_ref):
    rhs, half = coef1_ref.shape[0], coef2_ref.shape[0]
    me = me_ref[0]
    zeros = tuple(jnp.zeros((K, LANES), F32) for _ in range(half))

    def run(matrix_ref, first):
        terms = [
            (
                functools.partial(lambda j, k: matrix_ref[j, k], j),
                functools.partial(lambda j, r, k: picks_ref[first + r, pl.ds(j * K + k, 1), :], j),
            )
            for j in range(NC)
        ]
        return contract(terms, zeros, LANES)

    rows = own_rows_of(list2_ref[...], me, M, 1)
    copy_of = iota((LANES, LANES), 1) // M
    tables = []
    for j in range(NC):
        row = jnp.concatenate([rows[j : j + 1], rows[j : j + 1]], axis=1)
        tables.append(jnp.where((iota((LANES, LANES), 0) - copy_of * M == row) & (row >= 0), 1.0, 0.0))
    table = jnp.concatenate(tables, axis=1).astype(BF16)
    picked = dot(coef2_ref[...].reshape(half * K, LANES), table).reshape(half, K, NC * LANES)
    for j in range(NC):
        picks_ref[:half, j * K : (j + 1) * K, :] = picked[:, :, j * LANES : (j + 1) * LANES]
    for r, acc in enumerate(run(m2_ref, 0)):
        far2_ref[r] = acc
    rows = own_rows_of(list1_ref[...], me, LANES, 2)
    table = jnp.concatenate(
        [jnp.where(iota((LANES, LANES), 0) == rows[j : j + 1], 1.0, 0.0) for j in range(NC)], axis=1
    ).astype(BF16)
    picked = dot(coef1_ref[...].reshape(rhs * K, LANES), table).reshape(rhs, K, NC * LANES)
    for j in range(NC):
        picks_ref[:, j * K : (j + 1) * K, :] = picked[:, :, j * LANES : (j + 1) * LANES]
    for first in (0, half):
        for r, acc in enumerate(run(m1_ref, first)):
            far1_ref[first + r] = acc


def halo_codes(nodes, me, count, offset):
    local = nodes - me * count
    code = jnp.where(local < 0, local + 5, jnp.where(local >= count, local - count + 1, 0))
    code = jnp.where(code > 0, code + offset, 0)
    wide = jnp.concatenate([code.astype(F32)] + [jnp.zeros((8 - code.shape[0], count), F32)], axis=0).astype(BF16)
    return dot(wide, end_columns(count, offset))


def down_kernel(bits, me_ref, leaves_ref, early_ref, late_ref, far1_in_ref, far2_in_ref, z_ref, *refs):
    near_refs = refs[:PIECES]
    (blocks_ref, basis_ref, list1_ref, list2_ref, top_ref, ends_ref, m3_ref, d1_ref, d2_ref, d3_ref,
     out_hbm, out_ref, every_ref, picks_ref, far1_ref, x_ref, x0_ref, rows_ref, z_leaves_ref, sems) = refs[PIECES:]
    rhs, order = z_ref.shape
    leaves = order // M
    top = leaves // 8
    half = rhs // 2
    me = me_ref[0]
    devices = 1 << bits
    own_rows = half // 2 * K

    def block(device, rows):
        at = bit_reverse(jnp.bitwise_xor(device, me), bits)
        early = early_ref[jnp.minimum(at, devices // 2 - 1), rows]
        late = late_ref[jnp.maximum(at - devices // 2, 0), rows]
        return jnp.where(at < devices // 2, early.astype(F32), late.astype(F32))

    before = jnp.maximum(me - 1, 0)
    after = jnp.minimum(me + 1, devices - 1)

    z_before = block(before, slice(own_rows + K + rhs, own_rows + K + 2 * rhs)).astype(BF16)
    z_after = block(after, slice(own_rows + K, own_rows + K + rhs)).astype(BF16)
    put_leaves(z_leaves_ref, z_before, 0)
    for t in range(3):
        put_leaves(z_leaves_ref, z_ref[:, t * LANES : (t + 1) * LANES], 2 + 2 * t)
        put_leaves(z_leaves_ref, z_ref[:, order - (3 - t) * LANES : order - (2 - t) * LANES or None], 8 + 2 * t)
    put_leaves(z_leaves_ref, z_after, 14)
    head = near_group(lambda j, e: z_leaves_ref[leaves_ref[j, e]], blocks_ref[:, :, :256].reshape(NEAR * M, 256), rhs)
    skip = leaves + 2 * HN - 16
    tail = near_group(
        lambda j, e: z_leaves_ref[leaves_ref[j, leaves - 4 + e] - skip], blocks_ref[:, :, order - 256 :].reshape(NEAR * M, 256), rhs
    )

    sides = slice(own_rows, own_rows + K)
    halo = jnp.where((iota((K, LANES), 1) & 2) > 0, block(before, sides), block(after, sides)).astype(BF16)
    codes = (halo_codes(list1_ref[...], me, LANES, 0) + halo_codes(list2_ref[...], me, M, 4)).astype(jnp.int32)
    lane_group = iota((LANES, LANES), 1) & -8
    sums = []
    for j in range(NC):
        code = codes[j : j + 1]
        table = jnp.where((iota((LANES, LANES), 0) == lane_group + code - 1) & (code > 0), 1.0, 0.0).astype(BF16)
        x_ref[j] = dot(halo, table)
    for j in range(NC):
        total = jnp.zeros((K, LANES), F32)
        for k in range(K):
            total = total + ends_ref[j, k].astype(F32) * x_ref[j, k : k + 1, :]
        sums.append(total)
    outer = sums[0] + sums[1] + sums[2]
    turned = jnp.concatenate([pltpu.roll(outer, LANES - 8 * r, 1) if r else outer for r in range(rhs)], axis=0)
    coarse = turned.astype(BF16)
    fine = (turned - coarse.astype(F32)).astype(BF16)

    def scatter(count, offset):
        row, column = iota((LANES, LANES), 0), iota((LANES, LANES), 1)
        hit = row < 0
        for copy in range(LANES // count):
            for e, node in enumerate(end_nodes(count)):
                at = place_static(node, count, 2 if count == LANES else 1)
                hit = hit | ((column == copy * count + at) & (row == copy * M + offset + e))
        return jnp.where(hit, 1.0, 0.0).astype(BF16)

    put = scatter(LANES, 0)
    outer1 = (dot(coarse, put) + dot(fine, put)).reshape(rhs, K, LANES)
    put = scatter(M, 4)
    outer2 = (dot(coarse[: half * K], put) + dot(fine[: half * K], put)).reshape(half, K, LANES)

    group = iota((own_rows, LANES), 1) // top
    per = LANES // top
    for tile in range(devices // per):
        source = early_ref if tile < devices // per // 2 else late_ref
        first = tile * per - (0 if tile < devices // per // 2 else devices // 2)
        parts = [source[first + q, :own_rows].astype(F32) for q in range(per)]
        for g in range(per):
            merged = None
            for q in range(per):
                shift = (q - g) * top % LANES
                moved = pltpu.roll(parts[q], shift, 1) if shift else parts[q]
                merged = moved if merged is None else jnp.where(group == q, moved, merged)
            every_ref[g * own_rows : (g + 1) * own_rows, tile * LANES : (tile + 1) * LANES] = merged.astype(BF16)
    nodes = top_ref[...]
    rows = bit_reverse(jnp.bitwise_xor(nodes // top, me), bits) * top + nodes % top
    hot = []
    for j in range(NFAR):
        hot.append(jnp.where(iota((devices * top, top), 0) == rows[j : j + 1], 1.0, 0.0).astype(BF16))
    for h in range(NFAR // per):
        wide = None
        for q in range(per):
            put = jnp.where(iota((top, LANES), 0) + q * top == iota((top, LANES), 1), 1.0, 0.0).astype(BF16)
            part = dot(hot[h * per + q], put)
            wide = part if wide is None else wide + part
        picked = dot(every_ref[...], wide.astype(BF16))
        picks_ref[:, h * K : (h + 1) * K, :] = picked.reshape(rhs, K, LANES)
    zeros = tuple(jnp.zeros((K, LANES), F32) for _ in range(half))
    groups_of = [1, 0, 3, 2]

    def slot(r):
        quarter = rhs // 4
        return groups_of[r // quarter] * quarter + r % quarter

    low = iota((K, LANES), 1) < M
    kept = {}
    for first in range(0, rhs, half):
        terms = [
            (
                functools.partial(lambda h, k: m3_ref[h, k], h),
                functools.partial(lambda h, r, k: picks_ref[slot(first + r), pl.ds(h * K + k, 1), :], h),
            )
            for h in range(NFAR // per)
        ]
        for r, acc in enumerate(contract(terms, zeros, LANES)):
            acc = acc + pltpu.roll(acc, 64, 1)
            acc = rounded(acc + pltpu.roll(acc, 32, 1))
            if first == 0:
                x_ref[r] = acc
            else:
                x_ref[r] = jnp.where(low, x_ref[r], acc)

    terms = [(lambda m: d3_ref[m], lambda r, m: x_ref[r, pl.ds(m, 1), :])]
    start = tuple(far2_in_ref[r] + outer2[r] for r in range(half))
    for r, acc in enumerate(contract(terms, start, LANES)):
        value = rounded(acc)
        swapped = pltpu.roll(value, M, 1)
        x_ref[r] = jnp.where(low, value, swapped)
        x_ref[r + half] = jnp.where(low, swapped, value)

    for first in (0, half):
        terms = [(lambda m: d2_ref[m], lambda r, m: x_ref[first + r, pl.ds(m, 1), :])]
        start = tuple(far1_in_ref[first + r] + outer1[first + r] for r in range(half))
        for r, acc in enumerate(contract(terms, start, LANES)):
            far1_ref[first + r] = rounded(acc)

    for first in (0, half):
        for s in range(2):
            lanes = slice(s * LANES, (s + 1) * LANES)
            terms = [(lambda m: d1_ref[m, :, lanes], lambda r, m: far1_ref[first + r, pl.ds(m, 1), :])]
            for r, acc in enumerate(contract(terms, zeros, LANES)):
                x0_ref[s, first + r] = acc
    unit = jnp.where(iota((leaves, leaves), 0) == iota((leaves, leaves), 1), 1.0, 0.0).astype(BF16)
    for outer in range(rhs // BATCH):
        turned = []
        for inner in range(BATCH):
            r = outer * BATCH + inner
            wide = jnp.concatenate([x0_ref[0, r], x0_ref[1, r]], axis=1).astype(BF16)
            turned.append(lax.dot_general(unit, wide, NT, preferred_element_type=F32))
        for inner in range(BATCH):
            at = 0
            for c in range(2):
                for b in range(2):
                    for a in range(2):
                        start = rhs * (4 * a + 2 * b + c) + outer * BATCH + inner
                        rows_ref[pl.ds(start, top, stride=8 * rhs), :K] = turned[inner][at : at + top]
                        at += top

    def far_group(g):
        lanes = slice(g * 256, (g + 1) * 256)
        coefs = rows_ref[g * 64 : (g + 1) * 64, :K].astype(BF16)
        return dot(coefs, basis_ref[:, lanes])

    total = leaves // 4
    parts = 4
    for part in range(parts):
        inside = range(part * total // parts, (part + 1) * total // parts)
        fars = [far_group(g) for g in inside]
        for g, far in zip(inside, fars):
            if g == 0:
                near = head
            elif g == total - 1:
                near = tail
            else:
                at = 0
                while g * 256 >= at + near_refs[0].shape[1]:
                    at += near_refs[0].shape[1]
                near = near_refs[at // near_refs[0].shape[1]][:, g * 256 - at : (g + 1) * 256 - at]
            out_ref[:, g * 256 : (g + 1) * 256] = (near + own_blocks(far, rhs)).astype(BF16)
        lanes = slice(part * order // parts, (part + 1) * order // parts)
        pltpu.make_async_copy(out_ref.at[:, lanes], out_hbm.at[:, lanes], sems.at[part]).start()
    for part in range(parts):
        lanes = slice(part * order // parts, (part + 1) * order // parts)
        pltpu.make_async_copy(out_ref.at[:, lanes], out_hbm.at[:, lanes], sems.at[part]).wait()


VM = pl.BlockSpec(memory_space=pltpu.VMEM)
SM = pl.BlockSpec(memory_space=pltpu.SMEM)
HBM = pl.BlockSpec(memory_space=pltpu.HBM)


def params(mib):
    return pltpu.CompilerParams(vmem_limit_bytes=mib * 2**20)


def cost(flops, moved):
    return pl.CostEstimate(flops=flops, bytes_accessed=moved, transcendentals=0)


def shape(dims, kind=BF16):
    return jax.ShapeDtypeStruct(dims, kind)


def body(
    right_sides, near_blocks, near_leaves, leaf_basis, transfer_first, transfer_second, transfer_third,
    coupling_first, coupling_second, list_first, list_second, top_coupling, top_nodes,
):
    position = lax.axis_index(AXES)
    devices = lax.axis_size("branch") * lax.axis_size("sub")
    bits = devices.bit_length() - 1
    rhs, order = right_sides.shape
    leaves = order // M
    half = rhs // 2
    me = position.astype(jnp.int32).reshape(1)
    near_local = near_leaves.T - (position * leaves - HN)
    lists = (list_first.T, list_second.T, top_nodes.T)

    sent_rows = half // 2 * K + K + 2 * rhs
    up_shapes = (shape((sent_rows, LANES)), shape((rhs, K, LANES)), shape((half, K, LANES)))
    up_scratch = [
        pltpu.VMEM((leaves * rhs, LANES), F32),
        pltpu.VMEM((leaves // LANES, rhs, K, LANES), F32),
        pltpu.VMEM((rhs, K, LANES), F32),
        pltpu.VMEM((half, K, LANES), F32),
    ]
    *upward, up1, up2, up3 = pl.pallas_call(
        first_kernel,
        out_shape=up_shapes
        + (shape((K, K, leaves)), shape((K, K, LANES)), shape((K, K, LANES))),
        in_specs=[VM] * 5,
        out_specs=(VM,) * 6,
        scratch_shapes=up_scratch,
        compiler_params=params(12),
        cost_estimate=cost(FIRST * 10**9, 3 * 2**20),
    )(right_sides, leaf_basis, transfer_first, transfer_second, transfer_third)
    vectors, basis, blocks = right_sides, leaf_basis, near_blocks
    cut = order // PIECES

    def prepare(up1, up2, up3):
        return pl.pallas_call(
            prep_rest_kernel,
            out_shape=(
                shape((K, K, leaves)), shape((K, K, LANES)), shape((K, K, LANES)),
                shape((NC, K, K, LANES)), shape((NC, K, K, LANES)),
                shape((NFAR * top_coupling.shape[3] // LANES, K, K, LANES)), shape((NC, K, K, LANES)),
            ),
            in_specs=[VM] * 6,
            out_specs=(VM,) * 7,
            scratch_shapes=[pltpu.VMEM((K * K, LANES), F32)],
            compiler_params=params(16),
            cost_estimate=cost(10**9, 9 * 2**20),
        )(up1, up2, up3, coupling_first, coupling_second, top_coupling)

    def near_piece(i, vectors):
        return pl.pallas_call(
            functools.partial(near_kernel, i * cut // CHUNK),
            out_shape=shape((rhs, cut), F32),
            in_specs=[SM, VM, VM],
            out_specs=VM,
            scratch_shapes=[pltpu.VMEM((leaves + 2 * HN, rhs, LANES), BF16)],
            compiler_params=params(16),
            cost_estimate=cost(10**9, 8 * 2**20),
        )(near_local, vectors, blocks)

    def couple(coef1, coef2, m1, m2):
        return pl.pallas_call(
            couple_kernel,
            out_shape=(shape((rhs, K, LANES), F32), shape((half, K, LANES), F32)),
            in_specs=[SM] + [VM] * 6,
            out_specs=(VM,) * 2,
            scratch_shapes=[pltpu.VMEM((rhs, NC * K, LANES), F32)],
            compiler_params=params(16),
            cost_estimate=cost(10**9, 8 * 2**20),
        )(me, coef1, coef2, lists[0], lists[1], m1, m2)

    def exchange(sent, works):
        every, done = sent[None], []
        for step, b in enumerate(reversed(range(bits))):
            pairs = [(i, i ^ (1 << b)) for i in range(devices)]
            other = lax.ppermute(every, AXES, pairs)
            if step < len(works):
                result = works[step](every)
                other, result = lax.optimization_barrier((other, result))
                done.append(result)
            if b:
                every = jnp.concatenate([every, other], axis=0)
        return every, other, done

    def held(values, every):
        return lax.optimization_barrier((*values, every))[:-1]

    def down(every, other, far1, far2, vectors, nears, prepared, keep):
        d1, d2, d3, _, _, m3, ends = prepared
        out = shape((rhs, order))
        results = pl.pallas_call(
            functools.partial(down_kernel, bits),
            out_shape=(out, out) if keep else (out,),
            in_specs=[SM, SM] + [VM] * 5 + [VM] * PIECES + [VM] * 10,
            out_specs=(HBM, VM) if keep else (HBM,),
            scratch_shapes=([] if keep else [pltpu.VMEM((rhs, order), BF16)])
            + [
                pltpu.VMEM((rhs * K, devices * (leaves // 8)), BF16),
                pltpu.VMEM((rhs, NFAR * K * (leaves // 8) // LANES, LANES), F32),
                pltpu.VMEM((rhs, K, LANES), F32),
                pltpu.VMEM((rhs, K, LANES), F32),
                pltpu.VMEM((leaves // LANES, rhs, K, LANES), F32),
                pltpu.VMEM((leaves * rhs, LANES), F32),
                pltpu.VMEM((16, rhs, LANES), BF16),
                pltpu.SemaphoreType.DMA((4,)),
            ],
            compiler_params=params(24),
            cost_estimate=cost(10**9, 8 * 2**20),
        )(me, near_local, every, other, far1, far2, vectors, *nears, blocks, basis, *lists, ends, m3, d1, d2, d3)
        return results

    sent, coef1, coef2 = upward
    prepared = []
    works = [
        lambda every: near_piece(0, *held((vectors,), every)),
        lambda every: prepared.extend(prepare(*held((up1, up2, up3), every))) or tuple(prepared),
        lambda every: couple(*held((coef1, coef2), every), *prepared[3:5]),
        lambda every: near_piece(1, *held((vectors,), every)),
    ]
    every, other, (near0, prepared, fars, near1) = exchange(sent, works)
    first_image, second_vectors = down(every, other, *fars, vectors, (near0, near1), prepared, True)
    sent, coef1, coef2 = pl.pallas_call(
        up_kernel,
        out_shape=up_shapes,
        in_specs=[VM] * 5,
        out_specs=(VM,) * 3,
        scratch_shapes=up_scratch,
        compiler_params=params(12),
        cost_estimate=cost(10**8, 3 * 2**20),
    )(second_vectors, basis, up1, up2, up3)
    works = [
        lambda every: near_piece(0, *held((second_vectors,), every)),
        lambda every: near_piece(1, *held((second_vectors,), every)),
        lambda every: couple(*held((coef1, coef2), every), *prepared[3:5]),
    ]
    every, other, (near0, near1, fars) = exchange(sent, works)
    (second_image,) = down(every, other, *fars, second_vectors, (near0, near1), prepared, False)
    return (first_image, second_image)


def solution(mesh):
    tree = P(None, None, AXES)
    placed = (
        P("groups", AXES), tree, P(AXES, None), P(None, AXES), tree, tree, tree,
        P(None, None, None, AXES), P(None, None, None, AXES), P(AXES, None), P(AXES, None),
        P(None, None, None, AXES), P(AXES, None),
    )
    return jax.shard_map(
        body, mesh=mesh, in_specs=placed, out_specs=(P("groups", AXES), P("groups", AXES)), check_vma=False
    )
```

time: 131 us -> 78.9 us (0.60)
  Pallas kernels: 88 us -> 50.1 us
  waiting for transfers between devices: 20 us -> 6.27 us
  local copies, waits for them, and re-layouts: 1.48 us -> 10.3 us
  other arithmetic: 6.27 us -> 0.85 us
  starting transfers between devices: 13.4 us -> 9.88 us
    pallas_call x12 -> x11, Pallas kernels: 88 us -> 50.1 us  [the longest x2 17.7 us: down(): pl.pallas_call(functools.partial(down_kernel, bits), out_shape=(out, out)...]
    ppermute x8, waiting for transfers between devices: 20 us -> 6.27 us  [exchange(): other = lax.ppermute(every, AXES, pairs)]
    unnamed x8 -> x36, local copies, waits for them, and re-layouts: 1.48 us -> 10.3 us
    concatenate x6, other arithmetic: 4.93 us -> 0.15 us  [exchange(): every = jnp.concatenate([every, other], axis=0)]
    ppermute x8, starting transfers between devices: 13.4 us -> 9.88 us  [exchange(): other = lax.ppermute(every, AXES, pairs)]
  transfers between devices with their start and end apart: 8 -> 8, of which waited for: 6 -> 6; matrix products, arithmetic and copies ran while one was open for 1% -> 1% of each run, Pallas kernels for 25% -> 30%
where the time goes in v1:
time: 78.9 us; the launch traced here: 78.4 us
  Pallas kernels  50.1 us (63%)
  local copies, waits for them, and re-layouts  10.3 us (13%)
  starting transfers between devices  9.88 us (13%)
  waiting for transfers between devices  6.27 us (8%)
  between operations  1.08 us (1%)
  other arithmetic  0.85 us (1%)
    pallas_call x2, Pallas kernels, down(): pl.pallas_call(functools.partial(down_kernel, bits), out_shape=(out, out)...  17.7 us
    pallas_call x4, Pallas kernels, near_piece(): pl.pallas_call(functools.partial(near_kernel, i * cut // CHUNK), out_shap...  12.9 us
    unnamed x36, local copies, waits for them, and re-layouts  10.3 us
    ppermute x8, starting transfers between devices, exchange(): other = lax.ppermute(every, AXES, pairs)  9.88 us
    pallas_call x2, Pallas kernels, couple(): pl.pallas_call(couple_kernel, out_shape=(shape((rhs, K, LANES), F32), sha...  7.76 us
    ppermute x8, waiting for transfers between devices, exchange(): other = lax.ppermute(every, AXES, pairs)  6.27 us
    pallas_call x1, Pallas kernels, body(): pl.pallas_call(first_kernel, out_shape=up_shapes + (shape((K, K, leaves))...  4.65 us
    pallas_call x1, Pallas kernels, body(): pl.pallas_call(up_kernel, out_shape=up_shapes, in_specs=[VM] * 5, out_spe...  4.24 us
  transfers between devices with their start and end apart: 8, of which 6 were waited for; matrix products, arithmetic and copies ran while one was open for 1% of the time, Pallas kernels for 30%

profile of v1, /device:TPU:0, one launch (start us, length us, event | category | flops | bytes accessed | tf_op | source)
XLA Modules:
  0.0 78.4 jit_solution(4648207040034556262)
XLA Ops:
  0.6 1.2 %copy-done.1 = bf16[32,16384]{1,0:T(8,128)(2,1)S(1)} copy-done((bf16[32,16384]{1,0:T(8,128)(2,1)S(1)}, bf16[32,16384]{1,0:T(8,128)(2,1)}, u32[]{:S(2)}) %copy-start.1) | copy-done | bytes 1048600
  1.9 1.0 %copy-done.3 = bf16[16,16384]{1,0:T(8,128)(2,1)S(1)} copy-done((bf16[16,16384]{1,0:T(8,128)(2,1)S(1)}, bf16[16,16384]{1,0:T(8,128)(2,1)}, u32[]{:S(2)}) %copy-start.3) | copy-done | bytes 524312
  2.9 1.0 %copy-done.12 = bf16[32,32,256]{2,1,0:T(8,128)(2,1)S(1)} copy-done((bf16[32,32,256]{2,1,0:T(8,128)(2,1)S(1)}, bf16[32,32,256]{2,1,0:T(8,128)(2,1)}, u32[]{:S(2)}) %copy-start.12) | copy-done | bytes 524312
  3.9 0.9 %copy-done.13 = bf16[32,32,128]{2,1,0:T(8,128)(2,1)S(1)} copy-done((bf16[32,32,128]{2,1,0:T(8,128)(2,1)S(1)}, bf16[32,32,128]{2,1,0:T(8,128)(2,1)}, u32[]{:S(2)}) %copy-start.13) | copy-done | bytes 262168
  4.9 0.9 %copy-done.14 = bf16[32,32,64]{2,1,0:T(8,128)(2,1)S(1)} copy-done((bf16[32,32,64]{2,1,0:T(8,128)(2,1)S(1)}, bf16[32,32,64]{2,1,0:T(8,128)(2,1)}, u32[]{:S(2)}) %copy-start.14) | copy-done | bytes 131096
  5.9 4.6 %shard_map.140 = (bf16[192,128]{1,0:T(8,128)(2,1)S(1)}, bf16[16,32,128]{2,1,0:T(8,128)(2,1)S(1)}, bf16[8,32,128]{2,1,0:T(8,128)(2,1)S(1)}, bf16[32,32,256]{2,1,0...) custom-call(bf16[16,16384]{1,0:T(8,128)(2,1)S(1)} %copy-done.3, ...), custom_call_target="tpu_custom_call" | custom-call | flops 1000000000 | bytes 3145728 | tf_op jit(solution)/shard_map/pallas_call | solution.py:563
  10.5 4.1 %collective-permute-start = (bf16[1,192,128]{2,1,0:T(8,128)(2,1)S(1)}, bf16[1,192,128]{2,1,0:T(8,128)(2,1)S(1)}, u32[]{:S(2)}, u32[]{:S(2)}) collective-permute-start(bf16[1,192,128]{2,1,0:T(8,128)(2,1)S(1)} %bitcast.10), channel_id=1, source_target_pairs={{0,8},{1,9},{2,10},{3,11},{4,12},{5,13},{6,14},{7,15},{8,0},{9,1},... | collective-permute-start | bytes 147464 | tf_op jit(solution)/shard_map/ppermute | solution.py:617
  15.3 4.0 %copy-done = bf16[5,64,16384]{2,1,0:T(8,128)(2,1)S(1)} copy-done((bf16[5,64,16384]{2,1,0:T(8,128)(2,1)S(1)}, bf16[5,64,16384]{2,1,0:T(8,128)(2,1)}, u32[]{:S(2)}) %copy-start) | copy-done | bytes 10485784
  19.3 1.0 %copy-done.4 = bf16[16,16384]{1,0:T(8,128)(2,1)S(1)} copy-done((bf16[16,16384]{1,0:T(8,128)(2,1)S(1)}, bf16[16,16384]{1,0:T(8,128)(2,1)}, u32[]{:S(2)}) %copy-start.4) | copy-done | bytes 524312
  20.4 3.3 %shard_map.141.refs_0_ = f32[16,8192]{1,0:T(8,128)S(1)} custom-call(s32[5,256]{1,0:T(8,128)S(1)} %subtract_bitcast_fusion.leaves_ref, bf16[16,16384]{1,0:T(8,128)(2,1)S(1)} %copy-done.4, bf16[5,64,16384]{2,1,0:T(8,128)(2,1)S(1)} %copy-done), custom_call_target="tpu_custom_call" | custom-call | flops 1000000000 | bytes 8388608 | tf_op jit(solution)/shard_map/pallas_call | solution.py:592
  23.7 1.6 %collective-permute-start.1 = (bf16[2,192,128]{2,1,0:T(8,128)(2,1)S(1)}, bf16[2,192,128]{2,1,0:T(8,128)(2,1)S(1)}, u32[]{:S(2)}, u32[]{:S(2)}) collective-permute-start(bf16[2,192,128]{2,1,0:T(8,128)(2,1)S(1)} %pad_maximum_fusion.4), channel_id=1, source_target_pairs={{0,4},{1,5},{2,6},{3,7},{4,0},{5,1},{6,2},{7,3},{8,12},{9,13},{10,... | collective-permute-start | bytes 294920 | tf_op jit(solution)/shard_map/ppermute | solution.py:617
  25.3 2.8 %shard_map.142 = (bf16[32,32,256]{2,1,0:T(8,128)(2,1)S(1)}, bf16[32,32,128]{2,1,0:T(8,128)(2,1)S(1)}, bf16[32,32,128]{2,1,0:T(8,128)(2,1)S(1)}, bf16[3,32,32,128...) custom-call(bf16[32,32,256]{2,1,0:T(8,128)(2,1)S(1)} %get-tuple-elem, ...), custom_call_target="tpu_custom_call" | custom-call | flops 1000000000 | bytes 9437184 | tf_op jit(solution)/shard_map/pallas_call | solution.py:577
  28.4 1.6 %collective-permute-start.2 = (bf16[4,192,128]{2,1,0:T(8,128)(2,1)S(1)}, bf16[4,192,128]{2,1,0:T(8,128)(2,1)S(1)}, u32[]{:S(2)}, u32[]{:S(2)}) collective-permute-start(bf16[4,192,128]{2,1,0:T(8,128)(2,1)S(1)} %pad_maximum_fusion.2), channel_id=1, source_target_pairs={{0,2},{1,3},{2,0},{3,1},{4,6},{5,7},{6,4},{7,5},{8,10},{9,11},{10,... | collective-permute-start | bytes 589832 | tf_op jit(solution)/shard_map/ppermute | solution.py:617
  30.0 3.9 %shard_map.143 = (f32[16,32,128]{2,1,0:T(8,128)S(1)}, f32[8,32,128]{2,1,0:T(8,128)S(1)}) custom-call(s32[1]{0:T(128)} %bitcast.me_ref, bf16[16,32,128]{2,1,0:T(8,128)(2,1)S(1)} %get-tuple-element.76.coef1_ref, bf16[8,32,128]{2,1,0:T(8,128)(2,1)S(1)} %get-tuple-element.77.coef2_ref, s32[3,128]{1,0:T(4,128)S(1)} %bitcast.20, s32[3,64]{1,0:T(4,128)S(1)} %bitcast.24, ...), custom_call_target="tpu_custom_call" | custom-call | flops 1000000000 | bytes 8388608 | tf_op jit(solution)/shard_map/pallas_call | solution.py:603
  34.5 3.3 %shard_map.144.refs_1_ = f32[16,8192]{1,0:T(8,128)S(1)} custom-call(s32[5,256]{1,0:T(8,128)S(1)} %subtract_bitcast_fusion.leaves_ref, bf16[16,16384]{1,0:T(8,128)(2,1)S(1)} %copy-done.5, bf16[5,64,16384]{2,1,0:T(8,128)(2,1)S(1)} %bitcast.9), custom_call_target="tpu_custom_call" | custom-call | flops 1000000000 | bytes 8388608 | tf_op jit(solution)/shard_map/pallas_call | solution.py:592
  37.9 8.9 %shard_map.145 = (bf16[16,16384]{1,0:T(8,128)(2,1)}, bf16[16,16384]{1,0:T(8,128)(2,1)S(1)}) custom-call(s32[1]{0:T(128)} %bitcast.me_ref, s32[5,256]{1,0:T(8,128)S(1)} %subtract_bitcast_fusion.leaves_ref, bf16[8,192,128]{2,1,0:T(8,128)(2,1)S(1)} %pad_maximum_fusion.early_ref, bf16[8,192,128]{2,1,0:T(8,128)(2,1)S(1)} %collective-permute-done.3.late_ref, ...), custom_call_target="tpu_custom_call" | custom-call | flops 1000000000 | bytes 8388608 | tf_op jit(solution)/shard_map/pallas_call | solution.py:632
  46.7 4.2 %shard_map.146 = (bf16[192,128]{1,0:T(8,128)(2,1)S(1)}, bf16[16,32,128]{2,1,0:T(8,128)(2,1)S(1)}, bf16[8,32,128]{2,1,0:T(8,128)(2,1)S(1)}) custom-call(bf16[16,16384]{1,0:T(8,128)(2,1)S(1)} %get-tuple-element.97.z_ref, bf16[32,16384]{1,0:T(8,128)(2,1)S(1)} %copy-done.2, bf16[32,32,256]{2,1,0:T(8,128)(2,1)S(1)} %get-tuple-element.63.up1_ref, ...), custom_call_target="tpu_custom_call" | custom-call | flops 100000000 | bytes 3145728 | tf_op jit(solution)/shard_map/pallas_call | solution.py:663
  51.4 3.1 %shard_map.147.refs_0_ = f32[16,8192]{1,0:T(8,128)S(1)} custom-call(s32[5,256]{1,0:T(8,128)S(1)} %subtract_bitcast_fusion.leaves_ref, bf16[16,16384]{1,0:T(8,128)(2,1)S(1)} %get-tuple-element.97.z_ref, bf16[5,64,16384]{2,1,0:T(8,128)(2,1)S(1)} %bitcast.9), custom_call_target="tpu_custom_call" | custom-call | flops 1000000000 | bytes 8388608 | tf_op jit(solution)/shard_map/pallas_call | solution.py:592
  54.4 2.7 %collective-permute-done.4 = bf16[1,192,128]{2,1,0:T(8,128)(2,1)S(1)} collective-permute-done((bf16[1,192,128]{2,1,0:T(8,128)(2,1)S(1)}, bf16[1,192,128]{2,1,0:T(8,128)(2,1)S(1)}, u32[]{:S(2)}, u32[]{:S(2)}) %collective-permute-start.4) | collective-permute-done | bytes 49184 | tf_op jit(solution)/shard_map/ppermute | solution.py:617
  57.5 3.3 %shard_map.148.refs_1_ = f32[16,8192]{1,0:T(8,128)S(1)} custom-call(s32[5,256]{1,0:T(8,128)S(1)} %subtract_bitcast_fusion.leaves_ref, bf16[16,16384]{1,0:T(8,128)(2,1)S(1)} %get-tuple-element.97.z_ref, bf16[5,64,16384]{2,1,0:T(8,128)(2,1)S(1)} %bitcast.9), custom_call_target="tpu_custom_call" | custom-call | flops 1000000000 | bytes 8388608 | tf_op jit(solution)/shard_map/pallas_call | solution.py:592
  61.8 1.6 %collective-permute-start.6 = (bf16[4,192,128]{2,1,0:T(8,128)(2,1)S(1)}, bf16[4,192,128]{2,1,0:T(8,128)(2,1)S(1)}, u32[]{:S(2)}, u32[]{:S(2)}) collective-permute-start(bf16[4,192,128]{2,1,0:T(8,128)(2,1)S(1)} %pad_maximum_fusion.3), channel_id=1, source_target_pairs={{0,2},{1,3},{2,0},{3,1},{4,6},{5,7},{6,4},{7,5},{8,10},{9,11},{10,... | collective-permute-start | bytes 589832 | tf_op jit(solution)/shard_map/ppermute | solution.py:617
  63.4 3.9 %shard_map.149 = (f32[16,32,128]{2,1,0:T(8,128)S(1)}, f32[8,32,128]{2,1,0:T(8,128)S(1)}) custom-call(s32[1]{0:T(128)} %bitcast.me_ref, bf16[16,32,128]{2,1,0:T(8,128)(2,1)S(1)} %get-tuple-element.101.coef1_ref, bf16[8,32,128]{2,1,0:T(8,128)(2,1)S(1)} %get-tuple-element.102.coef2_ref, s32[3,128]{1,0:T(4,128)S(1)} %bitcast.22, s32[3,64]{1,0:T(4,128)S(1)} %bitcast.26, ...), custom_call_target="tpu_custom_call" | custom-call | flops 1000000000 | bytes 8388608 | tf_op jit(solution)/shard_map/pallas_call | solution.py:603
  67.7 1.7 %collective-permute-done.7.late_ref = bf16[8,192,128]{2,1,0:T(8,128)(2,1)S(1)} collective-permute-done((bf16[8,192,128]{2,1,0:T(8,128)(2,1)S(1)}, bf16[8,192,128]{2,1,0:T(8,128)(2,1)S(1)}, u32[]{:S(2)}, u32[]{:S(2)}) %collective-permute-start.7) | collective-permute-done | bytes 393248 | tf_op jit(solution)/shard_map/ppermute | solution.py:617
  69.4 8.9 %shard_map.150 = bf16[16,16384]{1,0:T(8,128)(2,1)} custom-call(s32[1]{0:T(128)} %bitcast.me_ref, s32[5,256]{1,0:T(8,128)S(1)} %subtract_bitcast_fusion.leaves_ref, bf16[8,192,128]{2,1,0:T(8,128)(2,1)S(1)} %pad_maximum_fusion.1.early_ref, bf16[8,192,128]{2,1,0:T(8,128)(2,1)S(1)} %collective-permute-done.7.late_ref, ...), custom_call_target="tpu_custom_call" | custom-call | flops 1000000000 | bytes 8388608 | tf_op jit(solution)/shard_map/pallas_call | solution.py:632
  (47 shorter events, 3.8 us)
Async XLA Ops:
  0.6 1.2 %copy-start.1 = (bf16[32,16384]{1,0:T(8,128)(2,1)S(1)}, bf16[32,16384]{1,0:T(8,128)(2,1)}, u32[]{:S(2)}) copy-start(bf16[32,16384]{1,0:T(8,128)(2,1)} %refs_3_.3) | copy-start | bytes 3145732
  1.9 1.0 %copy-start.3 = (bf16[16,16384]{1,0:T(8,128)(2,1)S(1)}, bf16[16,16384]{1,0:T(8,128)(2,1)}, u32[]{:S(2)}) copy-start(bf16[16,16384]{1,0:T(8,128)(2,1)} %z_ref.5) | copy-start | bytes 1572868
  2.9 1.0 %copy-start.12 = (bf16[32,32,256]{2,1,0:T(8,128)(2,1)S(1)}, bf16[32,32,256]{2,1,0:T(8,128)(2,1)}, u32[]{:S(2)}) copy-start(bf16[32,32,256]{2,1,0:T(8,128)(2,1)} %first_ref.1) | copy-start | bytes 1572868
  5.8 19.5 %copy-start.6 = (bf16[8,32,32,32]{3,2,1,0:T(8,128)(2,1)S(1)}, bf16[8,32,32,32]{3,2,1,0:T(8,128)(2,1)}, u32[]{:S(2)}) copy-start(bf16[8,32,32,32]{3,2,1,0:T(8,128)(2,1)} %c3_ref.1) | copy-start | bytes 1572868
  5.8 24.1 %copy-start.10 = (s32[128,3]{0,1:T(4,128)S(1)}, s32[128,3]{0,1:T(4,128)}, u32[]{:S(2)}) copy-start(s32[128,3]{0,1:T(4,128)} %param.22) | copy-start | bytes 4612
  5.8 24.1 %copy-start.11 = (s32[64,3]{0,1:T(4,128)S(1)}, s32[64,3]{0,1:T(4,128)}, u32[]{:S(2)}) copy-start(s32[64,3]{0,1:T(4,128)} %param.23) | copy-start | bytes 2308
  10.5 13.1 %collective-permute-start = (bf16[1,192,128]{2,1,0:T(8,128)(2,1)S(1)}, bf16[1,192,128]{2,1,0:T(8,128)(2,1)S(1)}, u32[]{:S(2)}, u32[]{:S(2)}) collective-permute-start(bf16[1,192,128]{2,1,0:T(8,128)(2,1)S(1)} %bitcast.10), channel_id=1, source_target_pairs={{0,8},{1,9},{2,10},{3,11},{4,12},{5,13},{6,14},{7,15},{8,0},{9,1},... | collective-permute-start | bytes 147464 | tf_op jit(solution)/shard_map/ppermute | solution.py:617
  15.3 4.0 %copy-start = (bf16[5,64,16384]{2,1,0:T(8,128)(2,1)S(1)}, bf16[5,64,16384]{2,1,0:T(8,128)(2,1)}, u32[]{:S(2)}) copy-start(bf16[5,64,16384]{2,1,0:T(8,128)(2,1)} %refs_2_.3) | copy-start | bytes 31457284
  19.3 1.0 %copy-start.4 = (bf16[16,16384]{1,0:T(8,128)(2,1)S(1)}, bf16[16,16384]{1,0:T(8,128)(2,1)}, u32[]{:S(2)}) copy-start(bf16[16,16384]{1,0:T(8,128)(2,1)} %z_ref.5) | copy-start | bytes 1572868
  20.3 5.0 %copy-start.7 = (bf16[3,32,32,128]{3,2,1,0:T(8,128)(2,1)S(1)}, bf16[3,32,32,128]{3,2,1,0:T(8,128)(2,1)}, u32[]{:S(2)}) copy-start(bf16[3,32,32,128]{3,2,1,0:T(8,128)(2,1)} %c1_ref.1) | copy-start | bytes 2359300
  20.3 5.0 %copy-start.8 = (bf16[3,32,32,64]{3,2,1,0:T(8,128)(2,1)S(1)}, bf16[3,32,32,64]{3,2,1,0:T(8,128)(2,1)}, u32[]{:S(2)}) copy-start(bf16[3,32,32,64]{3,2,1,0:T(8,128)(2,1)} %c2_ref.1) | copy-start | bytes 1179652
  20.4 14.1 %slice-start = ((s8[10485760]{0:T(1024)(128)(4,1)}), s8[4194304]{0:T(1024)(128)(4,1)S(1)}, s32[]{:S(2)}) async-start(s8[10485760]{0:T(1024)(128)(4,1)} %bitcast.8), calls=%async_computation | async-start | bytes 8388608
  20.4 14.1 %slice-start.1 = ((s8[10485760]{0:T(1024)(128)(4,1)}), s8[4194304]{0:T(1024)(128)(4,1)S(1)}, s32[]{:S(2)}) async-start(s8[10485760]{0:T(1024)(128)(4,1)} %bitcast.8), calls=%async_computation.1 | async-start | bytes 8388608
  20.4 14.2 %copy-start.5 = (bf16[16,16384]{1,0:T(8,128)(2,1)S(1)}, bf16[16,16384]{1,0:T(8,128)(2,1)}, u32[]{:S(2)}) copy-start(bf16[16,16384]{1,0:T(8,128)(2,1)} %z_ref.5) | copy-start | bytes 1572868
  23.7 4.7 %collective-permute-start.1 = (bf16[2,192,128]{2,1,0:T(8,128)(2,1)S(1)}, bf16[2,192,128]{2,1,0:T(8,128)(2,1)S(1)}, u32[]{:S(2)}, u32[]{:S(2)}) collective-permute-start(bf16[2,192,128]{2,1,0:T(8,128)(2,1)S(1)} %pad_maximum_fusion.4), channel_id=1, source_target_pairs={{0,4},{1,5},{2,6},{3,7},{4,0},{5,1},{6,2},{7,3},{8,12},{9,13},{10,... | collective-permute-start | bytes 294920 | tf_op jit(solution)/shard_map/ppermute | solution.py:617
  25.3 9.2 %slice-start.2 = ((s8[10485760]{0:T(1024)(128)(4,1)}), s8[2097152]{0:T(1024)(128)(4,1)S(1)}, s32[]{:S(2)}) async-start(s8[10485760]{0:T(1024)(128)(4,1)} %bitcast.8), calls=%async_computation.2 | async-start | bytes 4194304
  25.3 12.5 %copy-start.2 = (bf16[32,16384]{1,0:T(8,128)(2,1)S(1)}, bf16[32,16384]{1,0:T(8,128)(2,1)}, u32[]{:S(2)}) copy-start(bf16[32,16384]{1,0:T(8,128)(2,1)} %refs_3_.3) | copy-start | bytes 3145732
  25.3 12.5 %copy-start.9 = (s32[32,8]{0,1:T(8,128)S(1)}, s32[32,8]{0,1:T(8,128)}, u32[]{:S(2)}) copy-start(s32[32,8]{0,1:T(8,128)} %param.25) | copy-start | bytes 3076
  28.4 6.0 %collective-permute-start.2 = (bf16[4,192,128]{2,1,0:T(8,128)(2,1)S(1)}, bf16[4,192,128]{2,1,0:T(8,128)(2,1)S(1)}, u32[]{:S(2)}, u32[]{:S(2)}) collective-permute-start(bf16[4,192,128]{2,1,0:T(8,128)(2,1)S(1)} %pad_maximum_fusion.2), channel_id=1, source_target_pairs={{0,2},{1,3},{2,0},{3,1},{4,6},{5,7},{6,4},{7,5},{8,10},{9,11},{10,... | collective-permute-start | bytes 589832 | tf_op jit(solution)/shard_map/ppermute | solution.py:617
  34.4 3.4 %collective-permute-start.3 = (bf16[8,192,128]{2,1,0:T(8,128)(2,1)S(1)}, bf16[8,192,128]{2,1,0:T(8,128)(2,1)S(1)}, u32[]{:S(2)}, u32[]{:S(2)}) collective-permute-start(bf16[8,192,128]{2,1,0:T(8,128)(2,1)S(1)} %pad_maximum_fusion.early_ref), channel_id=1, source_target_pairs={{0,1},{1,0},{2,3},{3,2},{4,5},{5,4},{6,7},{7,6},{8,9},{9,8},{10,11... | collective-permute-start | bytes 1179656 | tf_op jit(solution)/shard_map/ppermute | solution.py:617
  51.0 6.1 %collective-permute-start.4 = (bf16[1,192,128]{2,1,0:T(8,128)(2,1)S(1)}, bf16[1,192,128]{2,1,0:T(8,128)(2,1)S(1)}, u32[]{:S(2)}, u32[]{:S(2)}) collective-permute-start(bf16[1,192,128]{2,1,0:T(8,128)(2,1)S(1)} %bitcast.14), channel_id=1, source_target_pairs={{0,8},{1,9},{2,10},{3,11},{4,12},{5,13},{6,14},{7,15},{8,0},{9,1},... | collective-permute-start | bytes 147464 | tf_op jit(solution)/shard_map/ppermute | solution.py:617
  57.1 4.7 %collective-permute-start.5 = (bf16[2,192,128]{2,1,0:T(8,128)(2,1)S(1)}, bf16[2,192,128]{2,1,0:T(8,128)(2,1)S(1)}, u32[]{:S(2)}, u32[]{:S(2)}) collective-permute-start(bf16[2,192,128]{2,1,0:T(8,128)(2,1)S(1)} %pad_maximum_fusion.5), channel_id=1, source_target_pairs={{0,4},{1,5},{2,6},{3,7},{4,0},{5,1},{6,2},{7,3},{8,12},{9,13},{10,... | collective-permute-start | bytes 294920 | tf_op jit(solution)/shard_map/ppermute | solution.py:617
  61.8 5.7 %collective-permute-start.6 = (bf16[4,192,128]{2,1,0:T(8,128)(2,1)S(1)}, bf16[4,192,128]{2,1,0:T(8,128)(2,1)S(1)}, u32[]{:S(2)}, u32[]{:S(2)}) collective-permute-start(bf16[4,192,128]{2,1,0:T(8,128)(2,1)S(1)} %pad_maximum_fusion.3), channel_id=1, source_target_pairs={{0,2},{1,3},{2,0},{3,1},{4,6},{5,7},{6,4},{7,5},{8,10},{9,11},{10,... | collective-permute-start | bytes 589832 | tf_op jit(solution)/shard_map/ppermute | solution.py:617
  67.6 1.8 %collective-permute-start.7 = (bf16[8,192,128]{2,1,0:T(8,128)(2,1)S(1)}, bf16[8,192,128]{2,1,0:T(8,128)(2,1)S(1)}, u32[]{:S(2)}, u32[]{:S(2)}) collective-permute-start(bf16[8,192,128]{2,1,0:T(8,128)(2,1)S(1)} %pad_maximum_fusion.1.early_ref), channel_id=1, source_target_pairs={{0,1},{1,0},{2,3},{3,2},{4,5},{5,4},{6,7},{7,6},{8,9},{9,8},{10,11... | collective-permute-start | bytes 1179656 | tf_op jit(solution)/shard_map/ppermute | solution.py:617
  (2 other events, 1.9 us)

commit v2 on v1

--- a/solution.py
+++ b/solution.py
@@ -17,10 +17,8 @@
 LANES = 128
 AXES = ("branch", "sub")
 PIECES = 2
-GROUPS = 64
 UNROLL = 32
 FIRST = 1
-BATCH = 4
 CHUNK = 1024
 F32 = jnp.float32
 BF16 = jnp.bfloat16
@@ -127,44 +125,34 @@
             m3_ref[h, k : k + 8] = total.astype(BF16).reshape(8, K, LANES)
 
 
+def spread_basis(part):
+    low = iota((K, LANES), 1) < M
+    zero = jnp.zeros((K, LANES), BF16)
+    left, right = part[:, :LANES], part[:, LANES:]
+    first = jnp.concatenate([jnp.where(low, left, zero), jnp.where(low, zero, left), zero, zero], axis=0)
+    second = jnp.concatenate([zero, zero, jnp.where(low, right, zero), jnp.where(low, zero, right)], axis=0)
+    return jnp.concatenate([first, second], axis=1)
+
+
 def up_kernel(z_ref, basis_ref, up1_ref, up2_ref, up3_ref, sent_ref, coef1_ref, coef2_ref, rows_ref, x0_ref, x1_ref, x2_ref):
     rhs, order = z_ref.shape
     leaves = order // M
     top = leaves // 8
-    low = iota((rhs, LANES), 1) < M
-    zero = jnp.zeros((rhs, LANES), BF16)
-
-    for outer in range(leaves // (4 * GROUPS)):
-        coefs = []
-        for inner in range(GROUPS):
-            lanes = pl.ds(pl.multiple_of((outer * GROUPS + inner) * 256, 256), 256)
-            z = z_ref[:, lanes]
-            left, right = z[:, :LANES], z[:, LANES:]
-            first = jnp.concatenate([jnp.where(low, left, zero), jnp.where(low, zero, left)], axis=0)
-            second = jnp.concatenate([jnp.where(low, right, zero), jnp.where(low, zero, right)], axis=0)
-            none = jnp.zeros_like(first)
-            masked = jnp.concatenate(
-                [jnp.concatenate([first, none], axis=1), jnp.concatenate([none, second], axis=1)], axis=0
-            )
-            coefs.append(lax.dot_general(masked, basis_ref[:, lanes], NT, preferred_element_type=F32))
-        for inner in range(GROUPS):
-            rows_ref[pl.ds(pl.multiple_of((outer * GROUPS + inner) * 64, 64), 64), :K] = coefs[inner]
-
-    unit = jnp.where(iota((K, K), 0) == iota((K, K), 1), 1.0, 0.0).astype(BF16)
-    for outer in range(rhs // 4):
-        turned = []
-        for inner in range(4):
-            r = outer * 4 + inner
-            pieces = []
-            for c in range(2):
-                for b in range(2):
-                    for a in range(2):
-                        pieces.append(rows_ref[pl.ds(rhs * (4 * a + 2 * b + c) + r, top, stride=8 * rhs), :K])
-            tall = jnp.concatenate(pieces, axis=0).astype(BF16)
-            turned.append(lax.dot_general(unit, tall, NT, preferred_element_type=F32))
-        for inner in range(4):
-            x0_ref[0, outer * 4 + inner] = turned[inner][:, :LANES]
-            x0_ref[1, outer * 4 + inner] = turned[inner][:, LANES:]
+    groups = leaves // 4
+    for g in range(groups):
+        lanes = slice(g * 256, (g + 1) * 256)
+        rows_ref[g * rhs : (g + 1) * rhs] = lax.dot_general(
+            z_ref[:, lanes], spread_basis(basis_ref[:, lanes]), NT, preferred_element_type=F32
+        )
+    unit = jnp.where(iota((LANES, LANES), 0) == iota((LANES, LANES), 1), 1.0, 0.0).astype(BF16)
+    for r in range(rhs):
+        pieces = [rows_ref[pl.ds(a * rhs + r, top, stride=2 * rhs), :] for a in range(2)]
+        flat = jnp.concatenate(pieces, axis=0).astype(BF16)
+        both = jnp.concatenate([flat, flat], axis=0)
+        tall = lax.dot_general(unit, both, NT, preferred_element_type=F32)
+        keep = iota((K, LANES), 1) < M
+        for c in range(2):
+            x0_ref[c, r] = jnp.where(keep, tall[c * K : (c + 1) * K], tall[(2 + c) * K : (3 + c) * K])
 
     half = rhs // 2
     zeros = tuple(jnp.zeros((K, LANES), F32) for _ in range(half))
@@ -477,26 +465,21 @@
             terms = [(lambda m: d1_ref[m, :, lanes], lambda r, m: far1_ref[first + r, pl.ds(m, 1), :])]
             for r, acc in enumerate(contract(terms, zeros, LANES)):
                 x0_ref[s, first + r] = acc
-    unit = jnp.where(iota((leaves, leaves), 0) == iota((leaves, leaves), 1), 1.0, 0.0).astype(BF16)
-    for outer in range(rhs // BATCH):
-        turned = []
-        for inner in range(BATCH):
-            r = outer * BATCH + inner
-            wide = jnp.concatenate([x0_ref[0, r], x0_ref[1, r]], axis=1).astype(BF16)
-            turned.append(lax.dot_general(unit, wide, NT, preferred_element_type=F32))
-        for inner in range(BATCH):
-            at = 0
-            for c in range(2):
-                for b in range(2):
-                    for a in range(2):
-                        start = rhs * (4 * a + 2 * b + c) + outer * BATCH + inner
-                        rows_ref[pl.ds(start, top, stride=8 * rhs), :K] = turned[inner][at : at + top]
-                        at += top
+    groups = leaves // 4
+    node = iota((LANES, LANES), 0) & (groups - 1)
+    lane = (iota((LANES, LANES), 0) & -groups) + (node & 1) * top + (node >> 1)
+    turn = jnp.where(lane == iota((LANES, LANES), 1), 1.0, 0.0).astype(BF16)
+    for r in range(rhs):
+        flat = jnp.concatenate([x0_ref[0, r], x0_ref[1, r]], axis=0).astype(BF16)
+        both = jnp.concatenate([flat, flat], axis=0)
+        tall = lax.dot_general(turn, both, NT, preferred_element_type=F32)
+        keep = iota((groups, LANES), 1) < M
+        rows_ref[pl.ds(r, groups, stride=rhs), :] = jnp.where(keep, tall[:groups], tall[groups:])
 
     def far_group(g):
         lanes = slice(g * 256, (g + 1) * 256)
-        coefs = rows_ref[g * 64 : (g + 1) * 64, :K].astype(BF16)
-        return dot(coefs, basis_ref[:, lanes])
+        coefs = rows_ref[g * rhs : (g + 1) * rhs].astype(BF16)
+        return dot(coefs, spread_basis(basis_ref[:, lanes]))
 
     total = leaves // 4
     parts = 4
@@ -513,7 +496,7 @@
                 while g * 256 >= at + near_refs[0].shape[1]:
                     at += near_refs[0].shape[1]
                 near = near_refs[at // near_refs[0].shape[1]][:, g * 256 - at : (g + 1) * 256 - at]
-            out_ref[:, g * 256 : (g + 1) * 256] = (near + own_blocks(far, rhs)).astype(BF16)
+            out_ref[:, g * 256 : (g + 1) * 256] = (near + far).astype(BF16)
         lanes = slice(part * order // parts, (part + 1) * order // parts)
         pltpu.make_async_copy(out_ref.at[:, lanes], out_hbm.at[:, lanes], sems.at[part]).start()
     for part in range(parts):
@@ -528,6 +511,10 @@
 
 def params(mib):
     return pltpu.CompilerParams(vmem_limit_bytes=mib * 2**20)
+
+
+def whole(array):
+    return pl.BlockSpec(array.shape, lambda i: (0,) * len(array.shape), pipeline_mode=pl.Buffered(1))
 
 
 def cost(flops, moved):
@@ -555,7 +542,7 @@
     sent_rows = half // 2 * K + K + 2 * rhs
     up_shapes = (shape((sent_rows, LANES)), shape((rhs, K, LANES)), shape((half, K, LANES)))
     up_scratch = [
-        pltpu.VMEM((leaves * rhs, LANES), F32),
+        pltpu.VMEM((leaves // 4 * rhs, LANES), F32),
         pltpu.VMEM((leaves // LANES, rhs, K, LANES), F32),
         pltpu.VMEM((rhs, K, LANES), F32),
         pltpu.VMEM((half, K, LANES), F32),
@@ -564,10 +551,11 @@
         first_kernel,
         out_shape=up_shapes
         + (shape((K, K, leaves)), shape((K, K, LANES)), shape((K, K, LANES))),
-        in_specs=[VM] * 5,
+        grid=(1,),
+        in_specs=[whole(a) for a in (right_sides, leaf_basis, transfer_first, transfer_second, transfer_third)],
         out_specs=(VM,) * 6,
         scratch_shapes=up_scratch,
-        compiler_params=params(12),
+        compiler_params=params(56),
         cost_estimate=cost(FIRST * 10**9, 3 * 2**20),
     )(right_sides, leaf_basis, transfer_first, transfer_second, transfer_third)
     vectors, basis, blocks = right_sides, leaf_basis, near_blocks
@@ -641,7 +629,7 @@
                 pltpu.VMEM((rhs, K, LANES), F32),
                 pltpu.VMEM((rhs, K, LANES), F32),
                 pltpu.VMEM((leaves // LANES, rhs, K, LANES), F32),
-                pltpu.VMEM((leaves * rhs, LANES), F32),
+                pltpu.VMEM((leaves // 4 * rhs, LANES), F32),
                 pltpu.VMEM((16, rhs, LANES), BF16),
                 pltpu.SemaphoreType.DMA((4,)),
             ],

time: 78.9 us -> 73.9 us (0.937)
  local copies, waits for them, and re-layouts: 10.3 us -> 5.12 us
    unnamed x36 -> x38, local copies, waits for them, and re-layouts: 10.3 us -> 5.12 us
    pallas_call x1, Pallas kernels: 4.65 us -> 7.14 us  [body(): pl.pallas_call(first_kernel, out_shape=up_shapes + (shape((K, K, leaves))...]
    pallas_call x2, Pallas kernels: 17.7 us -> 15.7 us  [down(): pl.pallas_call(functools.partial(down_kernel, bits), out_shape=(out, out)...]
  transfers between devices with their start and end apart: 8 -> 8, of which waited for: 6 -> 6; matrix products, arithmetic and copies ran while one was open for 1% -> 1% of each run, Pallas kernels for 30% -> 32%
where the time goes in v2:
time: 73.9 us; the launch traced here: 73.7 us
  Pallas kernels  50.5 us (68%)
  starting transfers between devices  9.77 us (13%)
  waiting for transfers between devices  6.32 us (9%)
  local copies, waits for them, and re-layouts  5.12 us (7%)
  between operations  1.14 us (2%)
  other arithmetic  0.85 us (1%)
    pallas_call x2, Pallas kernels, down(): pl.pallas_call(functools.partial(down_kernel, bits), out_shape=(out, out)...  15.7 us
    pallas_call x4, Pallas kernels, near_piece(): pl.pallas_call(functools.partial(near_kernel, i * cut // CHUNK), out_shap...  12.7 us
    ppermute x8, starting transfers between devices, exchange(): other = lax.ppermute(every, AXES, pairs)  9.77 us
    pallas_call x2, Pallas kernels, couple(): pl.pallas_call(couple_kernel, out_shape=(shape((rhs, K, LANES), F32), sha...  7.76 us
    pallas_call x1, Pallas kernels, body(): pl.pallas_call(first_kernel, out_shape=up_shapes + (shape((K, K, leaves))...  7.14 us
    ppermute x8, waiting for transfers between devices, exchange(): other = lax.ppermute(every, AXES, pairs)  6.32 us
    unnamed x38, local copies, waits for them, and re-layouts  5.12 us
    pallas_call x1, Pallas kernels, body(): pl.pallas_call(up_kernel, out_shape=up_shapes, in_specs=[VM] * 5, out_spe...  4.37 us
  transfers between devices with their start and end apart: 8, of which 6 were waited for; matrix products, arithmetic and copies ran while one was open for 1% of the time, Pallas kernels for 32%

profile of v2, /device:TPU:0, one launch (start us, length us, event | category | flops | bytes accessed | tf_op | source)
XLA Modules:
  0.0 73.7 jit_solution(1632488528923482492)
XLA Ops:
  0.7 7.1 %shard_map.140 = (bf16[192,128]{1,0:T(8,128)(2,1)}, bf16[16,32,128]{2,1,0:T(8,128)(2,1)}, bf16[8,32,128]{2,1,0:T(8,128)(2,1)}, bf16[32,32,256]{2,1,0:T(8,128)(2,...) custom-call(bf16[16,16384]{1,0:T(8,128)(2,1)} %z_ref.5, bf16[32,16384]{1,0:T(8,128)(2,1)} %refs_3_.3, ...), custom_call_target="tpu_custom_call" | custom-call | flops 1000000000 | bytes 3145728 | tf_op jit(solution)/shard_map/pallas_call | solution.py:550
  7.8 4.0 %collective-permute-start = (bf16[1,192,128]{2,1,0:T(8,128)(2,1)}, bf16[1,192,128]{2,1,0:T(8,128)(2,1)S(1)}, u32[]{:S(2)}, u32[]{:S(2)}) collective-permute-start(bf16[1,192,128]{2,1,0:T(8,128)(2,1)} %bitcast.24), channel_id=1, source_target_pairs={{0,8},{1,9},{2,10},{3,11},{4,12},{5,13},{6,14},{7,15},{8,0},{9,1},... | collective-permute-start | bytes 147464 | tf_op jit(solution)/shard_map/ppermute | solution.py:605
  11.9 0.7 subtract_bitcast_fusion.leaves_ref
  12.6 4.0 %copy-done = bf16[5,64,16384]{2,1,0:T(8,128)(2,1)S(1)} copy-done((bf16[5,64,16384]{2,1,0:T(8,128)(2,1)S(1)}, bf16[5,64,16384]{2,1,0:T(8,128)(2,1)}, u32[]{:S(2)}) %copy-start) | copy-done | bytes 10485784
  16.6 1.0 %copy-done.2 = bf16[16,16384]{1,0:T(8,128)(2,1)S(1)} copy-done((bf16[16,16384]{1,0:T(8,128)(2,1)S(1)}, bf16[16,16384]{1,0:T(8,128)(2,1)}, u32[]{:S(2)}) %copy-start.2) | copy-done | bytes 524312
  17.7 3.1 %shard_map.141.refs_0_ = f32[16,8192]{1,0:T(8,128)S(1)} custom-call(s32[5,256]{1,0:T(8,128)S(1)} %subtract_bitcast_fusion.leaves_ref, bf16[16,16384]{1,0:T(8,128)(2,1)S(1)} %copy-done.2, bf16[5,64,16384]{2,1,0:T(8,128)(2,1)S(1)} %copy-done), custom_call_target="tpu_custom_call" | custom-call | flops 1000000000 | bytes 8388608 | tf_op jit(solution)/shard_map/pallas_call | solution.py:580
  20.8 1.6 %collective-permute-start.1 = (bf16[2,192,128]{2,1,0:T(8,128)(2,1)S(1)}, bf16[2,192,128]{2,1,0:T(8,128)(2,1)S(1)}, u32[]{:S(2)}, u32[]{:S(2)}) collective-permute-start(bf16[2,192,128]{2,1,0:T(8,128)(2,1)S(1)} %pad_maximum_fusion.4), channel_id=1, source_target_pairs={{0,4},{1,5},{2,6},{3,7},{4,0},{5,1},{6,2},{7,3},{8,12},{9,13},{10,... | collective-permute-start | bytes 294920 | tf_op jit(solution)/shard_map/ppermute | solution.py:605
  22.5 2.8 %shard_map.142 = (bf16[32,32,256]{2,1,0:T(8,128)(2,1)S(1)}, bf16[32,32,128]{2,1,0:T(8,128)(2,1)S(1)}, bf16[32,32,128]{2,1,0:T(8,128)(2,1)S(1)}, bf16[3,32,32,128...) custom-call(bf16[32,32,256]{2,1,0:T(8,128)(2,1)S(1)} %copy-done.4, ...), custom_call_target="tpu_custom_call" | custom-call | flops 1000000000 | bytes 9437184 | tf_op jit(solution)/shard_map/pallas_call | solution.py:565
  25.5 1.6 %collective-permute-start.2 = (bf16[4,192,128]{2,1,0:T(8,128)(2,1)S(1)}, bf16[4,192,128]{2,1,0:T(8,128)(2,1)S(1)}, u32[]{:S(2)}, u32[]{:S(2)}) collective-permute-start(bf16[4,192,128]{2,1,0:T(8,128)(2,1)S(1)} %pad_maximum_fusion.2), channel_id=1, source_target_pairs={{0,2},{1,3},{2,0},{3,1},{4,6},{5,7},{6,4},{7,5},{8,10},{9,11},{10,... | collective-permute-start | bytes 589832 | tf_op jit(solution)/shard_map/ppermute | solution.py:605
  27.1 3.9 %shard_map.143 = (f32[16,32,128]{2,1,0:T(8,128)S(1)}, f32[8,32,128]{2,1,0:T(8,128)S(1)}) custom-call(s32[1]{0:T(128)} %bitcast.me_ref, bf16[16,32,128]{2,1,0:T(8,128)(2,1)S(1)} %copy-done.13, bf16[8,32,128]{2,1,0:T(8,128)(2,1)S(1)} %copy-done.14, s32[3,128]{1,0:T(4,128)S(1)} %bitcast.16, s32[3,64]{1,0:T(4,128)S(1)} %bitcast.20, ...), custom_call_target="tpu_custom_call" | custom-call | flops 1000000000 | bytes 8388608 | tf_op jit(solution)/shard_map/pallas_call | solution.py:591
  31.0 0.5 collective-permute-done.2
  31.7 3.2 %shard_map.144.refs_1_ = f32[16,8192]{1,0:T(8,128)S(1)} custom-call(s32[5,256]{1,0:T(8,128)S(1)} %subtract_bitcast_fusion.leaves_ref, bf16[16,16384]{1,0:T(8,128)(2,1)S(1)} %copy-done.3, bf16[5,64,16384]{2,1,0:T(8,128)(2,1)S(1)} %bitcast.9), custom_call_target="tpu_custom_call" | custom-call | flops 1000000000 | bytes 8388608 | tf_op jit(solution)/shard_map/pallas_call | solution.py:580
  35.0 7.9 %shard_map.145 = (bf16[16,16384]{1,0:T(8,128)(2,1)}, bf16[16,16384]{1,0:T(8,128)(2,1)S(1)}) custom-call(s32[1]{0:T(128)} %bitcast.me_ref, s32[5,256]{1,0:T(8,128)S(1)} %subtract_bitcast_fusion.leaves_ref, bf16[8,192,128]{2,1,0:T(8,128)(2,1)S(1)} %pad_maximum_fusion.early_ref, bf16[8,192,128]{2,1,0:T(8,128)(2,1)S(1)} %collective-permute-done.3.late_ref, ...), custom_call_target="tpu_custom_call" | custom-call | flops 1000000000 | bytes 8388608 | tf_op jit(solution)/shard_map/pallas_call | solution.py:620
  42.8 4.4 %shard_map.146 = (bf16[192,128]{1,0:T(8,128)(2,1)S(1)}, bf16[16,32,128]{2,1,0:T(8,128)(2,1)S(1)}, bf16[8,32,128]{2,1,0:T(8,128)(2,1)S(1)}) custom-call(bf16[16,16384]{1,0:T(8,128)(2,1)S(1)} %get-tuple-element.97.z_ref, bf16[32,16384]{1,0:T(8,128)(2,1)S(1)} %copy-done.1, bf16[32,32,256]{2,1,0:T(8,128)(2,1)S(1)} %copy-done.4, ...), custom_call_target="tpu_custom_call" | custom-call | flops 100000000 | bytes 3145728 | tf_op jit(solution)/shard_map/pallas_call | solution.py:651
  47.2 0.4 collective-permute-start.4
  47.6 3.1 %shard_map.147.refs_0_ = f32[16,8192]{1,0:T(8,128)S(1)} custom-call(s32[5,256]{1,0:T(8,128)S(1)} %subtract_bitcast_fusion.leaves_ref, bf16[16,16384]{1,0:T(8,128)(2,1)S(1)} %get-tuple-element.97.z_ref, bf16[5,64,16384]{2,1,0:T(8,128)(2,1)S(1)} %bitcast.9), custom_call_target="tpu_custom_call" | custom-call | flops 1000000000 | bytes 8388608 | tf_op jit(solution)/shard_map/pallas_call | solution.py:580
  50.7 2.7 %collective-permute-done.4 = bf16[1,192,128]{2,1,0:T(8,128)(2,1)S(1)} collective-permute-done((bf16[1,192,128]{2,1,0:T(8,128)(2,1)S(1)}, bf16[1,192,128]{2,1,0:T(8,128)(2,1)S(1)}, u32[]{:S(2)}, u32[]{:S(2)}) %collective-permute-start.4) | collective-permute-done | bytes 49184 | tf_op jit(solution)/shard_map/ppermute | solution.py:605
  53.4 0.4 collective-permute-start.5
  53.8 3.3 %shard_map.148.refs_1_ = f32[16,8192]{1,0:T(8,128)S(1)} custom-call(s32[5,256]{1,0:T(8,128)S(1)} %subtract_bitcast_fusion.leaves_ref, bf16[16,16384]{1,0:T(8,128)(2,1)S(1)} %get-tuple-element.97.z_ref, bf16[5,64,16384]{2,1,0:T(8,128)(2,1)S(1)} %bitcast.9), custom_call_target="tpu_custom_call" | custom-call | flops 1000000000 | bytes 8388608 | tf_op jit(solution)/shard_map/pallas_call | solution.py:580
  57.0 1.0 %collective-permute-done.5 = bf16[2,192,128]{2,1,0:T(8,128)(2,1)S(1)} collective-permute-done((bf16[2,192,128]{2,1,0:T(8,128)(2,1)S(1)}, bf16[2,192,128]{2,1,0:T(8,128)(2,1)S(1)}, u32[]{:S(2)}, u32[]{:S(2)}) %collective-permute-start.5) | collective-permute-done | bytes 98336 | tf_op jit(solution)/shard_map/ppermute | solution.py:605
  58.1 1.6 %collective-permute-start.6 = (bf16[4,192,128]{2,1,0:T(8,128)(2,1)S(1)}, bf16[4,192,128]{2,1,0:T(8,128)(2,1)S(1)}, u32[]{:S(2)}, u32[]{:S(2)}) collective-permute-start(bf16[4,192,128]{2,1,0:T(8,128)(2,1)S(1)} %pad_maximum_fusion.3), channel_id=1, source_target_pairs={{0,2},{1,3},{2,0},{3,1},{4,6},{5,7},{6,4},{7,5},{8,10},{9,11},{10,... | collective-permute-start | bytes 589832 | tf_op jit(solution)/shard_map/ppermute | solution.py:605
  59.7 3.9 %shard_map.149 = (f32[16,32,128]{2,1,0:T(8,128)S(1)}, f32[8,32,128]{2,1,0:T(8,128)S(1)}) custom-call(s32[1]{0:T(128)} %bitcast.me_ref, bf16[16,32,128]{2,1,0:T(8,128)(2,1)S(1)} %get-tuple-element.101.coef1_ref, bf16[8,32,128]{2,1,0:T(8,128)(2,1)S(1)} %get-tuple-element.102.coef2_ref, s32[3,128]{1,0:T(4,128)S(1)} %bitcast.18, s32[3,64]{1,0:T(4,128)S(1)} %bitcast.22, ...), custom_call_target="tpu_custom_call" | custom-call | flops 1000000000 | bytes 8388608 | tf_op jit(solution)/shard_map/pallas_call | solution.py:591
  63.9 1.7 %collective-permute-done.7.late_ref = bf16[8,192,128]{2,1,0:T(8,128)(2,1)S(1)} collective-permute-done((bf16[8,192,128]{2,1,0:T(8,128)(2,1)S(1)}, bf16[8,192,128]{2,1,0:T(8,128)(2,1)S(1)}, u32[]{:S(2)}, u32[]{:S(2)}) %collective-permute-start.7) | collective-permute-done | bytes 393248 | tf_op jit(solution)/shard_map/ppermute | solution.py:605
  65.6 7.8 %shard_map.150 = bf16[16,16384]{1,0:T(8,128)(2,1)} custom-call(s32[1]{0:T(128)} %bitcast.me_ref, s32[5,256]{1,0:T(8,128)S(1)} %subtract_bitcast_fusion.leaves_ref, bf16[8,192,128]{2,1,0:T(8,128)(2,1)S(1)} %pad_maximum_fusion.1.early_ref, bf16[8,192,128]{2,1,0:T(8,128)(2,1)S(1)} %collective-permute-done.7.late_ref, ...), custom_call_target="tpu_custom_call" | custom-call | flops 1000000000 | bytes 8388608 | tf_op jit(solution)/shard_map/pallas_call | solution.py:620
  (49 shorter events, 0.8 us)
Async XLA Ops:
  0.6 21.8 %copy-start.5 = (bf16[8,32,32,32]{3,2,1,0:T(8,128)(2,1)S(1)}, bf16[8,32,32,32]{3,2,1,0:T(8,128)(2,1)}, u32[]{:S(2)}) copy-start(bf16[8,32,32,32]{3,2,1,0:T(8,128)(2,1)} %c3_ref.1) | copy-start | bytes 1572868
  0.6 21.8 %copy-start.8 = (bf16[3,32,32,128]{3,2,1,0:T(8,128)(2,1)S(1)}, bf16[3,32,32,128]{3,2,1,0:T(8,128)(2,1)}, u32[]{:S(2)}) copy-start(bf16[3,32,32,128]{3,2,1,0:T(8,128)(2,1)} %c1_ref.1) | copy-start | bytes 2359300
  0.7 26.4 %copy-start.12 = (s32[64,3]{0,1:T(4,128)S(1)}, s32[64,3]{0,1:T(4,128)}, u32[]{:S(2)}) copy-start(s32[64,3]{0,1:T(4,128)} %param.23) | copy-start | bytes 2308
  0.7 26.4 %copy-start.11 = (s32[128,3]{0,1:T(4,128)S(1)}, s32[128,3]{0,1:T(4,128)}, u32[]{:S(2)}) copy-start(s32[128,3]{0,1:T(4,128)} %param.22) | copy-start | bytes 4612
  7.8 12.9 %collective-permute-start = (bf16[1,192,128]{2,1,0:T(8,128)(2,1)}, bf16[1,192,128]{2,1,0:T(8,128)(2,1)S(1)}, u32[]{:S(2)}, u32[]{:S(2)}) collective-permute-start(bf16[1,192,128]{2,1,0:T(8,128)(2,1)} %bitcast.24), channel_id=1, source_target_pairs={{0,8},{1,9},{2,10},{3,11},{4,12},{5,13},{6,14},{7,15},{8,0},{9,1},... | collective-permute-start | bytes 147464 | tf_op jit(solution)/shard_map/ppermute | solution.py:605
  17.6 4.8 %copy-start.4 = (bf16[32,32,256]{2,1,0:T(8,128)(2,1)S(1)}, bf16[32,32,256]{2,1,0:T(8,128)(2,1)}, u32[]{:S(2)}) copy-start(bf16[32,32,256]{2,1,0:T(8,128)(2,1)} %get-tuple-element.63.up1_ref) | copy-start | bytes 1572868
  17.6 4.8 %copy-start.6 = (bf16[32,32,128]{2,1,0:T(8,128)(2,1)S(1)}, bf16[32,32,128]{2,1,0:T(8,128)(2,1)}, u32[]{:S(2)}) copy-start(bf16[32,32,128]{2,1,0:T(8,128)(2,1)} %get-tuple-element.64.up2_ref) | copy-start | bytes 786436
  17.6 4.8 %copy-start.7 = (bf16[32,32,128]{2,1,0:T(8,128)(2,1)S(1)}, bf16[32,32,128]{2,1,0:T(8,128)(2,1)}, u32[]{:S(2)}) copy-start(bf16[32,32,128]{2,1,0:T(8,128)(2,1)} %get-tuple-element.65.up3_ref) | copy-start | bytes 786436
  17.6 4.8 %copy-start.9 = (bf16[3,32,32,64]{3,2,1,0:T(8,128)(2,1)S(1)}, bf16[3,32,32,64]{3,2,1,0:T(8,128)(2,1)}, u32[]{:S(2)}) copy-start(bf16[3,32,32,64]{3,2,1,0:T(8,128)(2,1)} %c2_ref.1) | copy-start | bytes 1179652
  17.6 9.5 %copy-start.13 = (bf16[16,32,128]{2,1,0:T(8,128)(2,1)S(1)}, bf16[16,32,128]{2,1,0:T(8,128)(2,1)}, u32[]{:S(2)}) copy-start(bf16[16,32,128]{2,1,0:T(8,128)(2,1)} %get-tuple-element.76.coef1_ref) | copy-start | bytes 393220
  17.6 9.5 %copy-start.14 = (bf16[8,32,128]{2,1,0:T(8,128)(2,1)S(1)}, bf16[8,32,128]{2,1,0:T(8,128)(2,1)}, u32[]{:S(2)}) copy-start(bf16[8,32,128]{2,1,0:T(8,128)(2,1)} %get-tuple-element.77.coef2_ref) | copy-start | bytes 196612
  17.6 14.0 %slice-start = ((s8[10485760]{0:T(1024)(128)(4,1)}), s8[4194304]{0:T(1024)(128)(4,1)S(1)}, s32[]{:S(2)}) async-start(s8[10485760]{0:T(1024)(128)(4,1)} %bitcast.8), calls=%async_computation | async-start | bytes 8388608
  17.7 14.0 %slice-start.1 = ((s8[10485760]{0:T(1024)(128)(4,1)}), s8[4194304]{0:T(1024)(128)(4,1)S(1)}, s32[]{:S(2)}) async-start(s8[10485760]{0:T(1024)(128)(4,1)} %bitcast.8), calls=%async_computation.1 | async-start | bytes 8388608
  17.7 14.0 %copy-start.3 = (bf16[16,16384]{1,0:T(8,128)(2,1)S(1)}, bf16[16,16384]{1,0:T(8,128)(2,1)}, u32[]{:S(2)}) copy-start(bf16[16,16384]{1,0:T(8,128)(2,1)} %z_ref.5) | copy-start | bytes 1572868
  20.8 4.7 %collective-permute-start.1 = (bf16[2,192,128]{2,1,0:T(8,128)(2,1)S(1)}, bf16[2,192,128]{2,1,0:T(8,128)(2,1)S(1)}, u32[]{:S(2)}, u32[]{:S(2)}) collective-permute-start(bf16[2,192,128]{2,1,0:T(8,128)(2,1)S(1)} %pad_maximum_fusion.4), channel_id=1, source_target_pairs={{0,4},{1,5},{2,6},{3,7},{4,0},{5,1},{6,2},{7,3},{8,12},{9,13},{10,... | collective-permute-start | bytes 294920 | tf_op jit(solution)/shard_map/ppermute | solution.py:605
  22.5 9.2 %slice-start.2 = ((s8[10485760]{0:T(1024)(128)(4,1)}), s8[2097152]{0:T(1024)(128)(4,1)S(1)}, s32[]{:S(2)}) async-start(s8[10485760]{0:T(1024)(128)(4,1)} %bitcast.8), calls=%async_computation.2 | async-start | bytes 4194304
  22.5 12.5 %copy-start.1 = (bf16[32,16384]{1,0:T(8,128)(2,1)S(1)}, bf16[32,16384]{1,0:T(8,128)(2,1)}, u32[]{:S(2)}) copy-start(bf16[32,16384]{1,0:T(8,128)(2,1)} %refs_3_.3) | copy-start | bytes 3145732
  22.5 12.5 %copy-start.10 = (s32[32,8]{0,1:T(8,128)S(1)}, s32[32,8]{0,1:T(8,128)}, u32[]{:S(2)}) copy-start(s32[32,8]{0,1:T(8,128)} %param.25) | copy-start | bytes 3076
  25.5 6.0 %collective-permute-start.2 = (bf16[4,192,128]{2,1,0:T(8,128)(2,1)S(1)}, bf16[4,192,128]{2,1,0:T(8,128)(2,1)S(1)}, u32[]{:S(2)}, u32[]{:S(2)}) collective-permute-start(bf16[4,192,128]{2,1,0:T(8,128)(2,1)S(1)} %pad_maximum_fusion.2), channel_id=1, source_target_pairs={{0,2},{1,3},{2,0},{3,1},{4,6},{5,7},{6,4},{7,5},{8,10},{9,11},{10,... | collective-permute-start | bytes 589832 | tf_op jit(solution)/shard_map/ppermute | solution.py:605
  31.6 3.4 %collective-permute-start.3 = (bf16[8,192,128]{2,1,0:T(8,128)(2,1)S(1)}, bf16[8,192,128]{2,1,0:T(8,128)(2,1)S(1)}, u32[]{:S(2)}, u32[]{:S(2)}) collective-permute-start(bf16[8,192,128]{2,1,0:T(8,128)(2,1)S(1)} %pad_maximum_fusion.early_ref), channel_id=1, source_target_pairs={{0,1},{1,0},{2,3},{3,2},{4,5},{5,4},{6,7},{7,6},{8,9},{9,8},{10,11... | collective-permute-start | bytes 1179656 | tf_op jit(solution)/shard_map/ppermute | solution.py:605
  47.2 6.1 %collective-permute-start.4 = (bf16[1,192,128]{2,1,0:T(8,128)(2,1)S(1)}, bf16[1,192,128]{2,1,0:T(8,128)(2,1)S(1)}, u32[]{:S(2)}, u32[]{:S(2)}) collective-permute-start(bf16[1,192,128]{2,1,0:T(8,128)(2,1)S(1)} %bitcast.10), channel_id=1, source_target_pairs={{0,8},{1,9},{2,10},{3,11},{4,12},{5,13},{6,14},{7,15},{8,0},{9,1},... | collective-permute-start | bytes 147464 | tf_op jit(solution)/shard_map/ppermute | solution.py:605
  53.4 4.7 %collective-permute-start.5 = (bf16[2,192,128]{2,1,0:T(8,128)(2,1)S(1)}, bf16[2,192,128]{2,1,0:T(8,128)(2,1)S(1)}, u32[]{:S(2)}, u32[]{:S(2)}) collective-permute-start(bf16[2,192,128]{2,1,0:T(8,128)(2,1)S(1)} %pad_maximum_fusion.5), channel_id=1, source_target_pairs={{0,4},{1,5},{2,6},{3,7},{4,0},{5,1},{6,2},{7,3},{8,12},{9,13},{10,... | collective-permute-start | bytes 294920 | tf_op jit(solution)/shard_map/ppermute | solution.py:605
  58.1 5.7 %collective-permute-start.6 = (bf16[4,192,128]{2,1,0:T(8,128)(2,1)S(1)}, bf16[4,192,128]{2,1,0:T(8,128)(2,1)S(1)}, u32[]{:S(2)}, u32[]{:S(2)}) collective-permute-start(bf16[4,192,128]{2,1,0:T(8,128)(2,1)S(1)} %pad_maximum_fusion.3), channel_id=1, source_target_pairs={{0,2},{1,3},{2,0},{3,1},{4,6},{5,7},{6,4},{7,5},{8,10},{9,11},{10,... | collective-permute-start | bytes 589832 | tf_op jit(solution)/shard_map/ppermute | solution.py:605
  63.9 1.8 %collective-permute-start.7 = (bf16[8,192,128]{2,1,0:T(8,128)(2,1)S(1)}, bf16[8,192,128]{2,1,0:T(8,128)(2,1)S(1)}, u32[]{:S(2)}, u32[]{:S(2)}) collective-permute-start(bf16[8,192,128]{2,1,0:T(8,128)(2,1)S(1)} %pad_maximum_fusion.1.early_ref), channel_id=1, source_target_pairs={{0,1},{1,0},{2,3},{3,2},{4,5},{5,4},{6,7},{7,6},{8,9},{9,8},{10,11... | collective-permute-start | bytes 1179656 | tf_op jit(solution)/shard_map/ppermute | solution.py:605
  (3 other events, 8.2 us)

commit v3 on v2

--- a/solution.py
+++ b/solution.py
@@ -208,10 +208,20 @@
 
 
 def first_kernel(
-    z_ref, basis_ref, first_ref, second_ref, third_ref,
-    sent_ref, coef1_ref, coef2_ref, up1_ref, up2_ref, up3_ref, *scratch
+    z_hbm, basis_hbm, first_hbm, second_hbm, third_hbm,
+    sent_ref, coef1_ref, coef2_ref, up1_ref, up2_ref, up3_ref,
+    z_ref, basis_ref, first_ref, second_ref, third_ref, sems, *scratch
 ):
+    sources = (first_hbm, second_hbm, third_hbm, z_hbm, basis_hbm)
+    targets = (first_ref, second_ref, third_ref, z_ref, basis_ref)
+    copies = [pltpu.make_async_copy(a, b, sems.at[i]) for i, (a, b) in enumerate(zip(sources, targets))]
+    for copy in copies:
+        copy.start()
+    for copy in copies[:3]:
+        copy.wait()
     prep_up_kernel(first_ref, second_ref, third_ref, up1_ref, up2_ref, up3_ref)
+    for copy in copies[3:]:
+        copy.wait()
     up_kernel(z_ref, basis_ref, up1_ref, up2_ref, up3_ref, sent_ref, coef1_ref, coef2_ref, *scratch)
 
 
@@ -280,9 +290,25 @@
     return in_order(jnp.where(inside, place(jnp.clip(local, 0, count - 1), count, levels), -1), count, levels)
 
 
-def couple_kernel(me_ref, coef1_ref, coef2_ref, list1_ref, list2_ref, m1_ref, m2_ref, far1_ref, far2_ref, picks_ref):
+def couple_kernel(
+    bits, me_ref, coef1_ref, coef2_ref, list1_ref, list2_ref, top_ref, m1_ref, m2_ref, far1_ref, far2_ref, table_ref, picks_ref
+):
     rhs, half = coef1_ref.shape[0], coef2_ref.shape[0]
     me = me_ref[0]
+    devices, top = 1 << bits, top_ref.shape[1]
+    per = LANES // top
+    nodes = top_ref[...]
+    rows = bit_reverse(jnp.bitwise_xor(nodes // top, me), bits) * top + nodes % top
+    hot = []
+    for j in range(NFAR):
+        hot.append(jnp.where(iota((devices * top, top), 0) == rows[j : j + 1], 1.0, 0.0).astype(BF16))
+    for h in range(NFAR // per):
+        wide = None
+        for q in range(per):
+            put = jnp.where(iota((top, LANES), 0) + q * top == iota((top, LANES), 1), 1.0, 0.0).astype(BF16)
+            part = dot(hot[h * per + q], put)
+            wide = part if wide is None else wide + part
+        table_ref[h] = wide.astype(BF16)
     zeros = tuple(jnp.zeros((K, LANES), F32) for _ in range(half))
 
     def run(matrix_ref, first):
@@ -329,7 +355,7 @@
 
 def down_kernel(bits, me_ref, leaves_ref, early_ref, late_ref, far1_in_ref, far2_in_ref, z_ref, *refs):
     near_refs = refs[:PIECES]
-    (blocks_ref, basis_ref, list1_ref, list2_ref, top_ref, ends_ref, m3_ref, d1_ref, d2_ref, d3_ref,
+    (blocks_ref, basis_ref, list1_ref, list2_ref, table_ref, ends_ref, m3_ref, d1_ref, d2_ref, d3_ref,
      out_hbm, out_ref, every_ref, picks_ref, far1_ref, x_ref, x0_ref, rows_ref, z_leaves_ref, sems) = refs[PIECES:]
     rhs, order = z_ref.shape
     leaves = order // M
@@ -407,18 +433,8 @@
                 moved = pltpu.roll(parts[q], shift, 1) if shift else parts[q]
                 merged = moved if merged is None else jnp.where(group == q, moved, merged)
             every_ref[g * own_rows : (g + 1) * own_rows, tile * LANES : (tile + 1) * LANES] = merged.astype(BF16)
-    nodes = top_ref[...]
-    rows = bit_reverse(jnp.bitwise_xor(nodes // top, me), bits) * top + nodes % top
-    hot = []
-    for j in range(NFAR):
-        hot.append(jnp.where(iota((devices * top, top), 0) == rows[j : j + 1], 1.0, 0.0).astype(BF16))
     for h in range(NFAR // per):
-        wide = None
-        for q in range(per):
-            put = jnp.where(iota((top, LANES), 0) + q * top == iota((top, LANES), 1), 1.0, 0.0).astype(BF16)
-            part = dot(hot[h * per + q], put)
-            wide = part if wide is None else wide + part
-        picked = dot(every_ref[...], wide.astype(BF16))
+        picked = dot(every_ref[...], table_ref[h])
         picks_ref[:, h * K : (h + 1) * K, :] = picked.reshape(rhs, K, LANES)
     zeros = tuple(jnp.zeros((K, LANES), F32) for _ in range(half))
     groups_of = [1, 0, 3, 2]
@@ -513,10 +529,6 @@
     return pltpu.CompilerParams(vmem_limit_bytes=mib * 2**20)
 
 
-def whole(array):
-    return pl.BlockSpec(array.shape, lambda i: (0,) * len(array.shape), pipeline_mode=pl.Buffered(1))
-
-
 def cost(flops, moved):
     return pl.CostEstimate(flops=flops, bytes_accessed=moved, transcendentals=0)
 
@@ -551,10 +563,14 @@
         first_kernel,
         out_shape=up_shapes
         + (shape((K, K, leaves)), shape((K, K, LANES)), shape((K, K, LANES))),
-        grid=(1,),
-        in_specs=[whole(a) for a in (right_sides, leaf_basis, transfer_first, transfer_second, transfer_third)],
+        in_specs=[HBM] * 5,
         out_specs=(VM,) * 6,
-        scratch_shapes=up_scratch,
+        scratch_shapes=[
+            pltpu.VMEM(a.shape, BF16)
+            for a in (right_sides, leaf_basis, transfer_first, transfer_second, transfer_third)
+        ]
+        + [pltpu.SemaphoreType.DMA((5,))]
+        + up_scratch,
         compiler_params=params(56),
         cost_estimate=cost(FIRST * 10**9, 3 * 2**20),
     )(right_sides, leaf_basis, transfer_first, transfer_second, transfer_third)
@@ -589,14 +605,17 @@
 
     def couple(coef1, coef2, m1, m2):
         return pl.pallas_call(
-            couple_kernel,
-            out_shape=(shape((rhs, K, LANES), F32), shape((half, K, LANES), F32)),
-            in_specs=[SM] + [VM] * 6,
-            out_specs=(VM,) * 2,
+            functools.partial(couple_kernel, bits),
+            out_shape=(
+                shape((rhs, K, LANES), F32), shape((half, K, LANES), F32),
+                shape((NFAR * (leaves // 8) // LANES, devices * (leaves // 8), LANES)),
+            ),
+            in_specs=[SM] + [VM] * 7,
+            out_specs=(VM,) * 3,
             scratch_shapes=[pltpu.VMEM((rhs, NC * K, LANES), F32)],
             compiler_params=params(16),
             cost_estimate=cost(10**9, 8 * 2**20),
-        )(me, coef1, coef2, lists[0], lists[1], m1, m2)
+        )(me, coef1, coef2, *lists, m1, m2)
 
     def exchange(sent, works):
         every, done = sent[None], []
@@ -614,7 +633,7 @@
     def held(values, every):
         return lax.optimization_barrier((*values, every))[:-1]
 
-    def down(every, other, far1, far2, vectors, nears, prepared, keep):
+    def down(every, other, far1, far2, table, vectors, nears, prepared, keep):
         d1, d2, d3, _, _, m3, ends = prepared
         out = shape((rhs, order))
         results = pl.pallas_call(
@@ -635,7 +654,7 @@
             ],
             compiler_params=params(24),
             cost_estimate=cost(10**9, 8 * 2**20),
-        )(me, near_local, every, other, far1, far2, vectors, *nears, blocks, basis, *lists, ends, m3, d1, d2, d3)
+        )(me, near_local, every, other, far1, far2, vectors, *nears, blocks, basis, *lists[:2], table, ends, m3, d1, d2, d3)
         return results
 
     sent, coef1, coef2 = upward
@@ -658,11 +677,11 @@
         cost_estimate=cost(10**8, 3 * 2**20),
     )(second_vectors, basis, up1, up2, up3)
     works = [
+        lambda every: couple(*held((coef1, coef2), every), *prepared[3:5]),
         lambda every: near_piece(0, *held((second_vectors,), every)),
         lambda every: near_piece(1, *held((second_vectors,), every)),
-        lambda every: couple(*held((coef1, coef2), every), *prepared[3:5]),
     ]
-    every, other, (near0, near1, fars) = exchange(sent, works)
+    every, other, (fars, near0, near1) = exchange(sent, works)
     (second_image,) = down(every, other, *fars, second_vectors, (near0, near1), prepared, False)
     return (first_image, second_image)
 

time: 73.9 us -> 72.7 us (0.984)
  Pallas kernels: 50.5 us -> 49.6 us
    pallas_call x2, Pallas kernels: 15.7 us -> 14.7 us  [down(): pl.pallas_call(functools.partial(down_kernel, bits), out_shape=(out, out)...]
  transfers between devices with their start and end apart: 8 -> 8, of which waited for: 6 -> 6; matrix products, arithmetic and copies ran while one was open for 1% -> 1% of each run, Pallas kernels for 32% -> 33%
where the time goes in v3:
time: 72.7 us; the launch traced here: 72.5 us
  Pallas kernels  49.6 us (68%)
  starting transfers between devices  9.88 us (14%)
  waiting for transfers between devices  5.93 us (8%)
  local copies, waits for them, and re-layouts  5.12 us (7%)
  between operations  1.15 us (2%)
  other arithmetic  0.85 us (1%)
    pallas_call x2, Pallas kernels, down(): pl.pallas_call(functools.partial(down_kernel, bits), out_shape=(out, out)...  14.7 us
    pallas_call x4, Pallas kernels, near_piece(): pl.pallas_call(functools.partial(near_kernel, i * cut // CHUNK), out_shap...  12.4 us
    ppermute x8, starting transfers between devices, exchange(): other = lax.ppermute(every, AXES, pairs)  9.88 us
    pallas_call x2, Pallas kernels, couple(): pl.pallas_call(functools.partial(couple_kernel, bits), out_shape=(shape((...  8.32 us
    pallas_call x1, Pallas kernels, body(): pl.pallas_call(first_kernel, out_shape=up_shapes + (shape((K, K, leaves))...  6.87 us
    ppermute x8, waiting for transfers between devices, exchange(): other = lax.ppermute(every, AXES, pairs)  5.93 us
    unnamed x38, local copies, waits for them, and re-layouts  5.12 us
    pallas_call x1, Pallas kernels, body(): pl.pallas_call(up_kernel, out_shape=up_shapes, in_specs=[VM] * 5, out_spe...  4.37 us
  transfers between devices with their start and end apart: 8, of which 6 were waited for; matrix products, arithmetic and copies ran while one was open for 1% of the time, Pallas kernels for 33%

profile of v3, /device:TPU:0, one launch (start us, length us, event | category | flops | bytes accessed | tf_op | source)
XLA Modules:
  0.0 72.5 jit_solution(2410629277317380845)
XLA Ops:
  0.7 6.9 %shard_map.140 = (bf16[192,128]{1,0:T(8,128)(2,1)}, bf16[16,32,128]{2,1,0:T(8,128)(2,1)}, bf16[8,32,128]{2,1,0:T(8,128)(2,1)}, bf16[32,32,256]{2,1,0:T(8,128)(2,...) custom-call(bf16[16,16384]{1,0:T(8,128)(2,1)} %z_ref.3, bf16[32,16384]{1,0:T(8,128)(2,1)} %refs_3_.3, ...), custom_call_target="tpu_custom_call" | custom-call | flops 1000000000 | bytes 3145728 | tf_op jit(solution)/shard_map/pallas_call | solution.py:562
  7.6 4.1 %collective-permute-start = (bf16[1,192,128]{2,1,0:T(8,128)(2,1)}, bf16[1,192,128]{2,1,0:T(8,128)(2,1)S(1)}, u32[]{:S(2)}, u32[]{:S(2)}) collective-permute-start(bf16[1,192,128]{2,1,0:T(8,128)(2,1)} %bitcast.24), channel_id=1, source_target_pairs={{0,8},{1,9},{2,10},{3,11},{4,12},{5,13},{6,14},{7,15},{8,0},{9,1},... | collective-permute-start | bytes 147464 | tf_op jit(solution)/shard_map/ppermute | solution.py:624
  11.7 0.7 subtract_bitcast_fusion.leaves_ref
  12.4 4.0 %copy-done = bf16[5,64,16384]{2,1,0:T(8,128)(2,1)S(1)} copy-done((bf16[5,64,16384]{2,1,0:T(8,128)(2,1)S(1)}, bf16[5,64,16384]{2,1,0:T(8,128)(2,1)}, u32[]{:S(2)}) %copy-start) | copy-done | bytes 10485784
  16.4 1.0 %copy-done.2 = bf16[16,16384]{1,0:T(8,128)(2,1)S(1)} copy-done((bf16[16,16384]{1,0:T(8,128)(2,1)S(1)}, bf16[16,16384]{1,0:T(8,128)(2,1)}, u32[]{:S(2)}) %copy-start.2) | copy-done | bytes 524312
  17.5 3.1 %shard_map.141.refs_0_ = f32[16,8192]{1,0:T(8,128)S(1)} custom-call(s32[5,256]{1,0:T(8,128)S(1)} %subtract_bitcast_fusion.leaves_ref, bf16[16,16384]{1,0:T(8,128)(2,1)S(1)} %copy-done.2, bf16[5,64,16384]{2,1,0:T(8,128)(2,1)S(1)} %copy-done), custom_call_target="tpu_custom_call" | custom-call | flops 1000000000 | bytes 8388608 | tf_op jit(solution)/shard_map/pallas_call | solution.py:596
  20.6 1.6 %collective-permute-start.1 = (bf16[2,192,128]{2,1,0:T(8,128)(2,1)S(1)}, bf16[2,192,128]{2,1,0:T(8,128)(2,1)S(1)}, u32[]{:S(2)}, u32[]{:S(2)}) collective-permute-start(bf16[2,192,128]{2,1,0:T(8,128)(2,1)S(1)} %pad_maximum_fusion.4), channel_id=1, source_target_pairs={{0,4},{1,5},{2,6},{3,7},{4,0},{5,1},{6,2},{7,3},{8,12},{9,13},{10,... | collective-permute-start | bytes 294920 | tf_op jit(solution)/shard_map/ppermute | solution.py:624
  22.3 2.8 %shard_map.142 = (bf16[32,32,256]{2,1,0:T(8,128)(2,1)S(1)}, bf16[32,32,128]{2,1,0:T(8,128)(2,1)S(1)}, bf16[32,32,128]{2,1,0:T(8,128)(2,1)S(1)}, bf16[3,32,32,128...) custom-call(bf16[32,32,256]{2,1,0:T(8,128)(2,1)S(1)} %copy-done.4, ...), custom_call_target="tpu_custom_call" | custom-call | flops 1000000000 | bytes 9437184 | tf_op jit(solution)/shard_map/pallas_call | solution.py:581
  25.3 1.6 %collective-permute-start.2 = (bf16[4,192,128]{2,1,0:T(8,128)(2,1)S(1)}, bf16[4,192,128]{2,1,0:T(8,128)(2,1)S(1)}, u32[]{:S(2)}, u32[]{:S(2)}) collective-permute-start(bf16[4,192,128]{2,1,0:T(8,128)(2,1)S(1)} %pad_maximum_fusion.2), channel_id=1, source_target_pairs={{0,2},{1,3},{2,0},{3,1},{4,6},{5,7},{6,4},{7,5},{8,10},{9,11},{10,... | collective-permute-start | bytes 589832 | tf_op jit(solution)/shard_map/ppermute | solution.py:624
  26.9 4.1 %shard_map.143 = (f32[16,32,128]{2,1,0:T(8,128)S(1)}, f32[8,32,128]{2,1,0:T(8,128)S(1)}, bf16[2,512,128]{2,1,0:T(8,128)(2,1)S(1)}) custom-call(s32[1]{0:T(128)} %bitcast.me_ref, bf16[16,32,128]{2,1,0:T(8,128)(2,1)S(1)} %copy-done.13, bf16[8,32,128]{2,1,0:T(8,128)(2,1)S(1)} %copy-done.14, s32[3,128]{1,0:T(4,128)S(1)} %bitcast.14, s32[3,64]{1,0:T(4,128)S(1)} %bitcast.18, ...), custom_call_target="tpu_custom_call" | custom-call | flops 1000000000 | bytes 8388608 | tf_op jit(solution)/shard_map/pallas_call | solution.py:607
  31.5 3.2 %shard_map.144.refs_1_ = f32[16,8192]{1,0:T(8,128)S(1)} custom-call(s32[5,256]{1,0:T(8,128)S(1)} %subtract_bitcast_fusion.leaves_ref, bf16[16,16384]{1,0:T(8,128)(2,1)S(1)} %copy-done.3, bf16[5,64,16384]{2,1,0:T(8,128)(2,1)S(1)} %bitcast.9), custom_call_target="tpu_custom_call" | custom-call | flops 1000000000 | bytes 8388608 | tf_op jit(solution)/shard_map/pallas_call | solution.py:596
  34.8 7.4 %shard_map.145 = (bf16[16,16384]{1,0:T(8,128)(2,1)}, bf16[16,16384]{1,0:T(8,128)(2,1)S(1)}) custom-call(s32[1]{0:T(128)} %bitcast.me_ref, s32[5,256]{1,0:T(8,128)S(1)} %subtract_bitcast_fusion.leaves_ref, bf16[8,192,128]{2,1,0:T(8,128)(2,1)S(1)} %pad_maximum_fusion.early_ref, bf16[8,192,128]{2,1,0:T(8,128)(2,1)S(1)} %collective-permute-done.3.late_ref, ...), custom_call_target="tpu_custom_call" | custom-call | flops 1000000000 | bytes 8388608 | tf_op jit(solution)/shard_map/pallas_call | solution.py:639
  42.1 4.4 %shard_map.146 = (bf16[192,128]{1,0:T(8,128)(2,1)S(1)}, bf16[16,32,128]{2,1,0:T(8,128)(2,1)S(1)}, bf16[8,32,128]{2,1,0:T(8,128)(2,1)S(1)}) custom-call(bf16[16,16384]{1,0:T(8,128)(2,1)S(1)} %get-tuple-element.113.z_ref, bf16[32,16384]{1,0:T(8,128)(2,1)S(1)} %copy-done.1, bf16[32,32,256]{2,1,0:T(8,128)(2,1)S(1)} %copy-done.4, ...), custom_call_target="tpu_custom_call" | custom-call | flops 100000000 | bytes 3145728 | tf_op jit(solution)/shard_map/pallas_call | solution.py:670
  46.5 0.4 collective-permute-start.4
  46.9 4.3 %shard_map.147 = (f32[16,32,128]{2,1,0:T(8,128)S(1)}, f32[8,32,128]{2,1,0:T(8,128)S(1)}, bf16[2,512,128]{2,1,0:T(8,128)(2,1)S(1)}) custom-call(s32[1]{0:T(128)} %bitcast.me_ref, bf16[16,32,128]{2,1,0:T(8,128)(2,1)S(1)} %get-tuple-element.103.coef1_ref, bf16[8,32,128]{2,1,0:T(8,128)(2,1)S(1)} %get-tuple-element.104.coef2_ref, s32[3,128]{1,0:T(4,128)S(1)} %bitcast.16, ...), custom_call_target="tpu_custom_call" | custom-call | flops 1000000000 | bytes 8388608 | tf_op jit(solution)/shard_map/pallas_call | solution.py:607
  51.2 1.5 %collective-permute-done.4 = bf16[1,192,128]{2,1,0:T(8,128)(2,1)S(1)} collective-permute-done((bf16[1,192,128]{2,1,0:T(8,128)(2,1)S(1)}, bf16[1,192,128]{2,1,0:T(8,128)(2,1)S(1)}, u32[]{:S(2)}, u32[]{:S(2)}) %collective-permute-start.4) | collective-permute-done | bytes 49184 | tf_op jit(solution)/shard_map/ppermute | solution.py:624
  52.7 0.4 collective-permute-start.5
  53.1 3.1 %shard_map.148.refs_0_ = f32[16,8192]{1,0:T(8,128)S(1)} custom-call(s32[5,256]{1,0:T(8,128)S(1)} %subtract_bitcast_fusion.leaves_ref, bf16[16,16384]{1,0:T(8,128)(2,1)S(1)} %get-tuple-element.113.z_ref, bf16[5,64,16384]{2,1,0:T(8,128)(2,1)S(1)} %bitcast.9), custom_call_target="tpu_custom_call" | custom-call | flops 1000000000 | bytes 8388608 | tf_op jit(solution)/shard_map/pallas_call | solution.py:596
  56.2 1.2 %collective-permute-done.5 = bf16[2,192,128]{2,1,0:T(8,128)(2,1)S(1)} collective-permute-done((bf16[2,192,128]{2,1,0:T(8,128)(2,1)S(1)}, bf16[2,192,128]{2,1,0:T(8,128)(2,1)S(1)}, u32[]{:S(2)}, u32[]{:S(2)}) %collective-permute-start.5) | collective-permute-done | bytes 98336 | tf_op jit(solution)/shard_map/ppermute | solution.py:624
  57.4 1.6 %collective-permute-start.6 = (bf16[4,192,128]{2,1,0:T(8,128)(2,1)S(1)}, bf16[4,192,128]{2,1,0:T(8,128)(2,1)S(1)}, u32[]{:S(2)}, u32[]{:S(2)}) collective-permute-start(bf16[4,192,128]{2,1,0:T(8,128)(2,1)S(1)} %pad_maximum_fusion.3), channel_id=1, source_target_pairs={{0,2},{1,3},{2,0},{3,1},{4,6},{5,7},{6,4},{7,5},{8,10},{9,11},{10,... | collective-permute-start | bytes 589832 | tf_op jit(solution)/shard_map/ppermute | solution.py:624
  59.0 3.1 %shard_map.149.refs_1_ = f32[16,8192]{1,0:T(8,128)S(1)} custom-call(s32[5,256]{1,0:T(8,128)S(1)} %subtract_bitcast_fusion.leaves_ref, bf16[16,16384]{1,0:T(8,128)(2,1)S(1)} %get-tuple-element.113.z_ref, bf16[5,64,16384]{2,1,0:T(8,128)(2,1)S(1)} %bitcast.9), custom_call_target="tpu_custom_call" | custom-call | flops 1000000000 | bytes 8388608 | tf_op jit(solution)/shard_map/pallas_call | solution.py:596
  62.0 1.1 %collective-permute-done.6 = bf16[4,192,128]{2,1,0:T(8,128)(2,1)S(1)} collective-permute-done((bf16[4,192,128]{2,1,0:T(8,128)(2,1)S(1)}, bf16[4,192,128]{2,1,0:T(8,128)(2,1)S(1)}, u32[]{:S(2)}, u32[]{:S(2)}) %collective-permute-start.6) | collective-permute-done | bytes 196640 | tf_op jit(solution)/shard_map/ppermute | solution.py:624
  63.2 1.7 %collective-permute-done.7.late_ref = bf16[8,192,128]{2,1,0:T(8,128)(2,1)S(1)} collective-permute-done((bf16[8,192,128]{2,1,0:T(8,128)(2,1)S(1)}, bf16[8,192,128]{2,1,0:T(8,128)(2,1)S(1)}, u32[]{:S(2)}, u32[]{:S(2)}) %collective-permute-start.7) | collective-permute-done | bytes 393248 | tf_op jit(solution)/shard_map/ppermute | solution.py:624
  65.0 7.4 %shard_map.150 = bf16[16,16384]{1,0:T(8,128)(2,1)} custom-call(s32[1]{0:T(128)} %bitcast.me_ref, s32[5,256]{1,0:T(8,128)S(1)} %subtract_bitcast_fusion.leaves_ref, bf16[8,192,128]{2,1,0:T(8,128)(2,1)S(1)} %pad_maximum_fusion.1.early_ref, bf16[8,192,128]{2,1,0:T(8,128)(2,1)S(1)} %collective-permute-done.7.late_ref, ...), custom_call_target="tpu_custom_call" | custom-call | flops 1000000000 | bytes 8388608 | tf_op jit(solution)/shard_map/pallas_call | solution.py:639
  (49 shorter events, 0.9 us)
Async XLA Ops:
  0.6 21.6 %copy-start.5 = (bf16[8,32,32,32]{3,2,1,0:T(8,128)(2,1)S(1)}, bf16[8,32,32,32]{3,2,1,0:T(8,128)(2,1)}, u32[]{:S(2)}) copy-start(bf16[8,32,32,32]{3,2,1,0:T(8,128)(2,1)} %c3_ref.1) | copy-start | bytes 1572868
  0.6 21.6 %copy-start.8 = (bf16[3,32,32,128]{3,2,1,0:T(8,128)(2,1)S(1)}, bf16[3,32,32,128]{3,2,1,0:T(8,128)(2,1)}, u32[]{:S(2)}) copy-start(bf16[3,32,32,128]{3,2,1,0:T(8,128)(2,1)} %c1_ref.1) | copy-start | bytes 2359300
  0.7 26.2 %copy-start.12 = (s32[32,8]{0,1:T(8,128)S(1)}, s32[32,8]{0,1:T(8,128)}, u32[]{:S(2)}) copy-start(s32[32,8]{0,1:T(8,128)} %param.25) | copy-start | bytes 3076
  0.7 26.2 %copy-start.11 = (s32[64,3]{0,1:T(4,128)S(1)}, s32[64,3]{0,1:T(4,128)}, u32[]{:S(2)}) copy-start(s32[64,3]{0,1:T(4,128)} %param.23) | copy-start | bytes 2308
  0.7 26.2 %copy-start.10 = (s32[128,3]{0,1:T(4,128)S(1)}, s32[128,3]{0,1:T(4,128)}, u32[]{:S(2)}) copy-start(s32[128,3]{0,1:T(4,128)} %param.22) | copy-start | bytes 4612
  7.6 13.0 %collective-permute-start = (bf16[1,192,128]{2,1,0:T(8,128)(2,1)}, bf16[1,192,128]{2,1,0:T(8,128)(2,1)S(1)}, u32[]{:S(2)}, u32[]{:S(2)}) collective-permute-start(bf16[1,192,128]{2,1,0:T(8,128)(2,1)} %bitcast.24), channel_id=1, source_target_pairs={{0,8},{1,9},{2,10},{3,11},{4,12},{5,13},{6,14},{7,15},{8,0},{9,1},... | collective-permute-start | bytes 147464 | tf_op jit(solution)/shard_map/ppermute | solution.py:624
  17.4 4.8 %copy-start.4 = (bf16[32,32,256]{2,1,0:T(8,128)(2,1)S(1)}, bf16[32,32,256]{2,1,0:T(8,128)(2,1)}, u32[]{:S(2)}) copy-start(bf16[32,32,256]{2,1,0:T(8,128)(2,1)} %get-tuple-element.67.up1_ref) | copy-start | bytes 1572868
  17.4 4.8 %copy-start.6 = (bf16[32,32,128]{2,1,0:T(8,128)(2,1)S(1)}, bf16[32,32,128]{2,1,0:T(8,128)(2,1)}, u32[]{:S(2)}) copy-start(bf16[32,32,128]{2,1,0:T(8,128)(2,1)} %get-tuple-element.68.up2_ref) | copy-start | bytes 786436
  17.4 4.8 %copy-start.7 = (bf16[32,32,128]{2,1,0:T(8,128)(2,1)S(1)}, bf16[32,32,128]{2,1,0:T(8,128)(2,1)}, u32[]{:S(2)}) copy-start(bf16[32,32,128]{2,1,0:T(8,128)(2,1)} %get-tuple-element.69.up3_ref) | copy-start | bytes 786436
  17.4 4.9 %copy-start.9 = (bf16[3,32,32,64]{3,2,1,0:T(8,128)(2,1)S(1)}, bf16[3,32,32,64]{3,2,1,0:T(8,128)(2,1)}, u32[]{:S(2)}) copy-start(bf16[3,32,32,64]{3,2,1,0:T(8,128)(2,1)} %c2_ref.1) | copy-start | bytes 1179652
  17.4 9.5 %copy-start.13 = (bf16[16,32,128]{2,1,0:T(8,128)(2,1)S(1)}, bf16[16,32,128]{2,1,0:T(8,128)(2,1)}, u32[]{:S(2)}) copy-start(bf16[16,32,128]{2,1,0:T(8,128)(2,1)} %get-tuple-element.80.coef1_ref) | copy-start | bytes 393220
  17.4 9.5 %copy-start.14 = (bf16[8,32,128]{2,1,0:T(8,128)(2,1)S(1)}, bf16[8,32,128]{2,1,0:T(8,128)(2,1)}, u32[]{:S(2)}) copy-start(bf16[8,32,128]{2,1,0:T(8,128)(2,1)} %get-tuple-element.81.coef2_ref) | copy-start | bytes 196612
  17.4 14.0 %slice-start = ((s8[10485760]{0:T(1024)(128)(4,1)}), s8[4194304]{0:T(1024)(128)(4,1)S(1)}, s32[]{:S(2)}) async-start(s8[10485760]{0:T(1024)(128)(4,1)} %bitcast.8), calls=%async_computation | async-start | bytes 8388608
  17.5 14.0 %slice-start.1 = ((s8[10485760]{0:T(1024)(128)(4,1)}), s8[4194304]{0:T(1024)(128)(4,1)S(1)}, s32[]{:S(2)}) async-start(s8[10485760]{0:T(1024)(128)(4,1)} %bitcast.8), calls=%async_computation.1 | async-start | bytes 8388608
  17.5 14.0 %copy-start.3 = (bf16[16,16384]{1,0:T(8,128)(2,1)S(1)}, bf16[16,16384]{1,0:T(8,128)(2,1)}, u32[]{:S(2)}) copy-start(bf16[16,16384]{1,0:T(8,128)(2,1)} %z_ref.3) | copy-start | bytes 1572868
  20.6 4.7 %collective-permute-start.1 = (bf16[2,192,128]{2,1,0:T(8,128)(2,1)S(1)}, bf16[2,192,128]{2,1,0:T(8,128)(2,1)S(1)}, u32[]{:S(2)}, u32[]{:S(2)}) collective-permute-start(bf16[2,192,128]{2,1,0:T(8,128)(2,1)S(1)} %pad_maximum_fusion.4), channel_id=1, source_target_pairs={{0,4},{1,5},{2,6},{3,7},{4,0},{5,1},{6,2},{7,3},{8,12},{9,13},{10,... | collective-permute-start | bytes 294920 | tf_op jit(solution)/shard_map/ppermute | solution.py:624
  22.3 9.2 %slice-start.2 = ((s8[10485760]{0:T(1024)(128)(4,1)}), s8[2097152]{0:T(1024)(128)(4,1)S(1)}, s32[]{:S(2)}) async-start(s8[10485760]{0:T(1024)(128)(4,1)} %bitcast.8), calls=%async_computation.2 | async-start | bytes 4194304
  22.3 12.5 %copy-start.1 = (bf16[32,16384]{1,0:T(8,128)(2,1)S(1)}, bf16[32,16384]{1,0:T(8,128)(2,1)}, u32[]{:S(2)}) copy-start(bf16[32,16384]{1,0:T(8,128)(2,1)} %refs_3_.3) | copy-start | bytes 3145732
  25.3 6.0 %collective-permute-start.2 = (bf16[4,192,128]{2,1,0:T(8,128)(2,1)S(1)}, bf16[4,192,128]{2,1,0:T(8,128)(2,1)S(1)}, u32[]{:S(2)}, u32[]{:S(2)}) collective-permute-start(bf16[4,192,128]{2,1,0:T(8,128)(2,1)S(1)} %pad_maximum_fusion.2), channel_id=1, source_target_pairs={{0,2},{1,3},{2,0},{3,1},{4,6},{5,7},{6,4},{7,5},{8,10},{9,11},{10,... | collective-permute-start | bytes 589832 | tf_op jit(solution)/shard_map/ppermute | solution.py:624
  31.4 3.4 %collective-permute-start.3 = (bf16[8,192,128]{2,1,0:T(8,128)(2,1)S(1)}, bf16[8,192,128]{2,1,0:T(8,128)(2,1)S(1)}, u32[]{:S(2)}, u32[]{:S(2)}) collective-permute-start(bf16[8,192,128]{2,1,0:T(8,128)(2,1)S(1)} %pad_maximum_fusion.early_ref), channel_id=1, source_target_pairs={{0,1},{1,0},{2,3},{3,2},{4,5},{5,4},{6,7},{7,6},{8,9},{9,8},{10,11... | collective-permute-start | bytes 1179656 | tf_op jit(solution)/shard_map/ppermute | solution.py:624
  46.5 6.1 %collective-permute-start.4 = (bf16[1,192,128]{2,1,0:T(8,128)(2,1)S(1)}, bf16[1,192,128]{2,1,0:T(8,128)(2,1)S(1)}, u32[]{:S(2)}, u32[]{:S(2)}) collective-permute-start(bf16[1,192,128]{2,1,0:T(8,128)(2,1)S(1)} %bitcast.10), channel_id=1, source_target_pairs={{0,8},{1,9},{2,10},{3,11},{4,12},{5,13},{6,14},{7,15},{8,0},{9,1},... | collective-permute-start | bytes 147464 | tf_op jit(solution)/shard_map/ppermute | solution.py:624
  52.7 4.7 %collective-permute-start.5 = (bf16[2,192,128]{2,1,0:T(8,128)(2,1)S(1)}, bf16[2,192,128]{2,1,0:T(8,128)(2,1)S(1)}, u32[]{:S(2)}, u32[]{:S(2)}) collective-permute-start(bf16[2,192,128]{2,1,0:T(8,128)(2,1)S(1)} %pad_maximum_fusion.5), channel_id=1, source_target_pairs={{0,4},{1,5},{2,6},{3,7},{4,0},{5,1},{6,2},{7,3},{8,12},{9,13},{10,... | collective-permute-start | bytes 294920 | tf_op jit(solution)/shard_map/ppermute | solution.py:624
  57.4 5.7 %collective-permute-start.6 = (bf16[4,192,128]{2,1,0:T(8,128)(2,1)S(1)}, bf16[4,192,128]{2,1,0:T(8,128)(2,1)S(1)}, u32[]{:S(2)}, u32[]{:S(2)}) collective-permute-start(bf16[4,192,128]{2,1,0:T(8,128)(2,1)S(1)} %pad_maximum_fusion.3), channel_id=1, source_target_pairs={{0,2},{1,3},{2,0},{3,1},{4,6},{5,7},{6,4},{7,5},{8,10},{9,11},{10,... | collective-permute-start | bytes 589832 | tf_op jit(solution)/shard_map/ppermute | solution.py:624
  63.2 1.8 %collective-permute-start.7 = (bf16[8,192,128]{2,1,0:T(8,128)(2,1)S(1)}, bf16[8,192,128]{2,1,0:T(8,128)(2,1)S(1)}, u32[]{:S(2)}, u32[]{:S(2)}) collective-permute-start(bf16[8,192,128]{2,1,0:T(8,128)(2,1)S(1)} %pad_maximum_fusion.1.early_ref), channel_id=1, source_target_pairs={{0,1},{1,0},{2,3},{3,2},{4,5},{5,4},{6,7},{7,6},{8,9},{9,8},{10,11... | collective-permute-start | bytes 1179656 | tf_op jit(solution)/shard_map/ppermute | solution.py:624
  (3 other events, 8.2 us)

commit v4 on v3

--- a/solution.py
+++ b/solution.py
@@ -253,10 +253,11 @@
     return own_blocks(dot(jnp.concatenate(rows, axis=0), weights), rhs)
 
 
-def near_kernel(chunk0, leaves_ref, z_ref, blocks_ref, out_ref, z_leaves_ref):
+def near_kernel(chunk0, me_ref, leaves_ref, z_ref, blocks_ref, out_ref, z_leaves_ref):
     rhs, order = z_ref.shape
     chunks = out_ref.shape[1] // CHUNK
     per = CHUNK // M
+    base = me_ref[0] * (order // M) - HN
     first_tile = max(chunk0 * (CHUNK // LANES) - 1, 0)
     last_tile = min((chunk0 + chunks) * (CHUNK // LANES) + 1, order // LANES)
     for t in range(first_tile, last_tile):
@@ -269,7 +270,7 @@
             here = pl.ds(pl.multiple_of(c * CHUNK + g * 256, 256), 256)
             there = pl.ds(pl.multiple_of((chunk0 + c) * CHUNK + g * 256, 256), 256)
             weights = blocks_ref[:, :, there].reshape(NEAR * M, 256)
-            out_ref[:, here] = near_group(lambda j, e: z_leaves_ref[leaves_ref[j, leaf0 + e]], weights, rhs)
+            out_ref[:, here] = near_group(lambda j, e: z_leaves_ref[leaves_ref[j, leaf0 + e] - base], weights, rhs)
 
 
 def bit_reverse(value, bits):
@@ -381,10 +382,11 @@
         put_leaves(z_leaves_ref, z_ref[:, t * LANES : (t + 1) * LANES], 2 + 2 * t)
         put_leaves(z_leaves_ref, z_ref[:, order - (3 - t) * LANES : order - (2 - t) * LANES or None], 8 + 2 * t)
     put_leaves(z_leaves_ref, z_after, 14)
-    head = near_group(lambda j, e: z_leaves_ref[leaves_ref[j, e]], blocks_ref[:, :, :256].reshape(NEAR * M, 256), rhs)
+    base = me * leaves - HN
+    head = near_group(lambda j, e: z_leaves_ref[leaves_ref[j, e] - base], blocks_ref[:, :, :256].reshape(NEAR * M, 256), rhs)
     skip = leaves + 2 * HN - 16
     tail = near_group(
-        lambda j, e: z_leaves_ref[leaves_ref[j, leaves - 4 + e] - skip], blocks_ref[:, :, order - 256 :].reshape(NEAR * M, 256), rhs
+        lambda j, e: z_leaves_ref[leaves_ref[j, leaves - 4 + e] - base - skip], blocks_ref[:, :, order - 256 :].reshape(NEAR * M, 256), rhs
     )
 
     sides = slice(own_rows, own_rows + K)
@@ -548,7 +550,7 @@
     leaves = order // M
     half = rhs // 2
     me = position.astype(jnp.int32).reshape(1)
-    near_local = near_leaves.T - (position * leaves - HN)
+    near_columns = near_leaves.T
     lists = (list_first.T, list_second.T, top_nodes.T)
 
     sent_rows = half // 2 * K + K + 2 * rhs
@@ -596,12 +598,12 @@
         return pl.pallas_call(
             functools.partial(near_kernel, i * cut // CHUNK),
             out_shape=shape((rhs, cut), F32),
-            in_specs=[SM, VM, VM],
+            in_specs=[SM, SM, VM, VM],
             out_specs=VM,
             scratch_shapes=[pltpu.VMEM((leaves + 2 * HN, rhs, LANES), BF16)],
             compiler_params=params(16),
             cost_estimate=cost(10**9, 8 * 2**20),
-        )(near_local, vectors, blocks)
+        )(me, near_columns, vectors, blocks)
 
     def couple(coef1, coef2, m1, m2):
         return pl.pallas_call(
@@ -654,7 +656,7 @@
             ],
             compiler_params=params(24),
             cost_estimate=cost(10**9, 8 * 2**20),
-        )(me, near_local, every, other, far1, far2, vectors, *nears, blocks, basis, *lists[:2], table, ends, m3, d1, d2, d3)
+        )(me, near_columns, every, other, far1, far2, vectors, *nears, blocks, basis, *lists[:2], table, ends, m3, d1, d2, d3)
         return results
 
     sent, coef1, coef2 = upward

time: 72.7 us -> 72.8 us (level)
    unnamed x38 -> x42, local copies, waits for them, and re-layouts: 5.12 us -> 5.82 us
  transfers between devices with their start and end apart: 8 -> 8, of which waited for: 6 -> 6; matrix products, arithmetic and copies ran while one was open for 1% -> 0% of each run, Pallas kernels for 33% -> 33%
where the time goes in v4:
time: 72.8 us; the launch traced here: 72.6 us
  Pallas kernels  49.7 us (68%)
  starting transfers between devices  9.86 us (14%)
  waiting for transfers between devices  5.91 us (8%)
  local copies, waits for them, and re-layouts  5.82 us (8%)
  between operations  1.17 us (2%)
    pallas_call x2, Pallas kernels, down(): pl.pallas_call(functools.partial(down_kernel, bits), out_shape=(out, out)...  14.7 us
    pallas_call x4, Pallas kernels, near_piece(): pl.pallas_call(functools.partial(near_kernel, i * cut // CHUNK), out_shap...  12.5 us
    ppermute x8, starting transfers between devices, exchange(): other = lax.ppermute(every, AXES, pairs)  9.86 us
    pallas_call x2, Pallas kernels, couple(): pl.pallas_call(functools.partial(couple_kernel, bits), out_shape=(shape((...  8.31 us
    pallas_call x1, Pallas kernels, body(): pl.pallas_call(first_kernel, out_shape=up_shapes + (shape((K, K, leaves))...  6.88 us
    ppermute x8, waiting for transfers between devices, exchange(): other = lax.ppermute(every, AXES, pairs)  5.91 us
    unnamed x42, local copies, waits for them, and re-layouts  5.82 us
    pallas_call x1, Pallas kernels, body(): pl.pallas_call(up_kernel, out_shape=up_shapes, in_specs=[VM] * 5, out_spe...  4.36 us
  transfers between devices with their start and end apart: 8, of which 6 were waited for; matrix products, arithmetic and copies ran while one was open for 0% of the time, Pallas kernels for 33%

profile of v4, /device:TPU:0, one launch (start us, length us, event | category | flops | bytes accessed | tf_op | source)
XLA Modules:
  0.0 72.6 jit_solution(11996971128341331809)
XLA Ops:
  0.7 6.9 %shard_map.140 = (bf16[192,128]{1,0:T(8,128)(2,1)}, bf16[16,32,128]{2,1,0:T(8,128)(2,1)}, bf16[8,32,128]{2,1,0:T(8,128)(2,1)}, bf16[32,32,256]{2,1,0:T(8,128)(2,...) custom-call(bf16[16,16384]{1,0:T(8,128)(2,1)} %z_ref.3, bf16[32,16384]{1,0:T(8,128)(2,1)} %refs_3_.3, ...), custom_call_target="tpu_custom_call" | custom-call | flops 1000000000 | bytes 3145728 | tf_op jit(solution)/shard_map/pallas_call | solution.py:564
  7.6 4.1 %collective-permute-start = (bf16[1,192,128]{2,1,0:T(8,128)(2,1)}, bf16[1,192,128]{2,1,0:T(8,128)(2,1)S(1)}, u32[]{:S(2)}, u32[]{:S(2)}) collective-permute-start(bf16[1,192,128]{2,1,0:T(8,128)(2,1)} %bitcast.29), channel_id=1, source_target_pairs={{0,8},{1,9},{2,10},{3,11},{4,12},{5,13},{6,14},{7,15},{8,0},{9,1},... | collective-permute-start | bytes 147464 | tf_op jit(solution)/shard_map/ppermute | solution.py:626
  11.7 4.0 %copy-done = bf16[5,64,16384]{2,1,0:T(8,128)(2,1)S(1)} copy-done((bf16[5,64,16384]{2,1,0:T(8,128)(2,1)S(1)}, bf16[5,64,16384]{2,1,0:T(8,128)(2,1)}, u32[]{:S(2)}) %copy-start) | copy-done | bytes 10485784
  15.7 1.0 %copy-done.2 = bf16[16,16384]{1,0:T(8,128)(2,1)S(1)} copy-done((bf16[16,16384]{1,0:T(8,128)(2,1)S(1)}, bf16[16,16384]{1,0:T(8,128)(2,1)}, u32[]{:S(2)}) %copy-start.2) | copy-done | bytes 524312
  16.7 0.7 copy-done.10
  17.5 3.1 %shard_map.141.refs_0_ = f32[16,8192]{1,0:T(8,128)S(1)} custom-call(s32[1]{0:T(128)} %bitcast.me_ref, s32[5,256]{1,0:T(8,128)S(1)} %bitcast.13, bf16[16,16384]{1,0:T(8,128)(2,1)S(1)} %copy-done.2, bf16[5,64,16384]{2,1,0:T(8,128)(2,1)S(1)} %copy-done), custom_call_target="tpu_custom_call" | custom-call | flops 1000000000 | bytes 8388608 | tf_op jit(solution)/shard_map/pallas_call | solution.py:598
  20.6 1.6 %collective-permute-start.1 = (bf16[2,192,128]{2,1,0:T(8,128)(2,1)S(1)}, bf16[2,192,128]{2,1,0:T(8,128)(2,1)S(1)}, u32[]{:S(2)}, u32[]{:S(2)}) collective-permute-start(bf16[2,192,128]{2,1,0:T(8,128)(2,1)S(1)} %pad_maximum_fusion.4), channel_id=1, source_target_pairs={{0,4},{1,5},{2,6},{3,7},{4,0},{5,1},{6,2},{7,3},{8,12},{9,13},{10,... | collective-permute-start | bytes 294920 | tf_op jit(solution)/shard_map/ppermute | solution.py:626
  22.3 2.8 %shard_map.142 = (bf16[32,32,256]{2,1,0:T(8,128)(2,1)S(1)}, bf16[32,32,128]{2,1,0:T(8,128)(2,1)S(1)}, bf16[32,32,128]{2,1,0:T(8,128)(2,1)S(1)}, bf16[3,32,32,128...) custom-call(bf16[32,32,256]{2,1,0:T(8,128)(2,1)S(1)} %copy-done.4, ...), custom_call_target="tpu_custom_call" | custom-call | flops 1000000000 | bytes 9437184 | tf_op jit(solution)/shard_map/pallas_call | solution.py:583
  25.3 1.6 %collective-permute-start.2 = (bf16[4,192,128]{2,1,0:T(8,128)(2,1)S(1)}, bf16[4,192,128]{2,1,0:T(8,128)(2,1)S(1)}, u32[]{:S(2)}, u32[]{:S(2)}) collective-permute-start(bf16[4,192,128]{2,1,0:T(8,128)(2,1)S(1)} %pad_maximum_fusion.2), channel_id=1, source_target_pairs={{0,2},{1,3},{2,0},{3,1},{4,6},{5,7},{6,4},{7,5},{8,10},{9,11},{10,... | collective-permute-start | bytes 589832 | tf_op jit(solution)/shard_map/ppermute | solution.py:626
  27.0 4.1 %shard_map.143 = (f32[16,32,128]{2,1,0:T(8,128)S(1)}, f32[8,32,128]{2,1,0:T(8,128)S(1)}, bf16[2,512,128]{2,1,0:T(8,128)(2,1)S(1)}) custom-call(s32[1]{0:T(128)} %bitcast.me_ref, bf16[16,32,128]{2,1,0:T(8,128)(2,1)S(1)} %copy-done.15, bf16[8,32,128]{2,1,0:T(8,128)(2,1)S(1)} %copy-done.16, s32[3,128]{1,0:T(4,128)S(1)} %bitcast.19, s32[3,64]{1,0:T(4,128)S(1)} %bitcast.23, ...), custom_call_target="tpu_custom_call" | custom-call | flops 1000000000 | bytes 8388608 | tf_op jit(solution)/shard_map/pallas_call | solution.py:609
  31.6 3.3 %shard_map.144.refs_1_ = f32[16,8192]{1,0:T(8,128)S(1)} custom-call(s32[1]{0:T(128)} %bitcast.me_ref, s32[5,256]{1,0:T(8,128)S(1)} %bitcast.14, bf16[16,16384]{1,0:T(8,128)(2,1)S(1)} %copy-done.3, bf16[5,64,16384]{2,1,0:T(8,128)(2,1)S(1)} %bitcast.8), custom_call_target="tpu_custom_call" | custom-call | flops 1000000000 | bytes 8388608 | tf_op jit(solution)/shard_map/pallas_call | solution.py:598
  34.9 7.4 %shard_map.145 = (bf16[16,16384]{1,0:T(8,128)(2,1)}, bf16[16,16384]{1,0:T(8,128)(2,1)S(1)}) custom-call(s32[1]{0:T(128)} %bitcast.me_ref, s32[5,256]{1,0:T(8,128)S(1)} %bitcast.15, bf16[8,192,128]{2,1,0:T(8,128)(2,1)S(1)} %pad_maximum_fusion.early_ref, bf16[8,192,128]{2,1,0:T(8,128)(2,1)S(1)} %collective-permute-done.3.late_ref, ...), custom_call_target="tpu_custom_call" | custom-call | flops 1000000000 | bytes 8388608 | tf_op jit(solution)/shard_map/pallas_call | solution.py:641
  42.2 4.4 %shard_map.146 = (bf16[192,128]{1,0:T(8,128)(2,1)S(1)}, bf16[16,32,128]{2,1,0:T(8,128)(2,1)S(1)}, bf16[8,32,128]{2,1,0:T(8,128)(2,1)S(1)}) custom-call(bf16[16,16384]{1,0:T(8,128)(2,1)S(1)} %get-tuple-element.113.z_ref, bf16[32,16384]{1,0:T(8,128)(2,1)S(1)} %copy-done.1, bf16[32,32,256]{2,1,0:T(8,128)(2,1)S(1)} %copy-done.4, ...), custom_call_target="tpu_custom_call" | custom-call | flops 100000000 | bytes 3145728 | tf_op jit(solution)/shard_map/pallas_call | solution.py:672
  46.6 0.4 collective-permute-start.4
  47.0 4.3 %shard_map.147 = (f32[16,32,128]{2,1,0:T(8,128)S(1)}, f32[8,32,128]{2,1,0:T(8,128)S(1)}, bf16[2,512,128]{2,1,0:T(8,128)(2,1)S(1)}) custom-call(s32[1]{0:T(128)} %bitcast.me_ref, bf16[16,32,128]{2,1,0:T(8,128)(2,1)S(1)} %get-tuple-element.103.coef1_ref, bf16[8,32,128]{2,1,0:T(8,128)(2,1)S(1)} %get-tuple-element.104.coef2_ref, s32[3,128]{1,0:T(4,128)S(1)} %bitcast.21, ...), custom_call_target="tpu_custom_call" | custom-call | flops 1000000000 | bytes 8388608 | tf_op jit(solution)/shard_map/pallas_call | solution.py:609
  51.3 1.5 %collective-permute-done.4 = bf16[1,192,128]{2,1,0:T(8,128)(2,1)S(1)} collective-permute-done((bf16[1,192,128]{2,1,0:T(8,128)(2,1)S(1)}, bf16[1,192,128]{2,1,0:T(8,128)(2,1)S(1)}, u32[]{:S(2)}, u32[]{:S(2)}) %collective-permute-start.4) | collective-permute-done | bytes 49184 | tf_op jit(solution)/shard_map/ppermute | solution.py:626
  52.8 0.4 collective-permute-start.5
  53.2 3.1 %shard_map.148.refs_0_ = f32[16,8192]{1,0:T(8,128)S(1)} custom-call(s32[1]{0:T(128)} %bitcast.me_ref, s32[5,256]{1,0:T(8,128)S(1)} %bitcast.16, bf16[16,16384]{1,0:T(8,128)(2,1)S(1)} %get-tuple-element.113.z_ref, bf16[5,64,16384]{2,1,0:T(8,128)(2,1)S(1)} %bitcast.8), custom_call_target="tpu_custom_call" | custom-call | flops 1000000000 | bytes 8388608 | tf_op jit(solution)/shard_map/pallas_call | solution.py:598
  56.3 1.2 %collective-permute-done.5 = bf16[2,192,128]{2,1,0:T(8,128)(2,1)S(1)} collective-permute-done((bf16[2,192,128]{2,1,0:T(8,128)(2,1)S(1)}, bf16[2,192,128]{2,1,0:T(8,128)(2,1)S(1)}, u32[]{:S(2)}, u32[]{:S(2)}) %collective-permute-start.5) | collective-permute-done | bytes 98336 | tf_op jit(solution)/shard_map/ppermute | solution.py:626
  57.5 1.6 %collective-permute-start.6 = (bf16[4,192,128]{2,1,0:T(8,128)(2,1)S(1)}, bf16[4,192,128]{2,1,0:T(8,128)(2,1)S(1)}, u32[]{:S(2)}, u32[]{:S(2)}) collective-permute-start(bf16[4,192,128]{2,1,0:T(8,128)(2,1)S(1)} %pad_maximum_fusion.3), channel_id=1, source_target_pairs={{0,2},{1,3},{2,0},{3,1},{4,6},{5,7},{6,4},{7,5},{8,10},{9,11},{10,... | collective-permute-start | bytes 589832 | tf_op jit(solution)/shard_map/ppermute | solution.py:626
  59.1 3.1 %shard_map.149.refs_1_ = f32[16,8192]{1,0:T(8,128)S(1)} custom-call(s32[1]{0:T(128)} %bitcast.me_ref, s32[5,256]{1,0:T(8,128)S(1)} %bitcast.17, bf16[16,16384]{1,0:T(8,128)(2,1)S(1)} %get-tuple-element.113.z_ref, bf16[5,64,16384]{2,1,0:T(8,128)(2,1)S(1)} %bitcast.8), custom_call_target="tpu_custom_call" | custom-call | flops 1000000000 | bytes 8388608 | tf_op jit(solution)/shard_map/pallas_call | solution.py:598
  62.1 1.1 %collective-permute-done.6 = bf16[4,192,128]{2,1,0:T(8,128)(2,1)S(1)} collective-permute-done((bf16[4,192,128]{2,1,0:T(8,128)(2,1)S(1)}, bf16[4,192,128]{2,1,0:T(8,128)(2,1)S(1)}, u32[]{:S(2)}, u32[]{:S(2)}) %collective-permute-start.6) | collective-permute-done | bytes 196640 | tf_op jit(solution)/shard_map/ppermute | solution.py:626
  63.3 1.7 %collective-permute-done.7.late_ref = bf16[8,192,128]{2,1,0:T(8,128)(2,1)S(1)} collective-permute-done((bf16[8,192,128]{2,1,0:T(8,128)(2,1)S(1)}, bf16[8,192,128]{2,1,0:T(8,128)(2,1)S(1)}, u32[]{:S(2)}, u32[]{:S(2)}) %collective-permute-start.7) | collective-permute-done | bytes 393248 | tf_op jit(solution)/shard_map/ppermute | solution.py:626
  65.0 7.4 %shard_map.150 = bf16[16,16384]{1,0:T(8,128)(2,1)} custom-call(s32[1]{0:T(128)} %bitcast.me_ref, s32[5,256]{1,0:T(8,128)S(1)} %bitcast.18, bf16[8,192,128]{2,1,0:T(8,128)(2,1)S(1)} %pad_maximum_fusion.1.early_ref, bf16[8,192,128]{2,1,0:T(8,128)(2,1)S(1)} %collective-permute-done.7.late_ref, f32[16,32,128]{2,1,0:T(8,128)S(1)} %get-tuple-element.115.far1_in_ref, ...), custom_call_target="tpu_custom_call" | custom-call | flops 1000000000 | bytes 8388608 | tf_op jit(solution)/shard_map/pallas_call | solution.py:641
  (52 shorter events, 0.9 us)
Async XLA Ops:
  0.6 21.7 %copy-start.5 = (bf16[8,32,32,32]{3,2,1,0:T(8,128)(2,1)S(1)}, bf16[8,32,32,32]{3,2,1,0:T(8,128)(2,1)}, u32[]{:S(2)}) copy-start(bf16[8,32,32,32]{3,2,1,0:T(8,128)(2,1)} %c3_ref.1) | copy-start | bytes 1572868
  0.6 21.6 %copy-start.8 = (bf16[3,32,32,128]{3,2,1,0:T(8,128)(2,1)S(1)}, bf16[3,32,32,128]{3,2,1,0:T(8,128)(2,1)}, u32[]{:S(2)}) copy-start(bf16[3,32,32,128]{3,2,1,0:T(8,128)(2,1)} %c1_ref.1) | copy-start | bytes 2359300
  0.7 26.3 %copy-start.14 = (s32[32,8]{0,1:T(8,128)S(1)}, s32[32,8]{0,1:T(8,128)}, u32[]{:S(2)}) copy-start(s32[32,8]{0,1:T(8,128)} %param.25) | copy-start | bytes 3076
  0.7 26.3 %copy-start.13 = (s32[64,3]{0,1:T(4,128)S(1)}, s32[64,3]{0,1:T(4,128)}, u32[]{:S(2)}) copy-start(s32[64,3]{0,1:T(4,128)} %param.23) | copy-start | bytes 2308
  0.7 26.3 %copy-start.12 = (s32[128,3]{0,1:T(4,128)S(1)}, s32[128,3]{0,1:T(4,128)}, u32[]{:S(2)}) copy-start(s32[128,3]{0,1:T(4,128)} %param.22) | copy-start | bytes 4612
  7.6 13.0 %collective-permute-start = (bf16[1,192,128]{2,1,0:T(8,128)(2,1)}, bf16[1,192,128]{2,1,0:T(8,128)(2,1)S(1)}, u32[]{:S(2)}, u32[]{:S(2)}) collective-permute-start(bf16[1,192,128]{2,1,0:T(8,128)(2,1)} %bitcast.29), channel_id=1, source_target_pairs={{0,8},{1,9},{2,10},{3,11},{4,12},{5,13},{6,14},{7,15},{8,0},{9,1},... | collective-permute-start | bytes 147464 | tf_op jit(solution)/shard_map/ppermute | solution.py:626
  17.4 4.9 %copy-start.6 = (bf16[32,32,128]{2,1,0:T(8,128)(2,1)S(1)}, bf16[32,32,128]{2,1,0:T(8,128)(2,1)}, u32[]{:S(2)}) copy-start(bf16[32,32,128]{2,1,0:T(8,128)(2,1)} %get-tuple-element.68.up2_ref) | copy-start | bytes 786436
  17.4 4.9 %copy-start.7 = (bf16[32,32,128]{2,1,0:T(8,128)(2,1)S(1)}, bf16[32,32,128]{2,1,0:T(8,128)(2,1)}, u32[]{:S(2)}) copy-start(bf16[32,32,128]{2,1,0:T(8,128)(2,1)} %get-tuple-element.69.up3_ref) | copy-start | bytes 786436
  17.4 4.9 %copy-start.9 = (bf16[3,32,32,64]{3,2,1,0:T(8,128)(2,1)S(1)}, bf16[3,32,32,64]{3,2,1,0:T(8,128)(2,1)}, u32[]{:S(2)}) copy-start(bf16[3,32,32,64]{3,2,1,0:T(8,128)(2,1)} %c2_ref.1) | copy-start | bytes 1179652
  17.4 9.5 %copy-start.15 = (bf16[16,32,128]{2,1,0:T(8,128)(2,1)S(1)}, bf16[16,32,128]{2,1,0:T(8,128)(2,1)}, u32[]{:S(2)}) copy-start(bf16[16,32,128]{2,1,0:T(8,128)(2,1)} %get-tuple-element.80.coef1_ref) | copy-start | bytes 393220
  17.4 9.5 %copy-start.16 = (bf16[8,32,128]{2,1,0:T(8,128)(2,1)S(1)}, bf16[8,32,128]{2,1,0:T(8,128)(2,1)}, u32[]{:S(2)}) copy-start(bf16[8,32,128]{2,1,0:T(8,128)(2,1)} %get-tuple-element.81.coef2_ref) | copy-start | bytes 196612
  17.5 14.0 %slice-start = ((s8[10485760]{0:T(1024)(128)(4,1)}), s8[4194304]{0:T(1024)(128)(4,1)S(1)}, s32[]{:S(2)}) async-start(s8[10485760]{0:T(1024)(128)(4,1)} %bitcast.7), calls=%async_computation | async-start | bytes 8388608
  17.5 14.0 %slice-start.1 = ((s8[10485760]{0:T(1024)(128)(4,1)}), s8[4194304]{0:T(1024)(128)(4,1)S(1)}, s32[]{:S(2)}) async-start(s8[10485760]{0:T(1024)(128)(4,1)} %bitcast.7), calls=%async_computation.1 | async-start | bytes 8388608
  17.5 14.0 %copy-start.3 = (bf16[16,16384]{1,0:T(8,128)(2,1)S(1)}, bf16[16,16384]{1,0:T(8,128)(2,1)}, u32[]{:S(2)}) copy-start(bf16[16,16384]{1,0:T(8,128)(2,1)} %z_ref.3) | copy-start | bytes 1572868
  17.5 14.0 %copy-start.11 = (s32[256,5]{0,1:T(8,128)S(1)}, s32[256,5]{0,1:T(8,128)}, u32[]{:S(2)}) copy-start(s32[256,5]{0,1:T(8,128)} %param.15) | copy-start | bytes 15364
  20.6 4.7 %collective-permute-start.1 = (bf16[2,192,128]{2,1,0:T(8,128)(2,1)S(1)}, bf16[2,192,128]{2,1,0:T(8,128)(2,1)S(1)}, u32[]{:S(2)}, u32[]{:S(2)}) collective-permute-start(bf16[2,192,128]{2,1,0:T(8,128)(2,1)S(1)} %pad_maximum_fusion.4), channel_id=1, source_target_pairs={{0,4},{1,5},{2,6},{3,7},{4,0},{5,1},{6,2},{7,3},{8,12},{9,13},{10,... | collective-permute-start | bytes 294920 | tf_op jit(solution)/shard_map/ppermute | solution.py:626
  22.3 9.2 %slice-start.2 = ((s8[10485760]{0:T(1024)(128)(4,1)}), s8[2097152]{0:T(1024)(128)(4,1)S(1)}, s32[]{:S(2)}) async-start(s8[10485760]{0:T(1024)(128)(4,1)} %bitcast.7), calls=%async_computation.2 | async-start | bytes 4194304
  22.3 12.5 %copy-start.1 = (bf16[32,16384]{1,0:T(8,128)(2,1)S(1)}, bf16[32,16384]{1,0:T(8,128)(2,1)}, u32[]{:S(2)}) copy-start(bf16[32,16384]{1,0:T(8,128)(2,1)} %refs_3_.3) | copy-start | bytes 3145732
  25.3 6.0 %collective-permute-start.2 = (bf16[4,192,128]{2,1,0:T(8,128)(2,1)S(1)}, bf16[4,192,128]{2,1,0:T(8,128)(2,1)S(1)}, u32[]{:S(2)}, u32[]{:S(2)}) collective-permute-start(bf16[4,192,128]{2,1,0:T(8,128)(2,1)S(1)} %pad_maximum_fusion.2), channel_id=1, source_target_pairs={{0,2},{1,3},{2,0},{3,1},{4,6},{5,7},{6,4},{7,5},{8,10},{9,11},{10,... | collective-permute-start | bytes 589832 | tf_op jit(solution)/shard_map/ppermute | solution.py:626
  31.4 3.4 %collective-permute-start.3 = (bf16[8,192,128]{2,1,0:T(8,128)(2,1)S(1)}, bf16[8,192,128]{2,1,0:T(8,128)(2,1)S(1)}, u32[]{:S(2)}, u32[]{:S(2)}) collective-permute-start(bf16[8,192,128]{2,1,0:T(8,128)(2,1)S(1)} %pad_maximum_fusion.early_ref), channel_id=1, source_target_pairs={{0,1},{1,0},{2,3},{3,2},{4,5},{5,4},{6,7},{7,6},{8,9},{9,8},{10,11... | collective-permute-start | bytes 1179656 | tf_op jit(solution)/shard_map/ppermute | solution.py:626
  46.6 6.1 %collective-permute-start.4 = (bf16[1,192,128]{2,1,0:T(8,128)(2,1)S(1)}, bf16[1,192,128]{2,1,0:T(8,128)(2,1)S(1)}, u32[]{:S(2)}, u32[]{:S(2)}) collective-permute-start(bf16[1,192,128]{2,1,0:T(8,128)(2,1)S(1)} %bitcast.9), channel_id=1, source_target_pairs={{0,8},{1,9},{2,10},{3,11},{4,12},{5,13},{6,14},{7,15},{8,0},{9,1},... | collective-permute-start | bytes 147464 | tf_op jit(solution)/shard_map/ppermute | solution.py:626
  52.8 4.7 %collective-permute-start.5 = (bf16[2,192,128]{2,1,0:T(8,128)(2,1)S(1)}, bf16[2,192,128]{2,1,0:T(8,128)(2,1)S(1)}, u32[]{:S(2)}, u32[]{:S(2)}) collective-permute-start(bf16[2,192,128]{2,1,0:T(8,128)(2,1)S(1)} %pad_maximum_fusion.5), channel_id=1, source_target_pairs={{0,4},{1,5},{2,6},{3,7},{4,0},{5,1},{6,2},{7,3},{8,12},{9,13},{10,... | collective-permute-start | bytes 294920 | tf_op jit(solution)/shard_map/ppermute | solution.py:626
  57.5 5.7 %collective-permute-start.6 = (bf16[4,192,128]{2,1,0:T(8,128)(2,1)S(1)}, bf16[4,192,128]{2,1,0:T(8,128)(2,1)S(1)}, u32[]{:S(2)}, u32[]{:S(2)}) collective-permute-start(bf16[4,192,128]{2,1,0:T(8,128)(2,1)S(1)} %pad_maximum_fusion.3), channel_id=1, source_target_pairs={{0,2},{1,3},{2,0},{3,1},{4,6},{5,7},{6,4},{7,5},{8,10},{9,11},{10,... | collective-permute-start | bytes 589832 | tf_op jit(solution)/shard_map/ppermute | solution.py:626
  63.2 1.8 %collective-permute-start.7 = (bf16[8,192,128]{2,1,0:T(8,128)(2,1)S(1)}, bf16[8,192,128]{2,1,0:T(8,128)(2,1)S(1)}, u32[]{:S(2)}, u32[]{:S(2)}) collective-permute-start(bf16[8,192,128]{2,1,0:T(8,128)(2,1)S(1)} %pad_maximum_fusion.1.early_ref), channel_id=1, source_target_pairs={{0,1},{1,0},{2,3},{3,2},{4,5},{5,4},{6,7},{7,6},{8,9},{9,8},{10,11... | collective-permute-start | bytes 1179656 | tf_op jit(solution)/shard_map/ppermute | solution.py:626
  (5 other events, 13.8 us)
